TPU v7x, 32 devices: a whole 2x2x4 slice. The times are simulated.
32 devices in a mesh: var: 4 (over y, core), samp: 8 (over z, x).
Axes of the slice: x: 2, y: 2, z: 4, core: 2. Of those that a mesh axis runs over, the one named last changes fastest.
Arguments:
- dosages: float32 [6144, 4096], P('samp', 'var'), may hold values from 0 to 2
Outputs:
- ld_band: float32 [4096, 1024], P(('var', 'samp'))
All inputs are finite; a program needn't handle non-finite values.
Results may differ from a plain program's by a relative error of at most 0.0003.
Values sent between devices are 32-bit elements; how exact they have to be, the bound alone decides.
No kernel may reach another device: no remote copies, remote signals or barrier semaphores. Data moves between devices by JAX's collectives and lax.ppermute only.
A program may use at most 64 MiB of HBM per device.

v0:
```python
import jax
import jax.numpy as jnp
from jax import lax
from jax.sharding import PartitionSpec as P

EPS = 1e-06


def shifted(block, axis, distance):
    devices = range(lax.axis_size(axis))
    route = [(i - distance, i) for i in devices if i - distance in devices]
    return lax.ppermute(block, axis, route)


def band_rows(block, offset):
    rows = block.shape[0]
    cols = block.shape[1]
    width = cols // 2
    flat = jnp.concatenate([block.reshape(-1), jnp.zeros((width + 1,), block.dtype)])
    taken = lax.dynamic_slice_in_dim(flat, offset + 1, rows * (cols + 1))
    return taken.reshape(rows, cols + 1)[:, :width]


def local(dosages):
    samples_all = dosages.shape[0] * lax.axis_size("samp")
    totals = lax.psum(jnp.sum(dosages, 0), "samp")
    mean = totals / samples_all
    centered = dosages - mean
    spread = lax.psum(jnp.sum(centered * centered, 0), "samp") / samples_all
    scale = lax.rsqrt(spread + EPS)
    ahead, ahead_scale = shifted((centered, scale), "var", -1)
    extended = jnp.concatenate([centered, ahead], 1)
    wide_scale = jnp.concatenate([scale, ahead_scale])
    gram = lax.dot_general(
        centered,
        extended,
        (((0,), (0,)), ((), ())),
        precision=lax.Precision.HIGHEST,
        preferred_element_type=jnp.float32,
    )
    return lax.psum_scatter(
        band_rows(gram * wide_scale[None, :], 0) * scale[:, None] / samples_all,
        "samp",
        scatter_dimension=0,
        tiled=True,
    )


def solution(mesh):
    in_specs = (P("samp", "var"),)
    out_specs = P(("var", "samp"), None)
    return jax.shard_map(local, mesh=mesh, in_specs=in_specs, out_specs=out_specs, check_vma=False)
```

profile of v0, /device:TPU:0, one launch (start us, length us, event | category | flops | bytes accessed | tf_op | source)
XLA Modules:
  0.0 211.4 jit_solution(9677378872073294843)
XLA Ops:
  6.5 0.0 copy-start
  6.5 0.0 reduce-scatter.2.cloned.1.call-start
  6.5 2.3 %reduce_sum.18 = f32[1024]{0:T(1024)S(1)} reduce(f32[768,1024]{1,0:T(8,128)} %param.1, f32[]{:T(128)} %constant.3.clone.1), dimensions={0}, to_apply=%region_0.0 | reduce | flops 785408 | bytes 3149828 | tf_op jit(solution)/shard_map/reduce_sum | solution.py:26
  8.8 23.1 %psum.14 = f32[1024]{0:T(1024)S(1)} all-reduce(f32[1024]{0:T(1024)S(1)} %reduce_sum.18), channel_id=1, replica_groups=mesh['var'=4,'samp'=8] {'samp'}, use_global_device_ids=true, to_apply=%region_1.0 | all-reduce | flops 1024 | bytes 8192 | tf_op jit(solution)/shard_map/psum | solution.py:26
  31.9 0.0 copy-done
  31.9 2.1 %multiply_reduce_fusion = (f32[1024]{0:T(1024)S(1)}, f32[768,1024]{1,0:T(8,128)}) fusion(f32[768,1024]{1,0:T(8,128)S(1)} %copy-done, f32[1024]{0:T(1024)S(1)} %broadcast_multiply_fusion), kind=kLoop, calls=%fused_computation.8 | loop fusion | flops 2358272 | bytes 6299648 | tf_op jit(solution)/shard_map/reduce_sum | solution.py:29
  34.0 1.3 collective-permute-start
  35.3 17.1 %psum.15 = f32[1024]{0:T(1024)S(1)} all-reduce(f32[1024]{0:T(1024)S(1)} %get-tuple-element.5), channel_id=1, replica_groups=mesh['var'=4,'samp'=8] {'samp'}, use_global_device_ids=true, to_apply=%region_3.0 | all-reduce | flops 1024 | bytes 8192 | tf_op jit(solution)/shard_map/psum | solution.py:29
  52.5 1.3 collective-permute-start.1
  53.8 1.8 collective-permute-done.1
  55.5 0.0 collective-permute-done
  55.5 23.2 %multiply_bitcast_fusion = f32[128,16,8,128]{3,2,1,0:T(8,128)S(1)} fusion(f32[2048]{0:T(1024)S(1)} %pad_maximum_fusion, f32[768,1024]{1,0:T(8,128)} %get-tuple-element.6, f32[768,1024]{1,0:T(8,128)} %collective-permute-done), kind=kOutput, calls=%fused_computation.1 | convolution fusion | flops 19331022848 | bytes 14688256 | tf_op jit(solution)/shard_map/dot_general | solution.py:34
  78.7 2.0 copy.2
  80.7 4.7 %pad_slice_fusion = f32[2098176]{0:T(1024)} fusion(f32[2097152]{0:T(1024)S(1)} %bitcast.4), kind=kLoop, calls=%fused_computation | loop fusion | bytes 16781312 | tf_op jit(solution)/shard_map/dynamic_slice | solution.py:20
  85.4 12.9 %reshape.10 = f32[1024,2049]{1,0:T(8,128)} reshape(f32[2098176]{0:T(1024)} %pad_slice_fusion) | data formatting | bytes 16785408 | tf_op jit(solution)/shard_map/reshape | solution.py:21
  98.3 4.6 %fusion.4 = f32[1024,1024]{1,0:T(8,128)} fusion(f32[1024,2049]{1,0:T(8,128)} %reshape.10, f32[1024]{0:T(1024)S(1)} %add_rsqrt_fusion), kind=kLoop, calls=%fused_computation.7 | loop fusion | flops 2097152 | bytes 8392704 | tf_op jit(solution)/shard_map/div | solution.py:42
  103.0 0.0 reduce-scatter.2.cloned.1.call-update
  103.0 101.5 %reduce-scatter.2.cloned.1.call-done = f32[128,1024]{1,0:T(8,128)} async-done(((f32[1024,1024]{1,0:T(8,128)}), f32[128,1024]{1,0:T(8,128)}) %reduce-scatter.2.cloned.1.call-update) | async-done | bytes 524304 | tf_op jit(solution)/shard_map/reduce_scatter | solution.py:41
  (3 shorter events, 0.0 us)
Async XLA Ops:
  6.5 25.4 %copy-start = (f32[768,1024]{1,0:T(8,128)S(1)}, f32[768,1024]{1,0:T(8,128)}, u32[]{:S(2)}) copy-start(f32[768,1024]{1,0:T(8,128)} %param.1) | copy-start | bytes 9437188
  6.5 198.0 %reduce-scatter.2.cloned.1.call-start = ((), (), s32[]{:S(2)}) async-start(), calls=%async_computation.1 | async-start | bytes 4718592 | tf_op jit(solution)/shard_map/reduce_scatter | solution.py:41
  34.0 21.5 %collective-permute-start = (f32[768,1024]{1,0:T(8,128)}, f32[768,1024]{1,0:T(8,128)}, u32[]{:S(2)}, u32[]{:S(2)}) collective-permute-start(f32[768,1024]{1,0:T(8,128)} %get-tuple-element.6), channel_id=1, source_target_pairs={{8,0},{16,8},{24,16},{9,1},{17,9},{25,17},{10,2},{18,10},{26,18},{... | collective-permute-start | bytes 9437192 | tf_op jit(solution)/shard_map/ppermute | solution.py:12
  52.5 3.1 %collective-permute-start.1 = (f32[1024]{0:T(1024)S(1)}, f32[1024]{0:T(1024)S(1)}, u32[]{:S(2)}, u32[]{:S(2)}) collective-permute-start(f32[1024]{0:T(1024)S(1)} %add_rsqrt_fusion), channel_id=1, source_target_pairs={{8,0},{16,8},{24,16},{9,1},{17,9},{25,17},{10,2},{18,10},{26,18},{... | collective-permute-start | bytes 12296 | tf_op jit(solution)/shard_map/ppermute | solution.py:12
Sparse Core Ops, SparseCore 0:
  103.1 101.3 reduce-scatter.1
where the time goes:
time: 212 us; the launch traced here: 211 us
  waiting for transfers between devices  103 us (49%)
  blocking collectives  40.2 us (19%)
  matrix products  23.2 us (11%)
  local copies, waits for them, and re-layouts  19.6 us (9%)
  between operations  13.4 us (6%)
  other arithmetic  9 us (4%)
  starting transfers between devices  2.57 us (1%)
    reduce_scatter x1, waiting for transfers between devices, local(): lax.psum_scatter(band_rows(gram * wide_scale[None, :], 0) * scale[:, None...  102 us
    dot_general x1, matrix products, local(): lax.dot_general(centered, extended, (((0,), (0,)), ((), ())), precision=l...  23.2 us
    psum x1, blocking collectives, local(): totals = lax.psum(jnp.sum(dosages, 0), 'samp')  23.1 us
    psum x1, blocking collectives, local(): spread = lax.psum(jnp.sum(centered * centered, 0), 'samp') / samples_all  17.1 us
    reshape x1, local copies, waits for them, and re-layouts, band_rows(): return taken.reshape(rows, cols + 1)[:, :width]  12.9 us
    dynamic_slice x1, local copies, waits for them, and re-layouts, band_rows(): taken = lax.dynamic_slice_in_dim(flat, offset + 1, rows * (cols + 1))  4.72 us
    div x1, other arithmetic, local(): band_rows(gram * wide_scale[None, :], 0) * scale[:, None] / samples_all  4.61 us
  transfers between devices with their start and end apart: 3, of which 2 were waited for; matrix products, arithmetic and copies ran while one was open for 0% of the time, Pallas kernels for 0%

commit v1 on v0

v1 whole, which is shorter than its diff:
```python
import functools

import jax
import jax.numpy as jnp
from jax import lax
from jax.experimental import pallas as pl
from jax.experimental.pallas import tpu as pltpu
from jax.sharding import PartitionSpec as P

EPS = 1e-06
STATS = 8
VMEM = pl.BlockSpec(memory_space=pltpu.VMEM)


def params(mib):
    return pltpu.CompilerParams(vmem_limit_bytes=mib << 20)


def cost(flops, data):
    return pl.CostEstimate(flops=flops, bytes_accessed=data, transcendentals=0)


def split(value):
    high = value.astype(jnp.bfloat16)
    low = (value - high.astype(jnp.float32)).astype(jnp.bfloat16)
    return high, low


def centre(block):
    count = block.shape[0]
    mean = jnp.sum(block, 0, keepdims=True) / count
    centred = block - mean
    left = jnp.sum(centred, 0, keepdims=True) / count
    squares = jnp.sum(centred * centred, 0, keepdims=True)
    return centred, mean, left, squares


def prepare_kernel(block, high, low, high_t, low_t, stats):
    centred, mean, left, squares = centre(block[...])
    high[...], low[...] = split(centred)
    high_t[...], low_t[...] = split(centred.T)
    zero = jnp.zeros_like(mean)
    rows = [mean, zero, left, zero, squares, zero, zero, zero]
    stats[...] = jnp.concatenate(rows, 0)


def prepare(dosages, width):
    samples, cols = dosages.shape
    tall = pl.BlockSpec((samples, width), lambda i: (0, i))
    flat = pl.BlockSpec((width, samples), lambda i: (i, 0))
    half = jax.ShapeDtypeStruct((samples, cols), jnp.bfloat16)
    half_t = jax.ShapeDtypeStruct((cols, samples), jnp.bfloat16)
    return pl.pallas_call(
        prepare_kernel,
        grid=(cols // width,),
        in_specs=[tall],
        out_specs=[tall, tall, flat, flat, pl.BlockSpec((STATS, width), lambda i: (0, i))],
        out_shape=[half, half, half_t, half_t, jax.ShapeDtypeStruct((STATS, cols), jnp.float32)],
        compiler_params=params(32),
        cost_estimate=cost(10 * samples * cols, 12 * samples * cols),
        name="prepare",
    )(dosages)


def place(owner, me, order):
    apart = jnp.bitwise_xor(owner, me)
    spot = 0
    for bit in order:
        spot = spot * 2 + (lax.shift_right_logical(apart, bit) & 1)
    return spot


def product(high_t, low_t, rows, high, low):
    dot = functools.partial(jnp.dot, preferred_element_type=jnp.float32)
    a, b = high_t[rows, :], low_t[rows, :]
    return dot(a, high) + (dot(a, low) + dot(b, high))


def gram_kernel(parts, start, order, high_t, low_t, high, low, own_stats, ahead, send, keep):
    cols = high_t.shape[0]
    width = ahead.shape[1]
    share = cols // parts
    half = parts // 2
    me = lax.axis_index("samp")
    centred, mean, left, squares = centre(ahead[...])
    ahead_high, ahead_low = split(centred)
    own_high, own_low = high[...], low[...]
    mine = own_stats[...]
    rows = [mine[0:1], mean, mine[2:3], left, mine[4:5], squares, mine[6:8]]
    stats = jnp.concatenate(rows, 0)
    send[half * share :, :] = stats
    keep[half * share :, :] = stats
    for first in range(0, cols, width):
        band = pl.ds(first, width)
        if first <= start:
            tile = product(high_t, low_t, band, own_high, own_low)
        if first >= start:
            later = product(high_t, low_t, band, ahead_high, ahead_low)
        if first > start:
            tile = later
        if first == start:
            row = lax.broadcasted_iota(jnp.int32, tile.shape, 0)
            col = lax.broadcasted_iota(jnp.int32, tile.shape, 1)
            tile = jnp.where(col > row, tile, later)
        for part in range(width // share):
            spot = place(first // share + part, me, order)
            piece = tile[part * share : (part + 1) * share]
            there = pl.ds(pl.multiple_of((spot & (half - 1)) * share, share), share)

            @pl.when(spot >= half)
            def _():
                send[there, :] = piece

            @pl.when(spot < half)
            def _():
                keep[there, :] = piece


def gram(parts, start, order, high_t, low_t, high, low, stats, ahead):
    cols, samples = high_t.shape
    width = ahead.shape[1]
    index = start // width
    tall = pl.BlockSpec((samples, width), lambda i: (0, index))
    whole = pl.BlockSpec((cols, samples), lambda i: (0, 0))
    shape = (cols // 2 + STATS, width)
    out = jax.ShapeDtypeStruct(shape, jnp.float32)
    return pl.pallas_call(
        functools.partial(gram_kernel, parts, start, order),
        grid=(1,),
        in_specs=[
            whole,
            whole,
            tall,
            tall,
            pl.BlockSpec((STATS, width), lambda i: (0, index)),
            pl.BlockSpec((samples, width), lambda i: (0, 0)),
        ],
        out_specs=[pl.BlockSpec(shape, lambda i: (0, 0))] * 2,
        out_shape=[out, out],
        compiler_params=params(40),
        cost_estimate=cost(6 * cols * width * samples, 4 * samples * (cols + 2 * width)),
        name="gram",
    )(high_t, low_t, high, low, stats, ahead)


def halve_kernel(size, keep, got, send, rest):
    half = size // 2
    send[:half, :] = keep[half:size, :] + got[half:size, :]
    rest[:half, :] = keep[:half, :] + got[:half, :]
    stats = keep.shape[0] - size
    for out in (send, rest):
        out[half : half + stats, :] = keep[size:, :]
        out[half + stats :, :] = got[size:, :]


def halve(size, keep, got):
    stats = keep.shape[0] - size
    shape = (size // 2 + 2 * stats, keep.shape[1])
    out = jax.ShapeDtypeStruct(shape, jnp.float32)
    return pl.pallas_call(
        functools.partial(halve_kernel, size),
        in_specs=[VMEM, VMEM],
        out_specs=[VMEM, VMEM],
        out_shape=[out, out],
        compiler_params=params(16),
        cost_estimate=cost(size * keep.shape[1], 16 * size * keep.shape[1]),
        name="halve",
    )(keep, got)


def finish_kernel(parts, samples, pieces, *refs):
    out, body, marks, scales = refs[2 * pieces :]
    share, cols = out.shape
    total = samples * parts
    me = lax.axis_index("samp")
    start = 0
    for i in range(pieces):
        keep, got = refs[2 * i], refs[2 * i + 1]
        width = keep.shape[1]
        here = slice(start, start + width)
        body[:, here] = keep[:share, :] + got[:share, :]
        half = parts // 2
        stats = jnp.concatenate(
            [ref[share:, :].reshape(half, STATS, width) for ref in (keep, got)], 0
        )
        mean = jnp.sum(stats, 0, keepdims=True) / parts
        apart = (stats - mean) + pltpu.roll(stats, STATS - 2, 1)
        apart = apart - jnp.sum(apart, 0, keepdims=True) / parts
        kind = lax.broadcasted_iota(jnp.int32, stats.shape, 1)
        mark = jnp.where(kind < 2, apart, jnp.where(kind < 4, stats, 0.0))
        moved = jnp.sum(mark * mark, 0) * samples
        squares = jnp.sum(stats, 0)
        spread = (squares[4:6] + (moved[0:2] - moved[2:4])) / total
        marks[:, here] = mark.reshape(parts * STATS, width)
        scales[0:2, here] = lax.rsqrt(spread + EPS)
        start += width
    first = me * share
    if share % 128 == 0:
        window = pl.ds(pl.multiple_of(first, 128), share)
        row_marks, row_scale = marks[:, window], scales[0:1, window]
    else:
        inside = lax.rem(first, 128)
        window = pl.ds(pl.multiple_of(first - inside, 128), 128)
        back = lax.rem(128 - inside, 128)
        row_marks = pltpu.roll(marks[:, window], back, 1)[:, :share]
        row_scale = pltpu.roll(jnp.broadcast_to(scales[0:1, window], (8, 128)), back, 1)[0:1, :share]
    row_scale = jnp.broadcast_to(row_scale, (128, share)).T / total
    kind = lax.broadcasted_iota(jnp.int32, row_marks.shape, 0) % STATS
    signed = jnp.where(kind == 0, row_marks, jnp.where(kind == 2, -row_marks, 0.0)) * samples
    signed_next = pltpu.roll(signed, 1, 0)
    dot = functools.partial(
        lax.dot_general,
        dimension_numbers=(((0,), (0,)), ((), ())),
        precision=lax.Precision.HIGHEST,
        preferred_element_type=jnp.float32,
    )
    row = first + lax.broadcasted_iota(jnp.int32, (share, 128), 0)
    lane = lax.broadcasted_iota(jnp.int32, (share, 128), 1)
    own_fix, ahead_fix = dot(signed, marks[...]), dot(signed_next, marks[...])
    for left in range(0, cols, 128):
        here = slice(left, left + 128)
        own = lane + left > row
        fix = jnp.where(own, own_fix[:, here], ahead_fix[:, here])
        scale = jnp.where(own, scales[0:1, here], scales[1:2, here])
        body[:, here] = (body[:, here] + fix) * scale * row_scale
    turned = pltpu.roll(body[...], lax.rem(2 * cols - first - 1, cols), 1)
    row = lax.broadcasted_iota(jnp.int32, (share, cols), 0)
    step = 1
    while step < share:
        moved = pltpu.roll(turned, cols - step, 1)
        turned = jnp.where((row & step) != 0, moved, turned)
        step *= 2
    out[...] = turned


def finish(parts, samples, share, cols, pairs):
    flat = [array for pair in pairs for array in pair]
    return pl.pallas_call(
        functools.partial(finish_kernel, parts, samples, len(pairs)),
        in_specs=[VMEM] * len(flat),
        out_specs=VMEM,
        out_shape=jax.ShapeDtypeStruct((share, cols), jnp.float32),
        scratch_shapes=[
            pltpu.VMEM((share, cols), jnp.float32),
            pltpu.VMEM((parts * STATS, cols), jnp.float32),
            pltpu.VMEM((8, cols), jnp.float32),
        ],
        compiler_params=params(32),
        cost_estimate=cost(40 * share * cols, 16 * share * cols),
        name="finish",
    )(*flat)


def swap(array, bit, parts):
    return lax.ppermute(array, "samp", [(i, i ^ (1 << bit)) for i in range(parts)])


def local(dosages):
    samples, cols = dosages.shape
    parts = lax.axis_size("samp")
    blocks = lax.axis_size("var")
    share = cols // parts
    steps = parts.bit_length() - 1
    unit = cols // 8
    widths = [unit, unit, 2 * unit, 2 * unit, 2 * unit]
    starts = [sum(widths[:i]) for i in range(len(widths))]
    route = [(i, i - 1) for i in range(1, blocks)]
    order = tuple(range(steps))
    ahead = [
        lax.ppermute(dosages[:, start : start + width], "var", route)
        for start, width in zip(starts, widths)
    ]
    high, low, high_t, low_t, stats = prepare(dosages, 2 * unit)
    pairs = []
    for start, block in zip(starts, ahead):
        send, keep = gram(parts, start, order, high_t, low_t, high, low, stats, block)
        size = cols // 2
        for step in order[:-1]:
            got = swap(send, step, parts)
            send, keep = halve(size, keep, got)
            size //= 2
        pairs.append((keep, swap(send, order[-1], parts)))
    return finish(parts, samples, share, cols, pairs)


def solution(mesh):
    in_specs = (P("samp", "var"),)
    out_specs = P(("var", "samp"), None)
    return jax.shard_map(local, mesh=mesh, in_specs=in_specs, out_specs=out_specs, check_vma=False)
```

time: 212 us -> 100 us (0.47)
  the two profiles are of different devices: /device:TPU:0 before, /device:TPU:4 now
where the time goes in v1:
time: 100 us
  waiting for transfers between devices  44 us (44%)
  starting transfers between devices  33.4 us (33%)
  Pallas kernels  20.6 us (21%)
  local copies, waits for them, and re-layouts  1.98 us (2%)
    ppermute x15, waiting for transfers between devices, swap(): lax.ppermute(array, 'samp', [(i, i ^ 1 << bit) for i in range(parts)])  33.2 us
    ppermute x15, starting transfers between devices, swap(): lax.ppermute(array, 'samp', [(i, i ^ 1 << bit) for i in range(parts)])  21.8 us
    pallas_call x5, Pallas kernels, gram(): pl.pallas_call(functools.partial(gram_kernel, parts, start, order), grid=...  14.8 us
    ppermute x5, starting transfers between devices, local(): lax.ppermute(dosages[:, start:start + width], 'var', route)  11.5 us
    ppermute x5, waiting for transfers between devices, local(): lax.ppermute(dosages[:, start:start + width], 'var', route)  10.8 us
    pallas_call x1, Pallas kernels, finish(): pl.pallas_call(functools.partial(finish_kernel, parts, samples, len(pairs...  2.87 us
    pallas_call x1, Pallas kernels, prepare(): pl.pallas_call(prepare_kernel, grid=(cols // width,), in_specs=[tall], ou...  2.51 us
  transfers between devices with their start and end apart: 20, of which 11 were waited for; matrix products, arithmetic and copies ran while one was open for 0% of the time, Pallas kernels for 18%

profile of v1, /device:TPU:4, one launch (start us, length us, event | category | flops | bytes accessed | tf_op | source)
XLA Modules:
  0.0 100.1 jit_solution(5701817230786287819)
XLA Ops:
  0.0 0.0 copy-start
  0.0 1.9 %fusion = (f32[768,256]{1,0:T(8,128)S(1)}, f32[768,256]{1,0:T(8,128)S(1)}, f32[768,256]{1,0:T(8,128)S(1)}) fusion(f32[768,1024]{1,0:T(8,128)} %block.1), kind=kLoop, calls=%fused_computation | loop fusion | bytes 4718592 | tf_op jit(solution)/shard_map/slice | solution.py:270
  1.9 1.9 %collective-permute-start.16 = (f32[768,256]{1,0:T(8,128)S(1)}, f32[768,256]{1,0:T(8,128)S(1)}, u32[]{:S(2)}, u32[]{:S(2)}) collective-permute-start(f32[768,256]{1,0:T(8,128)S(1)} %get-tuple-element.75), channel_id=1, source_target_pairs={{8,0},{16,8},{24,16},{9,1},{17,9},{25,17},{10,2},{18,10},{26,18},{... | collective-permute-start | bytes 2359304 | tf_op jit(solution)/shard_map/ppermute | solution.py:270
  3.9 1.9 %collective-permute-start.12 = (f32[768,256]{1,0:T(8,128)S(1)}, f32[768,256]{1,0:T(8,128)S(1)}, u32[]{:S(2)}, u32[]{:S(2)}) collective-permute-start(f32[768,256]{1,0:T(8,128)S(1)} %get-tuple-element.77), channel_id=1, source_target_pairs={{8,0},{16,8},{24,16},{9,1},{17,9},{25,17},{10,2},{18,10},{26,18},{... | collective-permute-start | bytes 2359304 | tf_op jit(solution)/shard_map/ppermute | solution.py:270
  5.8 1.9 %collective-permute-start.8 = (f32[768,256]{1,0:T(8,128)S(1)}, f32[768,256]{1,0:T(8,128)S(1)}, u32[]{:S(2)}, u32[]{:S(2)}) collective-permute-start(f32[768,256]{1,0:T(8,128)S(1)} %get-tuple-element.76), channel_id=1, source_target_pairs={{8,0},{16,8},{24,16},{9,1},{17,9},{25,17},{10,2},{18,10},{26,18},{... | collective-permute-start | bytes 2359304 | tf_op jit(solution)/shard_map/ppermute | solution.py:270
  7.7 0.0 copy-done
  7.7 0.1 fusion.1
  7.8 1.9 %collective-permute-start.4 = (f32[768,128]{1,0:T(8,128)S(1)}, f32[768,128]{1,0:T(8,128)S(1)}, u32[]{:S(2)}, u32[]{:S(2)}) collective-permute-start(f32[768,128]{1,0:T(8,128)S(1)} %get-tuple-element.78), channel_id=1, source_target_pairs={{8,0},{16,8},{24,16},{9,1},{17,9},{25,17},{10,2},{18,10},{26,18},{... | collective-permute-start | bytes 1179656 | tf_op jit(solution)/shard_map/ppermute | solution.py:270
  9.7 2.5 %prepare.1 = (bf16[768,1024]{1,0:T(8,128)(2,1)S(1)}, bf16[768,1024]{1,0:T(8,128)(2,1)S(1)}, bf16[1024,768]{1,0:T(8,128)(2,1)S(1)}, bf16[1024,768]{1,0:T(8,128)(2,1)S(1)}, f32[8,1024]{1,0:T(8,128)S(1)}) custom-call(f32[768,1024]{1,0:T(8,128)S(1)} %copy-done), custom_call_target="tpu_custom_call" | custom-call | flops 7864320 | bytes 9437184 | tf_op jit(solution)/shard_map/prepare/pallas_call | solution.py:53
  12.2 1.1 %collective-permute-done.16.ahead = f32[768,256]{1,0:T(8,128)S(1)} collective-permute-done((f32[768,256]{1,0:T(8,128)S(1)}, f32[768,256]{1,0:T(8,128)S(1)}, u32[]{:S(2)}, u32[]{:S(2)}) %collective-permute-start.16) | collective-permute-done | bytes 786464 | tf_op jit(solution)/shard_map/ppermute | solution.py:270
  13.3 3.0 %gram.9 = (f32[520,256]{1,0:T(8,128)S(1)}, f32[520,256]{1,0:T(8,128)S(1)}) custom-call(bf16[1024,768]{1,0:T(8,128)(2,1)S(1)} %get-tuple-element.40.high_t, bf16[1024,768]{1,0:T(8,128)(2,1)S(1)} %get-tuple-element.41.low_t, bf16[768,1024]{1,0:T(8,128)(2,1)S(1)} %get-tuple-element.42.high, bf16[768,1024]{1,0:T(8,128)(2,1)S(1)} %get-tuple-element.43.low, ...), custom_call_target="tpu_custom_call" | custom-call | flops 1207959552 | bytes 4718592 | tf_op jit(solution)/shard_map/gram/pallas_call | solution.py:127
  16.3 1.5 %collective-permute-start.17 = (f32[520,256]{1,0:T(8,128)S(1)}, f32[520,256]{1,0:T(8,128)S(1)}, u32[]{:S(2)}, u32[]{:S(2)}) collective-permute-start(f32[520,256]{1,0:T(8,128)S(1)} %get-tuple-element.70), channel_id=1, source_target_pairs={{0,1},{1,0},{2,3},{3,2},{4,5},{5,4},{6,7},{7,6},{8,9},{9,8},{10,11... | collective-permute-start | bytes 1597448 | tf_op jit(solution)/shard_map/ppermute | solution.py:255
  17.8 4.0 %collective-permute-done.12.ahead = f32[768,256]{1,0:T(8,128)S(1)} collective-permute-done((f32[768,256]{1,0:T(8,128)S(1)}, f32[768,256]{1,0:T(8,128)S(1)}, u32[]{:S(2)}, u32[]{:S(2)}) %collective-permute-start.12) | collective-permute-done | bytes 786464 | tf_op jit(solution)/shard_map/ppermute | solution.py:270
  21.8 2.9 %gram.8 = (f32[520,256]{1,0:T(8,128)S(1)}, f32[520,256]{1,0:T(8,128)S(1)}) custom-call(bf16[1024,768]{1,0:T(8,128)(2,1)S(1)} %get-tuple-element.40.high_t, bf16[1024,768]{1,0:T(8,128)(2,1)S(1)} %get-tuple-element.41.low_t, bf16[768,1024]{1,0:T(8,128)(2,1)S(1)} %get-tuple-element.42.high, bf16[768,1024]{1,0:T(8,128)(2,1)S(1)} %get-tuple-element.43.low, ...), custom_call_target="tpu_custom_call" | custom-call | flops 1207959552 | bytes 4718592 | tf_op jit(solution)/shard_map/gram/pallas_call | solution.py:127
  24.7 1.5 %collective-permute-start.13 = (f32[520,256]{1,0:T(8,128)S(1)}, f32[520,256]{1,0:T(8,128)S(1)}, u32[]{:S(2)}, u32[]{:S(2)}) collective-permute-start(f32[520,256]{1,0:T(8,128)S(1)} %get-tuple-element.64), channel_id=1, source_target_pairs={{0,1},{1,0},{2,3},{3,2},{4,5},{5,4},{6,7},{7,6},{8,9},{9,8},{10,11... | collective-permute-start | bytes 1597448 | tf_op jit(solution)/shard_map/ppermute | solution.py:255
  26.2 4.0 %collective-permute-done.8.ahead = f32[768,256]{1,0:T(8,128)S(1)} collective-permute-done((f32[768,256]{1,0:T(8,128)S(1)}, f32[768,256]{1,0:T(8,128)S(1)}, u32[]{:S(2)}, u32[]{:S(2)}) %collective-permute-start.8) | collective-permute-done | bytes 786464 | tf_op jit(solution)/shard_map/ppermute | solution.py:270
  30.2 2.9 %gram.7 = (f32[520,256]{1,0:T(8,128)S(1)}, f32[520,256]{1,0:T(8,128)S(1)}) custom-call(bf16[1024,768]{1,0:T(8,128)(2,1)S(1)} %get-tuple-element.40.high_t, bf16[1024,768]{1,0:T(8,128)(2,1)S(1)} %get-tuple-element.41.low_t, bf16[768,1024]{1,0:T(8,128)(2,1)S(1)} %get-tuple-element.42.high, bf16[768,1024]{1,0:T(8,128)(2,1)S(1)} %get-tuple-element.43.low, ...), custom_call_target="tpu_custom_call" | custom-call | flops 1207959552 | bytes 4718592 | tf_op jit(solution)/shard_map/gram/pallas_call | solution.py:127
  33.2 1.5 %collective-permute-start.9 = (f32[520,256]{1,0:T(8,128)S(1)}, f32[520,256]{1,0:T(8,128)S(1)}, u32[]{:S(2)}, u32[]{:S(2)}) collective-permute-start(f32[520,256]{1,0:T(8,128)S(1)} %get-tuple-element.58), channel_id=1, source_target_pairs={{0,1},{1,0},{2,3},{3,2},{4,5},{5,4},{6,7},{7,6},{8,9},{9,8},{10,11... | collective-permute-start | bytes 1597448 | tf_op jit(solution)/shard_map/ppermute | solution.py:255
  34.7 3.8 %collective-permute-start = (f32[768,128]{1,0:T(8,128)S(1)}, f32[768,128]{1,0:T(8,128)S(1)}, u32[]{:S(2)}, u32[]{:S(2)}) collective-permute-start(f32[768,128]{1,0:T(8,128)S(1)} %get-tuple-element.79), channel_id=1, source_target_pairs={{8,0},{16,8},{24,16},{9,1},{17,9},{25,17},{10,2},{18,10},{26,18},{... | collective-permute-start | bytes 1179656 | tf_op jit(solution)/shard_map/ppermute | solution.py:270
  38.5 0.0 collective-permute-done.4.ahead
  38.5 2.8 %gram.6 = (f32[520,128]{1,0:T(8,128)S(1)}, f32[520,128]{1,0:T(8,128)S(1)}) custom-call(bf16[1024,768]{1,0:T(8,128)(2,1)S(1)} %get-tuple-element.40.high_t, bf16[1024,768]{1,0:T(8,128)(2,1)S(1)} %get-tuple-element.41.low_t, bf16[768,1024]{1,0:T(8,128)(2,1)S(1)} %get-tuple-element.42.high, bf16[768,1024]{1,0:T(8,128)(2,1)S(1)} %get-tuple-element.43.low, ...), custom_call_target="tpu_custom_call" | custom-call | flops 603979776 | bytes 3932160 | tf_op jit(solution)/shard_map/gram/pallas_call | solution.py:127
  41.4 0.6 collective-permute-start.5
  42.0 1.8 %collective-permute-done.ahead = f32[768,128]{1,0:T(8,128)S(1)} collective-permute-done((f32[768,128]{1,0:T(8,128)S(1)}, f32[768,128]{1,0:T(8,128)S(1)}, u32[]{:S(2)}, u32[]{:S(2)}) %collective-permute-start) | collective-permute-done | bytes 393248 | tf_op jit(solution)/shard_map/ppermute | solution.py:270
  43.8 3.1 %gram.5 = (f32[520,128]{1,0:T(8,128)S(1)}, f32[520,128]{1,0:T(8,128)S(1)}) custom-call(bf16[1024,768]{1,0:T(8,128)(2,1)S(1)} %get-tuple-element.40.high_t, bf16[1024,768]{1,0:T(8,128)(2,1)S(1)} %get-tuple-element.41.low_t, bf16[768,1024]{1,0:T(8,128)(2,1)S(1)} %get-tuple-element.42.high, bf16[768,1024]{1,0:T(8,128)(2,1)S(1)} %get-tuple-element.43.low, ...), custom_call_target="tpu_custom_call" | custom-call | flops 603979776 | bytes 3932160 | tf_op jit(solution)/shard_map/gram/pallas_call | solution.py:127
  46.9 0.6 collective-permute-start.1
  47.5 0.0 collective-permute-done.17.got
  47.5 0.1 halve.18
  47.6 1.6 %collective-permute-start.18 = (f32[272,256]{1,0:T(8,128)S(1)}, f32[272,256]{1,0:T(8,128)S(1)}, u32[]{:S(2)}, u32[]{:S(2)}) collective-permute-start(f32[272,256]{1,0:T(8,128)S(1)} %get-tuple-element.72), channel_id=1, source_target_pairs={{0,2},{1,3},{2,0},{3,1},{4,6},{5,7},{6,4},{7,5},{8,10},{9,11},{10,... | collective-permute-start | bytes 835592 | tf_op jit(solution)/shard_map/ppermute | solution.py:255
  49.2 0.0 collective-permute-done.13.got
  49.2 0.1 halve.16
  49.3 0.5 collective-permute-start.14
  49.8 4.4 %collective-permute-done.9.got = f32[520,256]{1,0:T(8,128)S(1)} collective-permute-done((f32[520,256]{1,0:T(8,128)S(1)}, f32[520,256]{1,0:T(8,128)S(1)}, u32[]{:S(2)}, u32[]{:S(2)}) %collective-permute-start.9) | collective-permute-done | bytes 532512 | tf_op jit(solution)/shard_map/ppermute | solution.py:255
  54.2 0.1 halve.14
  54.3 1.6 %collective-permute-start.10 = (f32[272,256]{1,0:T(8,128)S(1)}, f32[272,256]{1,0:T(8,128)S(1)}, u32[]{:S(2)}, u32[]{:S(2)}) collective-permute-start(f32[272,256]{1,0:T(8,128)S(1)} %get-tuple-element.60), channel_id=1, source_target_pairs={{0,2},{1,3},{2,0},{3,1},{4,6},{5,7},{6,4},{7,5},{8,10},{9,11},{10,... | collective-permute-start | bytes 835592 | tf_op jit(solution)/shard_map/ppermute | solution.py:255
  55.9 4.0 %collective-permute-done.5.got = f32[520,128]{1,0:T(8,128)S(1)} collective-permute-done((f32[520,128]{1,0:T(8,128)S(1)}, f32[520,128]{1,0:T(8,128)S(1)}, u32[]{:S(2)}, u32[]{:S(2)}) %collective-permute-start.5) | collective-permute-done | bytes 266272 | tf_op jit(solution)/shard_map/ppermute | solution.py:255
  59.9 1.6 %collective-permute-start.6 = (f32[272,128]{1,0:T(8,128)S(1)}, f32[272,128]{1,0:T(8,128)S(1)}, u32[]{:S(2)}, u32[]{:S(2)}) collective-permute-start(f32[272,128]{1,0:T(8,128)S(1)} %get-tuple-element.54), channel_id=1, source_target_pairs={{0,2},{1,3},{2,0},{3,1},{4,6},{5,7},{6,4},{7,5},{8,10},{9,11},{10,... | collective-permute-start | bytes 417800 | tf_op jit(solution)/shard_map/ppermute | solution.py:255
  61.5 2.8 %collective-permute-done.1.got = f32[520,128]{1,0:T(8,128)S(1)} collective-permute-done((f32[520,128]{1,0:T(8,128)S(1)}, f32[520,128]{1,0:T(8,128)S(1)}, u32[]{:S(2)}, u32[]{:S(2)}) %collective-permute-start.1) | collective-permute-done | bytes 266272 | tf_op jit(solution)/shard_map/ppermute | solution.py:255
  64.4 1.9 %collective-permute-start.2 = (f32[272,128]{1,0:T(8,128)S(1)}, f32[272,128]{1,0:T(8,128)S(1)}, u32[]{:S(2)}, u32[]{:S(2)}) collective-permute-start(f32[272,128]{1,0:T(8,128)S(1)} %get-tuple-element.48), channel_id=1, source_target_pairs={{0,2},{1,3},{2,0},{3,1},{4,6},{5,7},{6,4},{7,5},{8,10},{9,11},{10,... | collective-permute-start | bytes 417800 | tf_op jit(solution)/shard_map/ppermute | solution.py:255
  66.3 0.0 collective-permute-done.18.got
  66.4 2.7 %collective-permute-start.19 = (f32[160,256]{1,0:T(8,128)S(1)}, f32[160,256]{1,0:T(8,128)S(1)}, u32[]{:S(2)}, u32[]{:S(2)}) collective-permute-start(f32[160,256]{1,0:T(8,128)S(1)} %get-tuple-element.74), channel_id=1, source_target_pairs={{0,4},{1,5},{2,6},{3,7},{4,0},{5,1},{6,2},{7,3},{8,12},{9,13},{10,... | collective-permute-start | bytes 491528 | tf_op jit(solution)/shard_map/ppermute | solution.py:255
  69.0 0.0 collective-permute-done.14.got
  69.0 0.4 collective-permute-start.15
  69.5 0.0 collective-permute-done.10.got
  69.5 2.7 %collective-permute-start.11 = (f32[160,256]{1,0:T(8,128)S(1)}, f32[160,256]{1,0:T(8,128)S(1)}, u32[]{:S(2)}, u32[]{:S(2)}) collective-permute-start(f32[160,256]{1,0:T(8,128)S(1)} %get-tuple-element.62), channel_id=1, source_target_pairs={{0,4},{1,5},{2,6},{3,7},{4,0},{5,1},{6,2},{7,3},{8,12},{9,13},{10,... | collective-permute-start | bytes 491528 | tf_op jit(solution)/shard_map/ppermute | solution.py:255
  72.1 0.8 collective-permute-done.6.got
  72.9 2.2 %collective-permute-start.7 = (f32[160,128]{1,0:T(8,128)S(1)}, f32[160,128]{1,0:T(8,128)S(1)}, u32[]{:S(2)}, u32[]{:S(2)}) collective-permute-start(f32[160,128]{1,0:T(8,128)S(1)} %get-tuple-element.56), channel_id=1, source_target_pairs={{0,4},{1,5},{2,6},{3,7},{4,0},{5,1},{6,2},{7,3},{8,12},{9,13},{10,... | collective-permute-start | bytes 245768 | tf_op jit(solution)/shard_map/ppermute | solution.py:255
  75.1 0.5 collective-permute-done.2.got
  75.6 0.9 collective-permute-start.3
  76.6 19.8 %collective-permute-done.7.refs_3_ = f32[160,128]{1,0:T(8,128)S(1)} collective-permute-done((f32[160,128]{1,0:T(8,128)S(1)}, f32[160,128]{1,0:T(8,128)S(1)}, u32[]{:S(2)}, u32[]{:S(2)}) %collective-permute-start.7) | collective-permute-done | bytes 81952 | tf_op jit(solution)/shard_map/ppermute | solution.py:255
  96.3 0.9 collective-permute-done.3.refs_1_
  97.2 0.0 collective-permute-done.19.refs_9_
  97.2 0.0 collective-permute-done.15.refs_7_
  97.2 0.0 collective-permute-done.11.refs_5_
  97.2 2.9 %finish.1 = f32[128,1024]{1,0:T(8,128)} custom-call(f32[160,128]{1,0:T(8,128)S(1)} %get-tuple-element.49.refs_0_, f32[160,128]{1,0:T(8,128)S(1)} %collective-permute-done.3.refs_1_, f32[160,128]{1,0:T(8,128)S(1)} %get-tuple-element.55.refs_2_, f32[160,128]{1,0:T(8,128)S(1)} %collective-permute-done.7.refs_3_, f32[160,256]{1,0:T(8,128)S(1)} %get-tuple-element.61.refs_4_, ...), custom_call_target="tpu_custom_call" | custom-call | flops 5242880 | bytes 2097152 | tf_op jit(solution)/shard_map/finish/pallas_call | solution.py:238
  (7 shorter events, 0.2 us)
Async XLA Ops:
  0.0 7.7 %copy-start = (f32[768,1024]{1,0:T(8,128)S(1)}, f32[768,1024]{1,0:T(8,128)}, u32[]{:S(2)}) copy-start(f32[768,1024]{1,0:T(8,128)} %block.1) | copy-start | bytes 9437188
  1.9 11.4 %collective-permute-start.16 = (f32[768,256]{1,0:T(8,128)S(1)}, f32[768,256]{1,0:T(8,128)S(1)}, u32[]{:S(2)}, u32[]{:S(2)}) collective-permute-start(f32[768,256]{1,0:T(8,128)S(1)} %get-tuple-element.75), channel_id=1, source_target_pairs={{8,0},{16,8},{24,16},{9,1},{17,9},{25,17},{10,2},{18,10},{26,18},{... | collective-permute-start | bytes 2359304 | tf_op jit(solution)/shard_map/ppermute | solution.py:270
  3.9 17.9 %collective-permute-start.12 = (f32[768,256]{1,0:T(8,128)S(1)}, f32[768,256]{1,0:T(8,128)S(1)}, u32[]{:S(2)}, u32[]{:S(2)}) collective-permute-start(f32[768,256]{1,0:T(8,128)S(1)} %get-tuple-element.77), channel_id=1, source_target_pairs={{8,0},{16,8},{24,16},{9,1},{17,9},{25,17},{10,2},{18,10},{26,18},{... | collective-permute-start | bytes 2359304 | tf_op jit(solution)/shard_map/ppermute | solution.py:270
  5.8 24.4 %collective-permute-start.8 = (f32[768,256]{1,0:T(8,128)S(1)}, f32[768,256]{1,0:T(8,128)S(1)}, u32[]{:S(2)}, u32[]{:S(2)}) collective-permute-start(f32[768,256]{1,0:T(8,128)S(1)} %get-tuple-element.76), channel_id=1, source_target_pairs={{8,0},{16,8},{24,16},{9,1},{17,9},{25,17},{10,2},{18,10},{26,18},{... | collective-permute-start | bytes 2359304 | tf_op jit(solution)/shard_map/ppermute | solution.py:270
  7.8 30.7 %collective-permute-start.4 = (f32[768,128]{1,0:T(8,128)S(1)}, f32[768,128]{1,0:T(8,128)S(1)}, u32[]{:S(2)}, u32[]{:S(2)}) collective-permute-start(f32[768,128]{1,0:T(8,128)S(1)} %get-tuple-element.78), channel_id=1, source_target_pairs={{8,0},{16,8},{24,16},{9,1},{17,9},{25,17},{10,2},{18,10},{26,18},{... | collective-permute-start | bytes 1179656 | tf_op jit(solution)/shard_map/ppermute | solution.py:270
  16.3 31.2 %collective-permute-start.17 = (f32[520,256]{1,0:T(8,128)S(1)}, f32[520,256]{1,0:T(8,128)S(1)}, u32[]{:S(2)}, u32[]{:S(2)}) collective-permute-start(f32[520,256]{1,0:T(8,128)S(1)} %get-tuple-element.70), channel_id=1, source_target_pairs={{0,1},{1,0},{2,3},{3,2},{4,5},{5,4},{6,7},{7,6},{8,9},{9,8},{10,11... | collective-permute-start | bytes 1597448 | tf_op jit(solution)/shard_map/ppermute | solution.py:255
  24.7 24.5 %collective-permute-start.13 = (f32[520,256]{1,0:T(8,128)S(1)}, f32[520,256]{1,0:T(8,128)S(1)}, u32[]{:S(2)}, u32[]{:S(2)}) collective-permute-start(f32[520,256]{1,0:T(8,128)S(1)} %get-tuple-element.64), channel_id=1, source_target_pairs={{0,1},{1,0},{2,3},{3,2},{4,5},{5,4},{6,7},{7,6},{8,9},{9,8},{10,11... | collective-permute-start | bytes 1597448 | tf_op jit(solution)/shard_map/ppermute | solution.py:255
  33.2 21.1 %collective-permute-start.9 = (f32[520,256]{1,0:T(8,128)S(1)}, f32[520,256]{1,0:T(8,128)S(1)}, u32[]{:S(2)}, u32[]{:S(2)}) collective-permute-start(f32[520,256]{1,0:T(8,128)S(1)} %get-tuple-element.58), channel_id=1, source_target_pairs={{0,1},{1,0},{2,3},{3,2},{4,5},{5,4},{6,7},{7,6},{8,9},{9,8},{10,11... | collective-permute-start | bytes 1597448 | tf_op jit(solution)/shard_map/ppermute | solution.py:255
  34.7 9.1 %collective-permute-start = (f32[768,128]{1,0:T(8,128)S(1)}, f32[768,128]{1,0:T(8,128)S(1)}, u32[]{:S(2)}, u32[]{:S(2)}) collective-permute-start(f32[768,128]{1,0:T(8,128)S(1)} %get-tuple-element.79), channel_id=1, source_target_pairs={{8,0},{16,8},{24,16},{9,1},{17,9},{25,17},{10,2},{18,10},{26,18},{... | collective-permute-start | bytes 1179656 | tf_op jit(solution)/shard_map/ppermute | solution.py:270
  41.4 18.5 %collective-permute-start.5 = (f32[520,128]{1,0:T(8,128)S(1)}, f32[520,128]{1,0:T(8,128)S(1)}, u32[]{:S(2)}, u32[]{:S(2)}) collective-permute-start(f32[520,128]{1,0:T(8,128)S(1)} %get-tuple-element.52), channel_id=1, source_target_pairs={{0,1},{1,0},{2,3},{3,2},{4,5},{5,4},{6,7},{7,6},{8,9},{9,8},{10,11... | collective-permute-start | bytes 798728 | tf_op jit(solution)/shard_map/ppermute | solution.py:255
  46.9 17.4 %collective-permute-start.1 = (f32[520,128]{1,0:T(8,128)S(1)}, f32[520,128]{1,0:T(8,128)S(1)}, u32[]{:S(2)}, u32[]{:S(2)}) collective-permute-start(f32[520,128]{1,0:T(8,128)S(1)} %get-tuple-element.46), channel_id=1, source_target_pairs={{0,1},{1,0},{2,3},{3,2},{4,5},{5,4},{6,7},{7,6},{8,9},{9,8},{10,11... | collective-permute-start | bytes 798728 | tf_op jit(solution)/shard_map/ppermute | solution.py:255
  47.6 18.7 %collective-permute-start.18 = (f32[272,256]{1,0:T(8,128)S(1)}, f32[272,256]{1,0:T(8,128)S(1)}, u32[]{:S(2)}, u32[]{:S(2)}) collective-permute-start(f32[272,256]{1,0:T(8,128)S(1)} %get-tuple-element.72), channel_id=1, source_target_pairs={{0,2},{1,3},{2,0},{3,1},{4,6},{5,7},{6,4},{7,5},{8,10},{9,11},{10,... | collective-permute-start | bytes 835592 | tf_op jit(solution)/shard_map/ppermute | solution.py:255
  49.3 19.7 %collective-permute-start.14 = (f32[272,256]{1,0:T(8,128)S(1)}, f32[272,256]{1,0:T(8,128)S(1)}, u32[]{:S(2)}, u32[]{:S(2)}) collective-permute-start(f32[272,256]{1,0:T(8,128)S(1)} %get-tuple-element.66), channel_id=1, source_target_pairs={{0,2},{1,3},{2,0},{3,1},{4,6},{5,7},{6,4},{7,5},{8,10},{9,11},{10,... | collective-permute-start | bytes 835592 | tf_op jit(solution)/shard_map/ppermute | solution.py:255
  54.3 15.2 %collective-permute-start.10 = (f32[272,256]{1,0:T(8,128)S(1)}, f32[272,256]{1,0:T(8,128)S(1)}, u32[]{:S(2)}, u32[]{:S(2)}) collective-permute-start(f32[272,256]{1,0:T(8,128)S(1)} %get-tuple-element.60), channel_id=1, source_target_pairs={{0,2},{1,3},{2,0},{3,1},{4,6},{5,7},{6,4},{7,5},{8,10},{9,11},{10,... | collective-permute-start | bytes 835592 | tf_op jit(solution)/shard_map/ppermute | solution.py:255
  59.9 13.0 %collective-permute-start.6 = (f32[272,128]{1,0:T(8,128)S(1)}, f32[272,128]{1,0:T(8,128)S(1)}, u32[]{:S(2)}, u32[]{:S(2)}) collective-permute-start(f32[272,128]{1,0:T(8,128)S(1)} %get-tuple-element.54), channel_id=1, source_target_pairs={{0,2},{1,3},{2,0},{3,1},{4,6},{5,7},{6,4},{7,5},{8,10},{9,11},{10,... | collective-permute-start | bytes 417800 | tf_op jit(solution)/shard_map/ppermute | solution.py:255
  64.4 11.2 %collective-permute-start.2 = (f32[272,128]{1,0:T(8,128)S(1)}, f32[272,128]{1,0:T(8,128)S(1)}, u32[]{:S(2)}, u32[]{:S(2)}) collective-permute-start(f32[272,128]{1,0:T(8,128)S(1)} %get-tuple-element.48), channel_id=1, source_target_pairs={{0,2},{1,3},{2,0},{3,1},{4,6},{5,7},{6,4},{7,5},{8,10},{9,11},{10,... | collective-permute-start | bytes 417800 | tf_op jit(solution)/shard_map/ppermute | solution.py:255
  66.4 30.9 %collective-permute-start.19 = (f32[160,256]{1,0:T(8,128)S(1)}, f32[160,256]{1,0:T(8,128)S(1)}, u32[]{:S(2)}, u32[]{:S(2)}) collective-permute-start(f32[160,256]{1,0:T(8,128)S(1)} %get-tuple-element.74), channel_id=1, source_target_pairs={{0,4},{1,5},{2,6},{3,7},{4,0},{5,1},{6,2},{7,3},{8,12},{9,13},{10,... | collective-permute-start | bytes 491528 | tf_op jit(solution)/shard_map/ppermute | solution.py:255
  69.0 28.2 %collective-permute-start.15 = (f32[160,256]{1,0:T(8,128)S(1)}, f32[160,256]{1,0:T(8,128)S(1)}, u32[]{:S(2)}, u32[]{:S(2)}) collective-permute-start(f32[160,256]{1,0:T(8,128)S(1)} %get-tuple-element.68), channel_id=1, source_target_pairs={{0,4},{1,5},{2,6},{3,7},{4,0},{5,1},{6,2},{7,3},{8,12},{9,13},{10,... | collective-permute-start | bytes 491528 | tf_op jit(solution)/shard_map/ppermute | solution.py:255
  69.5 27.7 %collective-permute-start.11 = (f32[160,256]{1,0:T(8,128)S(1)}, f32[160,256]{1,0:T(8,128)S(1)}, u32[]{:S(2)}, u32[]{:S(2)}) collective-permute-start(f32[160,256]{1,0:T(8,128)S(1)} %get-tuple-element.62), channel_id=1, source_target_pairs={{0,4},{1,5},{2,6},{3,7},{4,0},{5,1},{6,2},{7,3},{8,12},{9,13},{10,... | collective-permute-start | bytes 491528 | tf_op jit(solution)/shard_map/ppermute | solution.py:255
  72.9 23.4 %collective-permute-start.7 = (f32[160,128]{1,0:T(8,128)S(1)}, f32[160,128]{1,0:T(8,128)S(1)}, u32[]{:S(2)}, u32[]{:S(2)}) collective-permute-start(f32[160,128]{1,0:T(8,128)S(1)} %get-tuple-element.56), channel_id=1, source_target_pairs={{0,4},{1,5},{2,6},{3,7},{4,0},{5,1},{6,2},{7,3},{8,12},{9,13},{10,... | collective-permute-start | bytes 245768 | tf_op jit(solution)/shard_map/ppermute | solution.py:255
  75.6 21.6 %collective-permute-start.3 = (f32[160,128]{1,0:T(8,128)S(1)}, f32[160,128]{1,0:T(8,128)S(1)}, u32[]{:S(2)}, u32[]{:S(2)}) collective-permute-start(f32[160,128]{1,0:T(8,128)S(1)} %get-tuple-element.50), channel_id=1, source_target_pairs={{0,4},{1,5},{2,6},{3,7},{4,0},{5,1},{6,2},{7,3},{8,12},{9,13},{10,... | collective-permute-start | bytes 245768 | tf_op jit(solution)/shard_map/ppermute | solution.py:255

commit v2 on v1

--- a/solution.py
+++ b/solution.py
@@ -10,6 +10,7 @@
 EPS = 1e-06
 STATS = 8
 VMEM = pl.BlockSpec(memory_space=pltpu.VMEM)
+ANY = pl.BlockSpec(memory_space=pl.ANY)
 
 
 def params(mib):
@@ -76,74 +77,102 @@
     return dot(a, high) + (dot(a, low) + dot(b, high))
 
 
-def gram_kernel(parts, start, order, high_t, low_t, high, low, own_stats, ahead, send, keep):
+def gram_kernel(piece, spots, order, high_t, low_t, high, low, own_stats, *refs):
+    first, last, start, width = piece
+    send, keep = refs[-2:]
     cols = high_t.shape[0]
-    width = ahead.shape[1]
-    share = cols // parts
-    half = parts // 2
+    share = (last - first) // spots
+    half = spots // 2
     me = lax.axis_index("samp")
-    centred, mean, left, squares = centre(ahead[...])
-    ahead_high, ahead_low = split(centred)
     own_high, own_low = high[...], low[...]
     mine = own_stats[...]
-    rows = [mine[0:1], mean, mine[2:3], left, mine[4:5], squares, mine[6:8]]
-    stats = jnp.concatenate(rows, 0)
-    send[half * share :, :] = stats
-    keep[half * share :, :] = stats
-    for first in range(0, cols, width):
-        band = pl.ds(first, width)
-        if first <= start:
+    if last > start:
+        centred, mean, left, squares = centre(refs[0][...])
+        ahead_high, ahead_low = split(centred)
+        rows = [mine[0:1], mean, mine[2:3], left, mine[4:5], squares, mine[6:8]]
+        mine = jnp.concatenate(rows, 0)
+    send[half * share :, :] = mine
+    keep[half * share :, :] = mine
+    tall = min(width, 2 * cols // 8)
+    for top in range(first, last, tall):
+        band = pl.ds(top, tall)
+        if top < start + width:
             tile = product(high_t, low_t, band, own_high, own_low)
-        if first >= start:
+        if top + tall > start:
             later = product(high_t, low_t, band, ahead_high, ahead_low)
-        if first > start:
-            tile = later
-        if first == start:
-            row = lax.broadcasted_iota(jnp.int32, tile.shape, 0)
-            col = lax.broadcasted_iota(jnp.int32, tile.shape, 1)
-            tile = jnp.where(col > row, tile, later)
-        for part in range(width // share):
-            spot = place(first // share + part, me, order)
-            piece = tile[part * share : (part + 1) * share]
+            if top >= start + width:
+                tile = later
+            else:
+                row = lax.broadcasted_iota(jnp.int32, tile.shape, 0) + top
+                col = lax.broadcasted_iota(jnp.int32, tile.shape, 1) + start
+                tile = jnp.where(col > row, tile, later)
+        for part in range(tall // share):
+            spot = place(top // share + part, me, order)
+            block = tile[part * share : (part + 1) * share]
             there = pl.ds(pl.multiple_of((spot & (half - 1)) * share, share), share)
 
             @pl.when(spot >= half)
             def _():
-                send[there, :] = piece
+                send[there, :] = block
 
             @pl.when(spot < half)
             def _():
-                keep[there, :] = piece
-
-
-def gram(parts, start, order, high_t, low_t, high, low, stats, ahead):
+                keep[there, :] = block
+
+
+def gram(piece, spots, order, prepared, ahead, after):
+    high, low, high_t, low_t, stats = prepared
+    first, last, start, width = piece
     cols, samples = high_t.shape
-    width = ahead.shape[1]
     index = start // width
     tall = pl.BlockSpec((samples, width), lambda i: (0, index))
     whole = pl.BlockSpec((cols, samples), lambda i: (0, 0))
-    shape = (cols // 2 + STATS, width)
+    shape = ((last - first) // 2 + STATS, width)
     out = jax.ShapeDtypeStruct(shape, jnp.float32)
-    return pl.pallas_call(
-        functools.partial(gram_kernel, parts, start, order),
+    extra = [] if ahead is None else [ahead]
+    return pl.pallas_call(
+        functools.partial(gram_kernel, piece, spots, order),
         grid=(1,),
-        in_specs=[
-            whole,
-            whole,
-            tall,
-            tall,
-            pl.BlockSpec((STATS, width), lambda i: (0, index)),
-            pl.BlockSpec((samples, width), lambda i: (0, 0)),
-        ],
+        in_specs=[whole, whole, tall, tall, pl.BlockSpec((STATS, width), lambda i: (0, index))]
+        + [pl.BlockSpec((samples, width), lambda i: (0, 0))] * len(extra)
+        + [ANY] * len(after),
         out_specs=[pl.BlockSpec(shape, lambda i: (0, 0))] * 2,
         out_shape=[out, out],
         compiler_params=params(40),
-        cost_estimate=cost(6 * cols * width * samples, 4 * samples * (cols + 2 * width)),
+        cost_estimate=cost(6 * (last - first) * width * samples, 4 * samples * (cols + 2 * width)),
         name="gram",
-    )(high_t, low_t, high, low, stats, ahead)
-
-
-def halve_kernel(size, keep, got, send, rest):
+    )(high_t, low_t, high, low, stats, *extra, *after)
+
+
+def cut_kernel(width, count, source, *refs):
+    outs, done = refs[-1 - count : -1], refs[-1]
+    copies = []
+    for i, out in enumerate(outs):
+        taken = source.at[:, pl.ds((i + 1) * width, width)]
+        copies.append(pltpu.make_async_copy(taken, out, done.at[i]))
+    for copy in copies:
+        copy.start()
+    for copy in copies:
+        copy.wait()
+
+
+def cut(dosages, width, after):
+    samples, cols = dosages.shape
+    count = cols // width - 1
+    block = jax.ShapeDtypeStruct((samples, width), dosages.dtype)
+    return pl.pallas_call(
+        functools.partial(cut_kernel, width, count),
+        in_specs=[ANY] * (1 + len(after)),
+        out_specs=[ANY] * count,
+        out_shape=[block] * count,
+        scratch_shapes=[pltpu.SemaphoreType.DMA((count,))],
+        cost_estimate=cost(0, 8 * samples * cols),
+        name="cut",
+    )(dosages, *after)
+
+
+def halve_kernel(size, keep, got, *refs):
+    send, rest = refs[-2:]
     half = size // 2
     send[:half, :] = keep[half:size, :] + got[half:size, :]
     rest[:half, :] = keep[:half, :] + got[:half, :]
@@ -153,31 +182,57 @@
         out[half + stats :, :] = got[size:, :]
 
 
-def halve(size, keep, got):
+def merge_kernel(size, keep, got, *refs):
+    out = refs[-1]
+    out[:size, :] = keep[:size, :] + got[:size, :]
+    stats = keep.shape[0] - size
+    out[size : size + stats, :] = keep[size:, :]
+    out[size + stats :, :] = got[size:, :]
+
+
+def halve(size, pair, after):
+    keep, got = pair
     stats = keep.shape[0] - size
     shape = (size // 2 + 2 * stats, keep.shape[1])
     out = jax.ShapeDtypeStruct(shape, jnp.float32)
     return pl.pallas_call(
         functools.partial(halve_kernel, size),
-        in_specs=[VMEM, VMEM],
+        in_specs=[VMEM, VMEM] + [ANY] * len(after),
         out_specs=[VMEM, VMEM],
         out_shape=[out, out],
         compiler_params=params(16),
         cost_estimate=cost(size * keep.shape[1], 16 * size * keep.shape[1]),
         name="halve",
-    )(keep, got)
-
-
-def finish_kernel(parts, samples, pieces, *refs):
+    )(keep, got, *after)
+
+
+def merge(size, pair, after):
+    keep, got = pair
+    stats = keep.shape[0] - size
+    shape = (size + 2 * stats, keep.shape[1])
+    return pl.pallas_call(
+        functools.partial(merge_kernel, size),
+        in_specs=[VMEM, VMEM] + [ANY] * len(after),
+        out_specs=VMEM,
+        out_shape=jax.ShapeDtypeStruct(shape, jnp.float32),
+        compiler_params=params(16),
+        cost_estimate=cost(size * keep.shape[1], 16 * size * keep.shape[1]),
+        name="merge",
+    )(keep, got, *after)
+
+
+def finish_kernel(parts, samples, starts, uses, *refs):
+    pieces = len(starts)
     out, body, marks, scales = refs[2 * pieces :]
     share, cols = out.shape
     total = samples * parts
     me = lax.axis_index("samp")
-    start = 0
-    for i in range(pieces):
+    upper = me >= parts // 2
+
+    def take(i):
         keep, got = refs[2 * i], refs[2 * i + 1]
         width = keep.shape[1]
-        here = slice(start, start + width)
+        here = slice(starts[i], starts[i] + width)
         body[:, here] = keep[:share, :] + got[:share, :]
         half = parts // 2
         stats = jnp.concatenate(
@@ -193,7 +248,12 @@
         spread = (squares[4:6] + (moved[0:2] - moved[2:4])) / total
         marks[:, here] = mark.reshape(parts * STATS, width)
         scales[0:2, here] = lax.rsqrt(spread + EPS)
-        start += width
+
+    for i in range(pieces):
+        if uses[i] is None:
+            take(i)
+        else:
+            pl.when(upper == uses[i])(functools.partial(take, i))
     first = me * share
     if share % 128 == 0:
         window = pl.ds(pl.multiple_of(first, 128), share)
@@ -233,10 +293,10 @@
     out[...] = turned
 
 
-def finish(parts, samples, share, cols, pairs):
+def finish(parts, samples, share, cols, starts, uses, pairs):
     flat = [array for pair in pairs for array in pair]
     return pl.pallas_call(
-        functools.partial(finish_kernel, parts, samples, len(pairs)),
+        functools.partial(finish_kernel, parts, samples, starts, uses),
         in_specs=[VMEM] * len(flat),
         out_specs=VMEM,
         out_shape=jax.ShapeDtypeStruct((share, cols), jnp.float32),
@@ -255,32 +315,71 @@
     return lax.ppermute(array, "samp", [(i, i ^ (1 << bit)) for i in range(parts)])
 
 
+def hand_over(array, upper, parts):
+    half = parts // 2
+    return lax.ppermute(array, "samp", [(i, i ^ half) for i in range(parts) if (i >= half) != upper])
+
+
 def local(dosages):
     samples, cols = dosages.shape
     parts = lax.axis_size("samp")
     blocks = lax.axis_size("var")
     share = cols // parts
     steps = parts.bit_length() - 1
-    unit = cols // 8
-    widths = [unit, unit, 2 * unit, 2 * unit, 2 * unit]
-    starts = [sum(widths[:i]) for i in range(len(widths))]
+    quarter, half = cols // 4, cols // 2
     route = [(i, i - 1) for i in range(1, blocks)]
-    order = tuple(range(steps))
-    ahead = [
-        lax.ppermute(dosages[:, start : start + width], "var", route)
-        for start, width in zip(starts, widths)
+    pieces = [
+        (0, half, half, half),
+        (0, cols, 0, quarter),
+        (0, cols, quarter, quarter),
+        (half, cols, half, quarter),
+        (half, cols, half + quarter, quarter),
     ]
-    high, low, high_t, low_t, stats = prepare(dosages, 2 * unit)
-    pairs = []
-    for start, block in zip(starts, ahead):
-        send, keep = gram(parts, start, order, high_t, low_t, high, low, stats, block)
-        size = cols // 2
-        for step in order[:-1]:
-            got = swap(send, step, parts)
-            send, keep = halve(size, keep, got)
-            size //= 2
-        pairs.append((keep, swap(send, order[-1], parts)))
-    return finish(parts, samples, share, cols, pairs)
+    uses = [False, None, None, True, True]
+
+    first = lax.ppermute(dosages[:, :quarter], "var", route)
+    prepared = prepare(dosages, quarter)
+    last = prepared[-1]
+    pairs = {}
+    ahead = [None, first]
+
+    def begin(i):
+        nonlocal last
+        piece = pieces[i]
+        whole = uses[i] is None
+        spots = parts if whole else parts // 2
+        order = tuple(range(steps if whole else steps - 1))
+        send, keep = gram(piece, spots, order, prepared, ahead[i], [last])
+        last = keep
+        pairs[i] = (keep, swap(send, 0, parts))
+
+    def advance(i, step):
+        nonlocal last
+        top = steps - 1
+        size = (pieces[i][1] - pieces[i][0]) >> step
+        if step < top or uses[i] is None:
+            send, keep = halve(size, pairs[i], [last])
+            pairs[i] = (keep, swap(send, step, parts))
+        else:
+            keep = merge(size, pairs[i], [last])
+            pairs[i] = (keep, hand_over(keep, uses[i], parts))
+        last = keep
+
+    begin(0)
+    ahead += [
+        lax.ppermute(block, "var", route) for block in cut(dosages, quarter, [last])
+    ]
+    plan = [(1, 0), (0, 1), (2, 0), (0, 2), (3, 0), (1, 1), (4, 0), (1, 2), (2, 1), (3, 1), (2, 2), (4, 1), (3, 2), (4, 2)]
+    for i, step in plan:
+        if step == 0:
+            begin(i)
+        elif step < steps:
+            advance(i, step)
+    for step in range(3, steps):
+        for i in range(len(pieces)):
+            advance(i, step)
+    starts = [piece[2] for piece in pieces]
+    return finish(parts, samples, share, cols, starts, uses, [pairs[i] for i in range(len(pieces))])
 
 
 def solution(mesh):

time: 100 us -> 176 us (1.76)
  the two profiles are of different devices: /device:TPU:4 before, /device:TPU:28 now
where the time goes in v2:
time: 176 us; the launch traced here: 175 us
  Pallas kernels  91.1 us (52%)
  waiting for transfers between devices  47.2 us (27%)
  starting transfers between devices  27.5 us (16%)
  local copies, waits for them, and re-layouts  9.46 us (5%)
    pallas_call x1, Pallas kernels, cut(): pl.pallas_call(functools.partial(cut_kernel, width, count), in_specs=[ANY...  72.6 us
    ppermute x12, waiting for transfers between devices, swap(): lax.ppermute(array, 'samp', [(i, i ^ 1 << bit) for i in range(parts)])  41.5 us
    ppermute x12, starting transfers between devices, swap(): lax.ppermute(array, 'samp', [(i, i ^ 1 << bit) for i in range(parts)])  14.4 us
    pallas_call x5, Pallas kernels, gram(): pl.pallas_call(functools.partial(gram_kernel, piece, spots, order), grid=...  12.7 us
    unnamed x16, local copies, waits for them, and re-layouts  7.4 us
    ppermute x3, starting transfers between devices, local(): lax.ppermute(block, 'var', route)  6.35 us
    ppermute x3, waiting for transfers between devices, hand_over(): lax.ppermute(array, 'samp', [(i, i ^ half) for i in range(parts) if (i >=...  5.62 us
    ppermute x3, starting transfers between devices, hand_over(): lax.ppermute(array, 'samp', [(i, i ^ half) for i in range(parts) if (i >=...  4.84 us
  transfers between devices with their start and end apart: 19, of which 12 were waited for; matrix products, arithmetic and copies ran while one was open for 0% of the time, Pallas kernels for 50%

profile of v2, /device:TPU:28, one launch (start us, length us, event | category | flops | bytes accessed | tf_op | source)
XLA Modules:
  0.0 175.5 jit_solution(4611449128051136602)
XLA Ops:
  0.0 2.1 %slice.3 = f32[768,256]{1,0:T(8,128)} slice(f32[768,1024]{1,0:T(8,128)} %source.1), slice={[0:768], [0:256]} | slice | bytes 1572864 | tf_op jit(solution)/shard_map/slice | solution.py:340
  2.1 1.9 %collective-permute-start.1 = (f32[768,256]{1,0:T(8,128)}, f32[768,256]{1,0:T(8,128)}, u32[]{:S(2)}, u32[]{:S(2)}) collective-permute-start(f32[768,256]{1,0:T(8,128)} %slice.3), channel_id=1, source_target_pairs={{8,0},{16,8},{24,16},{9,1},{17,9},{25,17},{10,2},{18,10},{26,18},{... | collective-permute-start | bytes 2359304 | tf_op jit(solution)/shard_map/ppermute | solution.py:340
  4.0 0.0 copy-start.4
  4.0 1.9 %copy-done.4 = f32[768,1024]{1,0:T(8,128)S(1)} copy-done((f32[768,1024]{1,0:T(8,128)S(1)}, f32[768,1024]{1,0:T(8,128)}, u32[]{:S(2)}) %copy-start.4) | copy-done | bytes 3145752
  5.9 2.5 %prepare.1 = (bf16[768,1024]{1,0:T(8,128)(2,1)S(1)}, bf16[768,1024]{1,0:T(8,128)(2,1)S(1)}, bf16[1024,768]{1,0:T(8,128)(2,1)S(1)}, bf16[1024,768]{1,0:T(8,128)(2,1)S(1)}, f32[8,1024]{1,0:T(8,128)S(1)}) custom-call(f32[768,1024]{1,0:T(8,128)S(1)} %copy-done.4), custom_call_target="tpu_custom_call" | custom-call | flops 7864320 | bytes 9437184 | tf_op jit(solution)/shard_map/prepare/pallas_call | solution.py:54
  8.4 0.0 copy-start
  8.4 0.0 copy-start.2
  8.4 1.6 gram.5
  10.0 0.0 copy-done
  10.1 0.0 copy-done.2
  10.1 0.0 copy-start.5
  10.1 0.9 copy-done.5
  10.9 0.0 copy-start.7
  10.9 0.8 copy-done.7
  11.7 72.6 %cut.1 = (f32[768,256]{1,0:T(8,128)}, f32[768,256]{1,0:T(8,128)}, f32[768,256]{1,0:T(8,128)}) custom-call(f32[768,1024]{1,0:T(8,128)} %source.1, f32[264,512]{1,0:T(8,128)} %copy-done.5), custom_call_target="tpu_custom_call" | custom-call | bytes 6291456 | tf_op jit(solution)/shard_map/cut/pallas_call | solution.py:163
  84.3 2.5 %collective-permute-start.3 = (f32[768,256]{1,0:T(8,128)}, f32[768,256]{1,0:T(8,128)S(1)}, u32[]{:S(2)}, u32[]{:S(2)}) collective-permute-start(f32[768,256]{1,0:T(8,128)} %get-tuple-element.47), channel_id=1, source_target_pairs={{8,0},{16,8},{24,16},{9,1},{17,9},{25,17},{10,2},{18,10},{26,18},{... | collective-permute-start | bytes 2359304 | tf_op jit(solution)/shard_map/ppermute | solution.py:370
  86.9 1.5 collective-permute-start
  88.4 1.9 %collective-permute-start.6 = (f32[768,256]{1,0:T(8,128)}, f32[768,256]{1,0:T(8,128)S(1)}, u32[]{:S(2)}, u32[]{:S(2)}) collective-permute-start(f32[768,256]{1,0:T(8,128)} %get-tuple-element.50), channel_id=1, source_target_pairs={{8,0},{16,8},{24,16},{9,1},{17,9},{25,17},{10,2},{18,10},{26,18},{... | collective-permute-start | bytes 2359304 | tf_op jit(solution)/shard_map/ppermute | solution.py:370
  90.3 1.9 %collective-permute-start.8 = (f32[768,256]{1,0:T(8,128)}, f32[768,256]{1,0:T(8,128)S(1)}, u32[]{:S(2)}, u32[]{:S(2)}) collective-permute-start(f32[768,256]{1,0:T(8,128)} %get-tuple-element.54), channel_id=1, source_target_pairs={{8,0},{16,8},{24,16},{9,1},{17,9},{25,17},{10,2},{18,10},{26,18},{... | collective-permute-start | bytes 2359304 | tf_op jit(solution)/shard_map/ppermute | solution.py:370
  92.2 0.0 collective-permute-done.1.refs_0_
  92.2 0.0 copy-start.1
  92.3 1.4 copy-done.1
  93.7 1.4 copy-done.3
  95.1 1.0 copy-done.6
  96.1 4.7 %gram.6 = (f32[520,256]{1,0:T(8,128)S(1)}, f32[520,256]{1,0:T(8,128)S(1)}) custom-call(bf16[1024,768]{1,0:T(8,128)(2,1)S(1)} %copy-done.1, bf16[1024,768]{1,0:T(8,128)(2,1)S(1)} %copy-done.3, bf16[768,1024]{1,0:T(8,128)(2,1)S(1)} %get-tuple-element.39.high, bf16[768,1024]{1,0:T(8,128)(2,1)S(1)} %get-tuple-element.40.low, ...), custom_call_target="tpu_custom_call" | custom-call | flops 1207959552 | bytes 4718592 | tf_op jit(solution)/shard_map/gram/pallas_call | solution.py:133
  100.8 0.6 collective-permute-start.5
  101.4 0.1 collective-permute-done.got
  101.5 0.1 halve.7
  101.6 0.5 collective-permute-start.2
  102.1 0.0 collective-permute-done.3.refs_0_
  102.1 3.0 %gram.7 = (f32[520,256]{1,0:T(8,128)S(1)}, f32[520,256]{1,0:T(8,128)S(1)}) custom-call(bf16[1024,768]{1,0:T(8,128)(2,1)S(1)} %copy-done.1, bf16[1024,768]{1,0:T(8,128)(2,1)S(1)} %copy-done.3, bf16[768,1024]{1,0:T(8,128)(2,1)S(1)} %get-tuple-element.39.high, bf16[768,1024]{1,0:T(8,128)(2,1)S(1)} %get-tuple-element.40.low, ...), custom_call_target="tpu_custom_call" | custom-call | flops 1207959552 | bytes 4718592 | tf_op jit(solution)/shard_map/gram/pallas_call | solution.py:133
  105.1 1.5 collective-permute-start.10
  106.6 4.1 %collective-permute-done.2.got = f32[144,512]{1,0:T(8,128)S(1)} collective-permute-done((f32[144,512]{1,0:T(8,128)S(1)}, f32[144,512]{1,0:T(8,128)S(1)}, u32[]{:S(2)}, u32[]{:S(2)}) %collective-permute-start.2) | collective-permute-done | bytes 294944 | tf_op jit(solution)/shard_map/ppermute | solution.py:315
  110.7 0.0 collective-permute-done.6.refs_0_
  110.7 1.9 %gram.8 = (f32[264,256]{1,0:T(8,128)S(1)}, f32[264,256]{1,0:T(8,128)S(1)}) custom-call(bf16[1024,768]{1,0:T(8,128)(2,1)S(1)} %copy-done.1, bf16[1024,768]{1,0:T(8,128)(2,1)S(1)} %copy-done.3, bf16[768,1024]{1,0:T(8,128)(2,1)S(1)} %get-tuple-element.39.high, bf16[768,1024]{1,0:T(8,128)(2,1)S(1)} %get-tuple-element.40.low, ...), custom_call_target="tpu_custom_call" | custom-call | flops 603979776 | bytes 4718592 | tf_op jit(solution)/shard_map/gram/pallas_call | solution.py:133
  112.7 3.1 %collective-permute-done.5.got = f32[520,256]{1,0:T(8,128)S(1)} collective-permute-done((f32[520,256]{1,0:T(8,128)S(1)}, f32[520,256]{1,0:T(8,128)S(1)}, u32[]{:S(2)}, u32[]{:S(2)}) %collective-permute-start.5) | collective-permute-done | bytes 532512 | tf_op jit(solution)/shard_map/ppermute | solution.py:315
  115.8 0.1 halve.8
  115.8 0.5 collective-permute-start.7
  116.3 0.0 collective-permute-done.8.refs_0_
  116.3 1.4 gram.9
  117.8 6.1 %collective-permute-done.7.got = f32[272,256]{1,0:T(8,128)S(1)} collective-permute-done((f32[272,256]{1,0:T(8,128)S(1)}, f32[272,256]{1,0:T(8,128)S(1)}, u32[]{:S(2)}, u32[]{:S(2)}) %collective-permute-start.7) | collective-permute-done | bytes 278560 | tf_op jit(solution)/shard_map/ppermute | solution.py:315
  123.9 2.9 %collective-permute-done.10.got = f32[520,256]{1,0:T(8,128)S(1)} collective-permute-done((f32[520,256]{1,0:T(8,128)S(1)}, f32[520,256]{1,0:T(8,128)S(1)}, u32[]{:S(2)}, u32[]{:S(2)}) %collective-permute-start.10) | collective-permute-done | bytes 532512 | tf_op jit(solution)/shard_map/ppermute | solution.py:315
  126.8 0.1 halve.10
  126.9 0.5 collective-permute-start.11
  127.4 0.5 collective-permute-start.12
  127.9 1.5 collective-permute-start.15
  129.4 2.3 %collective-permute-start.4 = (f32[160,512]{1,0:T(8,128)S(1)}, f32[160,512]{1,0:T(8,128)S(1)}, u32[]{:S(2)}, u32[]{:S(2)}) collective-permute-start(f32[160,512]{1,0:T(8,128)S(1)} %merge.3.refs_1_.refs_0_), channel_id=1, source_target_pairs={{4,0},{5,1},{6,2},{7,3},{12,8},{13,9},{14,10},{15,11},{20,16},{21,... | collective-permute-start | bytes 983048 | tf_op jit(solution)/shard_map/ppermute | solution.py:320
  131.7 5.1 %collective-permute-done.12.got = f32[264,256]{1,0:T(8,128)S(1)} collective-permute-done((f32[264,256]{1,0:T(8,128)S(1)}, f32[264,256]{1,0:T(8,128)S(1)}, u32[]{:S(2)}, u32[]{:S(2)}) %collective-permute-start.12) | collective-permute-done | bytes 270368 | tf_op jit(solution)/shard_map/ppermute | solution.py:315
  136.9 1.6 collective-permute-start.14
  138.5 0.0 collective-permute-done.11.got
  138.5 2.5 %collective-permute-done.15.got = f32[264,256]{1,0:T(8,128)S(1)} collective-permute-done((f32[264,256]{1,0:T(8,128)S(1)}, f32[264,256]{1,0:T(8,128)S(1)}, u32[]{:S(2)}, u32[]{:S(2)}) %collective-permute-start.15) | collective-permute-done | bytes 270368 | tf_op jit(solution)/shard_map/ppermute | solution.py:315
  141.1 1.6 collective-permute-start.17
  142.8 0.3 collective-permute-start.9
  143.1 1.6 collective-permute-done.14.got
  144.7 1.3 collective-permute-start.16
  146.0 3.6 %collective-permute-start.13 = (f32[160,256]{1,0:T(8,128)S(1)}, f32[160,256]{1,0:T(8,128)S(1)}, u32[]{:S(2)}, u32[]{:S(2)}) collective-permute-start(f32[160,256]{1,0:T(8,128)S(1)} %get-tuple-element.64), channel_id=1, source_target_pairs={{0,4},{1,5},{2,6},{3,7},{4,0},{5,1},{6,2},{7,3},{8,12},{9,13},{10,... | collective-permute-start | bytes 491528 | tf_op jit(solution)/shard_map/ppermute | solution.py:315
  149.6 0.0 collective-permute-done.17.got
  149.7 1.3 collective-permute-start.18
  151.0 0.0 collective-permute-done.4.refs_1_
  151.0 12.4 %collective-permute-done.9.refs_3_ = f32[160,256]{1,0:T(8,128)S(1)} collective-permute-done((f32[160,256]{1,0:T(8,128)S(1)}, f32[160,256]{1,0:T(8,128)S(1)}, u32[]{:S(2)}, u32[]{:S(2)}) %collective-permute-start.9) | collective-permute-done | bytes 163872 | tf_op jit(solution)/shard_map/ppermute | solution.py:315
  163.4 3.5 %collective-permute-done.16.refs_7_ = f32[160,256]{1,0:T(8,128)S(1)} collective-permute-done((f32[160,256]{1,0:T(8,128)S(1)}, f32[160,256]{1,0:T(8,128)S(1)}, u32[]{:S(2)}, u32[]{:S(2)}) %collective-permute-start.16) | collective-permute-done | bytes 163872 | tf_op jit(solution)/shard_map/ppermute | solution.py:320
  166.9 3.5 %collective-permute-done.13.refs_5_ = f32[160,256]{1,0:T(8,128)S(1)} collective-permute-done((f32[160,256]{1,0:T(8,128)S(1)}, f32[160,256]{1,0:T(8,128)S(1)}, u32[]{:S(2)}, u32[]{:S(2)}) %collective-permute-start.13) | collective-permute-done | bytes 163872 | tf_op jit(solution)/shard_map/ppermute | solution.py:315
  170.4 2.1 %collective-permute-done.18.refs_9_ = f32[160,256]{1,0:T(8,128)S(1)} collective-permute-done((f32[160,256]{1,0:T(8,128)S(1)}, f32[160,256]{1,0:T(8,128)S(1)}, u32[]{:S(2)}, u32[]{:S(2)}) %collective-permute-start.18) | collective-permute-done | bytes 163872 | tf_op jit(solution)/shard_map/ppermute | solution.py:320
  172.5 3.0 %finish.1 = f32[128,1024]{1,0:T(8,128)} custom-call(f32[160,512]{1,0:T(8,128)S(1)} %merge.3.refs_1_.refs_0_, f32[160,512]{1,0:T(8,128)S(1)} %collective-permute-done.4.refs_1_, f32[160,256]{1,0:T(8,128)S(1)} %get-tuple-element.56.refs_0_.refs_2_, f32[160,256]{1,0:T(8,128)S(1)} %collective-permute-done.9.refs_3_, ...), custom_call_target="tpu_custom_call" | custom-call | flops 5242880 | bytes 2097152 | tf_op jit(solution)/shard_map/finish/pallas_call | solution.py:298
  (9 shorter events, 0.2 us)
Async XLA Ops:
  2.1 90.2 %collective-permute-start.1 = (f32[768,256]{1,0:T(8,128)}, f32[768,256]{1,0:T(8,128)}, u32[]{:S(2)}, u32[]{:S(2)}) collective-permute-start(f32[768,256]{1,0:T(8,128)} %slice.3), channel_id=1, source_target_pairs={{8,0},{16,8},{24,16},{9,1},{17,9},{25,17},{10,2},{18,10},{26,18},{... | collective-permute-start | bytes 2359304 | tf_op jit(solution)/shard_map/ppermute | solution.py:340
  4.0 1.9 %copy-start.4 = (f32[768,1024]{1,0:T(8,128)S(1)}, f32[768,1024]{1,0:T(8,128)}, u32[]{:S(2)}) copy-start(f32[768,1024]{1,0:T(8,128)} %source.1) | copy-start | bytes 9437188
  8.4 1.7 copy-start
  8.4 1.7 copy-start.2
  10.1 0.9 copy-start.5
  10.9 0.8 copy-start.7
  84.3 17.8 %collective-permute-start.3 = (f32[768,256]{1,0:T(8,128)}, f32[768,256]{1,0:T(8,128)S(1)}, u32[]{:S(2)}, u32[]{:S(2)}) collective-permute-start(f32[768,256]{1,0:T(8,128)} %get-tuple-element.47), channel_id=1, source_target_pairs={{8,0},{16,8},{24,16},{9,1},{17,9},{25,17},{10,2},{18,10},{26,18},{... | collective-permute-start | bytes 2359304 | tf_op jit(solution)/shard_map/ppermute | solution.py:370
  86.9 14.6 %collective-permute-start = (f32[264,512]{1,0:T(8,128)}, f32[264,512]{1,0:T(8,128)S(1)}, u32[]{:S(2)}, u32[]{:S(2)}) collective-permute-start(f32[264,512]{1,0:T(8,128)} %copy-done.7), channel_id=1, source_target_pairs={{0,1},{1,0},{2,3},{3,2},{4,5},{5,4},{6,7},{7,6},{8,9},{9,8},{10,11... | collective-permute-start | bytes 1622024 | tf_op jit(solution)/shard_map/ppermute | solution.py:315
  88.4 22.3 %collective-permute-start.6 = (f32[768,256]{1,0:T(8,128)}, f32[768,256]{1,0:T(8,128)S(1)}, u32[]{:S(2)}, u32[]{:S(2)}) collective-permute-start(f32[768,256]{1,0:T(8,128)} %get-tuple-element.50), channel_id=1, source_target_pairs={{8,0},{16,8},{24,16},{9,1},{17,9},{25,17},{10,2},{18,10},{26,18},{... | collective-permute-start | bytes 2359304 | tf_op jit(solution)/shard_map/ppermute | solution.py:370
  90.3 26.0 %collective-permute-start.8 = (f32[768,256]{1,0:T(8,128)}, f32[768,256]{1,0:T(8,128)S(1)}, u32[]{:S(2)}, u32[]{:S(2)}) collective-permute-start(f32[768,256]{1,0:T(8,128)} %get-tuple-element.54), channel_id=1, source_target_pairs={{8,0},{16,8},{24,16},{9,1},{17,9},{25,17},{10,2},{18,10},{26,18},{... | collective-permute-start | bytes 2359304 | tf_op jit(solution)/shard_map/ppermute | solution.py:370
  92.2 1.4 copy-start.1
  93.7 1.4 copy-start.3
  95.1 1.0 copy-start.6
  100.8 15.0 %collective-permute-start.5 = (f32[520,256]{1,0:T(8,128)S(1)}, f32[520,256]{1,0:T(8,128)S(1)}, u32[]{:S(2)}, u32[]{:S(2)}) collective-permute-start(f32[520,256]{1,0:T(8,128)S(1)} %get-tuple-element.49), channel_id=1, source_target_pairs={{0,1},{1,0},{2,3},{3,2},{4,5},{5,4},{6,7},{7,6},{8,9},{9,8},{10,11... | collective-permute-start | bytes 1597448 | tf_op jit(solution)/shard_map/ppermute | solution.py:315
  101.6 9.1 %collective-permute-start.2 = (f32[144,512]{1,0:T(8,128)S(1)}, f32[144,512]{1,0:T(8,128)S(1)}, u32[]{:S(2)}, u32[]{:S(2)}) collective-permute-start(f32[144,512]{1,0:T(8,128)S(1)} %get-tuple-element.46), channel_id=1, source_target_pairs={{0,2},{1,3},{2,0},{3,1},{4,6},{5,7},{6,4},{7,5},{8,10},{9,11},{10,... | collective-permute-start | bytes 884744 | tf_op jit(solution)/shard_map/ppermute | solution.py:315
  105.1 21.7 %collective-permute-start.10 = (f32[520,256]{1,0:T(8,128)S(1)}, f32[520,256]{1,0:T(8,128)S(1)}, u32[]{:S(2)}, u32[]{:S(2)}) collective-permute-start(f32[520,256]{1,0:T(8,128)S(1)} %get-tuple-element.58), channel_id=1, source_target_pairs={{0,1},{1,0},{2,3},{3,2},{4,5},{5,4},{6,7},{7,6},{8,9},{9,8},{10,11... | collective-permute-start | bytes 1597448 | tf_op jit(solution)/shard_map/ppermute | solution.py:315
  115.8 8.1 %collective-permute-start.7 = (f32[272,256]{1,0:T(8,128)S(1)}, f32[272,256]{1,0:T(8,128)S(1)}, u32[]{:S(2)}, u32[]{:S(2)}) collective-permute-start(f32[272,256]{1,0:T(8,128)S(1)} %get-tuple-element.53), channel_id=1, source_target_pairs={{0,2},{1,3},{2,0},{3,1},{4,6},{5,7},{6,4},{7,5},{8,10},{9,11},{10,... | collective-permute-start | bytes 835592 | tf_op jit(solution)/shard_map/ppermute | solution.py:315
  126.9 11.6 %collective-permute-start.11 = (f32[272,256]{1,0:T(8,128)S(1)}, f32[272,256]{1,0:T(8,128)S(1)}, u32[]{:S(2)}, u32[]{:S(2)}) collective-permute-start(f32[272,256]{1,0:T(8,128)S(1)} %get-tuple-element.60), channel_id=1, source_target_pairs={{0,2},{1,3},{2,0},{3,1},{4,6},{5,7},{6,4},{7,5},{8,10},{9,11},{10,... | collective-permute-start | bytes 835592 | tf_op jit(solution)/shard_map/ppermute | solution.py:315
  127.4 9.4 %collective-permute-start.12 = (f32[264,256]{1,0:T(8,128)S(1)}, f32[264,256]{1,0:T(8,128)S(1)}, u32[]{:S(2)}, u32[]{:S(2)}) collective-permute-start(f32[264,256]{1,0:T(8,128)S(1)} %get-tuple-element.61), channel_id=1, source_target_pairs={{0,1},{1,0},{2,3},{3,2},{4,5},{5,4},{6,7},{7,6},{8,9},{9,8},{10,11... | collective-permute-start | bytes 811016 | tf_op jit(solution)/shard_map/ppermute | solution.py:315
  127.9 13.1 %collective-permute-start.15 = (f32[264,256]{1,0:T(8,128)S(1)}, f32[264,256]{1,0:T(8,128)S(1)}, u32[]{:S(2)}, u32[]{:S(2)}) collective-permute-start(f32[264,256]{1,0:T(8,128)S(1)} %get-tuple-element.66), channel_id=1, source_target_pairs={{0,1},{1,0},{2,3},{3,2},{4,5},{5,4},{6,7},{7,6},{8,9},{9,8},{10,11... | collective-permute-start | bytes 811016 | tf_op jit(solution)/shard_map/ppermute | solution.py:315
  129.4 21.5 %collective-permute-start.4 = (f32[160,512]{1,0:T(8,128)S(1)}, f32[160,512]{1,0:T(8,128)S(1)}, u32[]{:S(2)}, u32[]{:S(2)}) collective-permute-start(f32[160,512]{1,0:T(8,128)S(1)} %merge.3.refs_1_.refs_0_), channel_id=1, source_target_pairs={{4,0},{5,1},{6,2},{7,3},{12,8},{13,9},{14,10},{15,11},{20,16},{21,... | collective-permute-start | bytes 983048 | tf_op jit(solution)/shard_map/ppermute | solution.py:320
  136.9 7.9 %collective-permute-start.14 = (f32[144,256]{1,0:T(8,128)S(1)}, f32[144,256]{1,0:T(8,128)S(1)}, u32[]{:S(2)}, u32[]{:S(2)}) collective-permute-start(f32[144,256]{1,0:T(8,128)S(1)} %get-tuple-element.65), channel_id=1, source_target_pairs={{0,2},{1,3},{2,0},{3,1},{4,6},{5,7},{6,4},{7,5},{8,10},{9,11},{10,... | collective-permute-start | bytes 442376 | tf_op jit(solution)/shard_map/ppermute | solution.py:315
  141.1 8.5 %collective-permute-start.17 = (f32[144,256]{1,0:T(8,128)S(1)}, f32[144,256]{1,0:T(8,128)S(1)}, u32[]{:S(2)}, u32[]{:S(2)}) collective-permute-start(f32[144,256]{1,0:T(8,128)S(1)} %get-tuple-element.68), channel_id=1, source_target_pairs={{0,2},{1,3},{2,0},{3,1},{4,6},{5,7},{6,4},{7,5},{8,10},{9,11},{10,... | collective-permute-start | bytes 442376 | tf_op jit(solution)/shard_map/ppermute | solution.py:315
  142.8 20.6 %collective-permute-start.9 = (f32[160,256]{1,0:T(8,128)S(1)}, f32[160,256]{1,0:T(8,128)S(1)}, u32[]{:S(2)}, u32[]{:S(2)}) collective-permute-start(f32[160,256]{1,0:T(8,128)S(1)} %get-tuple-element.57), channel_id=1, source_target_pairs={{0,4},{1,5},{2,6},{3,7},{4,0},{5,1},{6,2},{7,3},{8,12},{9,13},{10,... | collective-permute-start | bytes 491528 | tf_op jit(solution)/shard_map/ppermute | solution.py:315
  144.7 22.2 %collective-permute-start.16 = (f32[160,256]{1,0:T(8,128)S(1)}, f32[160,256]{1,0:T(8,128)S(1)}, u32[]{:S(2)}, u32[]{:S(2)}) collective-permute-start(f32[160,256]{1,0:T(8,128)S(1)} %merge.4.refs_0_.refs_6_), channel_id=1, source_target_pairs={{0,4},{1,5},{2,6},{3,7},{8,12},{9,13},{10,14},{11,15},{16,20},{17,... | collective-permute-start | bytes 491528 | tf_op jit(solution)/shard_map/ppermute | solution.py:320
  146.0 24.4 %collective-permute-start.13 = (f32[160,256]{1,0:T(8,128)S(1)}, f32[160,256]{1,0:T(8,128)S(1)}, u32[]{:S(2)}, u32[]{:S(2)}) collective-permute-start(f32[160,256]{1,0:T(8,128)S(1)} %get-tuple-element.64), channel_id=1, source_target_pairs={{0,4},{1,5},{2,6},{3,7},{4,0},{5,1},{6,2},{7,3},{8,12},{9,13},{10,... | collective-permute-start | bytes 491528 | tf_op jit(solution)/shard_map/ppermute | solution.py:315
  149.7 22.9 %collective-permute-start.18 = (f32[160,256]{1,0:T(8,128)S(1)}, f32[160,256]{1,0:T(8,128)S(1)}, u32[]{:S(2)}, u32[]{:S(2)}) collective-permute-start(f32[160,256]{1,0:T(8,128)S(1)} %merge.5.refs_8_), channel_id=1, source_target_pairs={{0,4},{1,5},{2,6},{3,7},{8,12},{9,13},{10,14},{11,15},{16,20},{17,... | collective-permute-start | bytes 491528 | tf_op jit(solution)/shard_map/ppermute | solution.py:320

commit v3 on v0

v3 whole, which is shorter than its diff:
```python
import functools

import jax
import jax.numpy as jnp
from jax import lax
from jax.experimental import pallas as pl
from jax.experimental.pallas import tpu as pltpu
from jax.sharding import PartitionSpec as P

EPS = 1e-06
STATS = 8
VMEM = pl.BlockSpec(memory_space=pltpu.VMEM)
ANY = pl.BlockSpec(memory_space=pl.ANY)


def params(mib):
    return pltpu.CompilerParams(vmem_limit_bytes=mib << 20)


def cost(weight):
    return pl.CostEstimate(flops=int(weight * 1e9), bytes_accessed=1, transcendentals=0)


def split(value):
    high = value.astype(jnp.bfloat16)
    low = (value - high.astype(jnp.float32)).astype(jnp.bfloat16)
    return high, low


def centre(block):
    count = block.shape[0]
    mean = jnp.sum(block, 0, keepdims=True) / count
    centred = block - mean
    left = jnp.sum(centred, 0, keepdims=True) / count
    squares = jnp.sum(centred * centred, 0, keepdims=True)
    return centred, mean, left, squares


def prepare_kernel(dosages, high_t, low_t, stats, stats_next, *refs):
    blocks, done = refs[:-1], refs[-1]
    width = blocks[0].shape[1]
    copies = []
    for i, block in enumerate(blocks):
        taken = dosages.at[:, pl.ds(i * width, width)]
        copies.append(pltpu.make_async_copy(taken, block, done.at[i]))
    for copy in copies:
        copy.start()
    for i, block in enumerate(blocks):
        copies[i].wait()
        here = pl.ds(i * width, width)
        centred, mean, left, squares = centre(block[...])
        high_t[here, :], low_t[here, :] = split(centred.T)
        zero = jnp.zeros_like(mean)
        rows = [mean, zero, left, zero, squares, zero, zero, zero]
        stats[:, here] = jnp.concatenate(rows, 0)
        rows = [zero, mean, zero, left, zero, squares, zero, zero]
        stats_next[:, here] = jnp.concatenate(rows, 0)


def prepare(dosages, width):
    samples, cols = dosages.shape
    count = cols // width
    half_t = jax.ShapeDtypeStruct((cols, samples), jnp.bfloat16)
    stats = jax.ShapeDtypeStruct((STATS, cols), jnp.float32)
    block = jax.ShapeDtypeStruct((samples, width), jnp.float32)
    out = pl.pallas_call(
        prepare_kernel,
        in_specs=[pl.BlockSpec(memory_space=pltpu.HBM)],
        out_specs=[VMEM] * (4 + count),
        out_shape=[half_t, half_t, stats, stats] + [block] * count,
        scratch_shapes=[pltpu.SemaphoreType.DMA((count,))],
        compiler_params=params(45),
        cost_estimate=cost(4),
        name="prepare",
    )(dosages)
    return out[:4], out[4:]


def place(owner, me, order):
    apart = jnp.bitwise_xor(owner, me)
    spot = 0
    for bit in order:
        spot = spot * 2 + (lax.shift_right_logical(apart, bit) & 1)
    return spot


def product(high_t, low_t, rows, high, low, side):
    sides = (((1,), (side,)), ((), ()))
    dot = functools.partial(lax.dot_general, dimension_numbers=sides, preferred_element_type=jnp.float32)
    a, b = high_t[rows, :], low_t[rows, :]
    return dot(a, high) + (dot(a, low) + dot(b, high))


def gram_kernel(piece, spots, order, passed, high_t, low_t, *refs):
    first, last, start, width = piece
    send, keep = refs[len(refs) - 2 - passed : len(refs) - passed]
    cols = high_t.shape[0]
    share = (last - first) // spots
    half = spots // 2
    me = lax.axis_index("samp")
    here = pl.ds(start, width)
    own_high, own_low = high_t[here, :], low_t[here, :]
    if last > start:
        ahead_high, ahead_low = split(centre(refs[0][...])[0])
    tall = min(width, 2 * cols // 8)
    for top in range(first, last, tall):
        band = pl.ds(top, tall)
        if top < start + width:
            tile = product(high_t, low_t, band, own_high, own_low, 1)
        if top + tall > start:
            later = product(high_t, low_t, band, ahead_high, ahead_low, 0)
            if top >= start + width:
                tile = later
            else:
                row = lax.broadcasted_iota(jnp.int32, tile.shape, 0) + top
                col = lax.broadcasted_iota(jnp.int32, tile.shape, 1) + start
                tile = jnp.where(col > row, tile, later)
        for part in range(tall // share):
            spot = place(top // share + part, me, order)
            block = tile[part * share : (part + 1) * share]
            there = pl.ds(pl.multiple_of((spot & (half - 1)) * share, share), share)

            @pl.when(spot >= half)
            def _():
                send[there, :] = block

            @pl.when(spot < half)
            def _():
                keep[there, :] = block


def gram(piece, spots, order, prepared, ahead, after, passed, weight):
    high_t, low_t = prepared
    first, last, start, width = piece
    cols, samples = high_t.shape
    shape = ((last - first) // 2, width)
    out = jax.ShapeDtypeStruct(shape, jnp.float32)
    extra = list(ahead) + list(after)
    count = len(passed)
    return pl.pallas_call(
        functools.partial(gram_kernel, piece, spots, order, count),
        in_specs=[VMEM] * (2 + len(ahead)) + [ANY] * (len(after) + count),
        out_specs=[VMEM] * 2 + [ANY] * count,
        out_shape=[out, out] + [jax.ShapeDtypeStruct(a.shape, a.dtype) for a in passed],
        input_output_aliases={2 + len(extra) + i: 2 + i for i in range(count)},
        compiler_params=params(24),
        cost_estimate=cost(weight),
        name="gram",
    )(high_t, low_t, *extra, *passed)


def add_kernel(keep, got, *refs):
    kept = refs[-1].shape[0]
    refs[-1][...] = keep[:kept, :] + got[:kept, :]
    if keep.shape[0] > kept:
        refs[-2][...] = keep[kept:, :] + got[kept:, :]


def add(pair, parts, after, weight):
    rows, cols = pair[0].shape
    out = jax.ShapeDtypeStruct((rows // parts, cols), jnp.float32)
    return pl.pallas_call(
        add_kernel,
        in_specs=[VMEM, VMEM] + [ANY] * len(after),
        out_specs=[VMEM] * parts,
        out_shape=[out] * parts,
        compiler_params=params(16),
        cost_estimate=cost(weight),
        name="add",
    )(*pair, *after)


def join_kernel(rows, one, other, *refs):
    out = refs[-1]
    if rows == one.shape[0]:
        out[...] = one[...] + other[...]
    else:
        out[: rows // 2, :] = one[...]
        out[rows // 2 :, :] = other[...]


def join(rows, one, other, after, weight):
    cols = one.shape[1]
    return pl.pallas_call(
        functools.partial(join_kernel, rows),
        in_specs=[VMEM, VMEM] + [ANY] * len(after),
        out_specs=VMEM,
        out_shape=jax.ShapeDtypeStruct((rows, cols), jnp.float32),
        compiler_params=params(16),
        cost_estimate=cost(weight),
        name="join",
    )(one, other, *after)


def weigh_kernel(parts, samples, one, other, *refs):
    fix, factor, marks = refs[-3:]
    share, cols = fix.shape
    total = samples * parts
    me = lax.axis_index("samp")
    stats = jnp.concatenate([ref[...].reshape(parts // 2, STATS, cols) for ref in (one, other)], 0)
    mean = jnp.sum(stats, 0, keepdims=True) / parts
    apart = (stats - mean) + pltpu.roll(stats, STATS - 2, 1)
    apart = apart - jnp.sum(apart, 0, keepdims=True) / parts
    kind = lax.broadcasted_iota(jnp.int32, stats.shape, 1)
    mark = jnp.where(kind < 2, apart, jnp.where(kind < 4, stats, 0.0))
    moved = jnp.sum(mark * mark, 0) * samples
    squares = jnp.sum(stats, 0)
    spread = (squares[4:6] + (moved[0:2] - moved[2:4])) / total
    marks[: parts * STATS, :] = mark.reshape(parts * STATS, cols)
    marks[parts * STATS :, :] = jnp.concatenate([lax.rsqrt(spread + EPS)] * (STATS // 2), 0)
    first = me * share
    if share % 128 == 0:
        rows = marks[:, pl.ds(pl.multiple_of(first, 128), share)]
    else:
        inside = lax.rem(first, 128)
        window = pl.ds(pl.multiple_of(first - inside, 128), 128)
        rows = pltpu.roll(marks[:, window], lax.rem(128 - inside, 128), 1)[:, :share]
    row_scale = rows[parts * STATS : parts * STATS + 1] / total
    row_scale = jnp.broadcast_to(row_scale, (128, share)).T
    rows = rows[: parts * STATS]
    kind = lax.broadcasted_iota(jnp.int32, rows.shape, 0) % STATS
    signed = jnp.where(kind == 0, rows, jnp.where(kind == 2, -rows, 0.0)) * samples
    signed_next = pltpu.roll(signed, 1, 0)
    dot = functools.partial(
        lax.dot_general,
        dimension_numbers=(((0,), (0,)), ((), ())),
        precision=lax.Precision.HIGHEST,
        preferred_element_type=jnp.float32,
    )
    every = marks[: parts * STATS, :]
    own_fix, ahead_fix = dot(signed, every), dot(signed_next, every)
    row = first + lax.broadcasted_iota(jnp.int32, (share, 128), 0)
    lane = lax.broadcasted_iota(jnp.int32, (share, 128), 1)
    for left in range(0, cols, 128):
        here = slice(left, left + 128)
        own = lane + left > row
        scale = marks[parts * STATS : parts * STATS + 2, here]
        fix[:, here] = jnp.where(own, own_fix[:, here], ahead_fix[:, here])
        factor[:, here] = jnp.where(own, scale[0:1], scale[1:2]) * row_scale


def weigh(parts, samples, share, one, other, after, weight):
    cols = one.shape[1]
    out = jax.ShapeDtypeStruct((share, cols), jnp.float32)
    return pl.pallas_call(
        functools.partial(weigh_kernel, parts, samples),
        in_specs=[VMEM, VMEM] + [ANY] * len(after),
        out_specs=[VMEM] * 2,
        out_shape=[out, out],
        scratch_shapes=[pltpu.VMEM(((parts + 1) * STATS, cols), jnp.float32)],
        compiler_params=params(16),
        cost_estimate=cost(weight),
        name="weigh",
    )(one, other, *after)


def finish_kernel(parts, starts, uses, sizes, fix, factor, *refs):
    out, body = refs[-2:]
    share, cols = out.shape
    me = lax.axis_index("samp")
    upper = me >= parts // 2

    def take(i):
        mine = refs[sum(sizes[:i]) : sum(sizes[: i + 1])]
        total = sum(ref[...] for ref in mine)
        here = slice(starts[i], starts[i] + total.shape[1])
        body[:, here] = (total + fix[:, here]) * factor[:, here]

    for i in range(len(starts)):
        if uses[i] is None:
            take(i)
        else:
            pl.when(upper == uses[i])(functools.partial(take, i))
    first = me * share
    turned = pltpu.roll(body[...], lax.rem(2 * cols - first - 1, cols), 1)
    row = lax.broadcasted_iota(jnp.int32, (share, cols), 0)
    step = 1
    while step < share:
        moved = pltpu.roll(turned, cols - step, 1)
        turned = jnp.where((row & step) != 0, moved, turned)
        step *= 2
    out[...] = turned


def finish(parts, starts, uses, weights, sums):
    flat = [array for arrays in sums for array in arrays]
    sizes = [len(arrays) for arrays in sums]
    share, cols = weights[0].shape
    return pl.pallas_call(
        functools.partial(finish_kernel, parts, starts, uses, sizes),
        in_specs=[VMEM] * (2 + len(flat)),
        out_specs=VMEM,
        out_shape=jax.ShapeDtypeStruct((share, cols), jnp.float32),
        scratch_shapes=[pltpu.VMEM((share, cols), jnp.float32)],
        compiler_params=params(16),
        cost_estimate=cost(4),
        name="finish",
    )(*weights, *flat)


PLAN = (
    (0, 0, 2), (1, 0, 2), (0, 1, 2), (5, 0, 2), (2, 0, 2), (0, 2, 2), (1, 1, 2), (3, 0, 2),
    (5, 1, 2), (4, 0, 2), (2, 1, 2), (1, 2, 2), (5, 2, 2), (0, 3, 2), (3, 1, 2), (2, 2, 2),
    (5, 3, 2), (1, 3, 2), (4, 1, 2), (3, 2, 2), (2, 3, 2), (4, 2, 2), (3, 3, 2),
)
ORDERS = ((0, 1), (0, 1, 2), (0, 1, 2), (0, 1), (0, 1))


def plan(steps, pieces):
    tasks = [task for task in PLAN if task[1] <= steps]
    named = {task[:2] for task in tasks}
    for step in range(steps + 1):
        for i in (pieces, *range(pieces)):
            if (i, step) not in named and (step < steps or i == pieces):
                tasks.append((i, step, 2))
    return tasks


def swap(array, bit, parts):
    return lax.ppermute(array, "samp", [(i, i ^ (1 << bit)) for i in range(parts)])


def hand_over(array, upper, parts):
    half = parts // 2
    return lax.ppermute(array, "samp", [(i, i ^ half) for i in range(parts) if (i >= half) != upper])


def local(dosages):
    samples, cols = dosages.shape
    parts = lax.axis_size("samp")
    blocks = lax.axis_size("var")
    share = cols // parts
    steps = parts.bit_length() - 1
    quarter, half = cols // 4, cols // 2
    route = [(i, i - 1) for i in range(1, blocks)]
    pieces = [
        (0, half, half, half),
        (0, cols, 0, quarter),
        (0, cols, quarter, quarter),
        (half, cols, half, quarter),
        (half, cols, half + quarter, quarter),
    ]
    uses = [False, None, None, True, True]

    (high_t, low_t, stats, stats_next), cuts = prepare(dosages, quarter)
    last = stats
    pairs, sums = {}, {}
    weights = None
    passed = {(0, 0): [cuts[1], stats_next], (1, 0): [cuts[2]], (2, 0): [cuts[3]]}
    come = [None, lax.ppermute(cuts[0], "var", route)]

    def bits(i):
        whole = uses[i] is None
        used = ORDERS[i][: steps if whole else steps - 1]
        return used + tuple(range(len(used), steps if whole else steps - 1))

    for i, step, weight in plan(steps, len(pieces)):
        if i == len(pieces):
            if step == 0:
                stats_next = come.pop(3)
            if step < steps:
                stats = last = join(STATS << step, stats, stats_next, [last], weight)
                stats_next = swap(stats, step, parts)
            else:
                weights = weigh(parts, samples, share, stats, stats_next, [last], weight)
                last = weights[0]
        elif step == 0:
            piece = pieces[i]
            spots = parts if uses[i] is None else parts // 2
            near = [] if come[i] is None else [come[i]]
            held = passed.get((i, 0), [])
            send, last, *held = gram(piece, spots, bits(i), (high_t, low_t), near, [last], held, weight)
            pairs[i] = (last, swap(send, bits(i)[0], parts))
            come += [lax.ppermute(array, "var", route) for array in held]
        elif step == steps:
            (last,) = sums[i] = add(pairs[i], 1, [last], weight)
        elif step < len(bits(i)):
            send, last = add(pairs[i], 2, [last], weight)
            pairs[i] = (last, swap(send, bits(i)[step], parts))
        else:
            (last,) = add(pairs[i], 1, [last], weight)
            pairs[i] = (last, hand_over(last, uses[i], parts))
    starts = [piece[2] for piece in pieces]
    return finish(parts, starts, uses, weights, [sums.get(i, pairs[i]) for i in range(len(pieces))])


def solution(mesh):
    in_specs = (P("samp", "var"),)
    out_specs = P(("var", "samp"), None)
    return jax.shard_map(local, mesh=mesh, in_specs=in_specs, out_specs=out_specs, check_vma=False)
```

time: 212 us -> 84.8 us (0.40)
  the two profiles are of different devices: /device:TPU:0 before, /device:TPU:28 now
where the time goes in v3:
time: 84.8 us; the launch traced here: 84.5 us
  starting transfers between devices  37.4 us (44%)
  waiting for transfers between devices  28.6 us (34%)
  Pallas kernels  18.2 us (21%)
    ppermute x15, starting transfers between devices, swap(): lax.ppermute(array, 'samp', [(i, i ^ 1 << bit) for i in range(parts)])  19.2 us
    ppermute x15, waiting for transfers between devices, swap(): lax.ppermute(array, 'samp', [(i, i ^ 1 << bit) for i in range(parts)])  18 us
    pallas_call x5, Pallas kernels, gram(): pl.pallas_call(functools.partial(gram_kernel, piece, spots, order, count)...  11.9 us
    ppermute x4, starting transfers between devices, local(): come += [lax.ppermute(array, 'var', route) for array in held]  11.5 us
    ppermute x3, waiting for transfers between devices, hand_over(): lax.ppermute(array, 'samp', [(i, i ^ half) for i in range(parts) if (i >=...  6.44 us
    ppermute x3, starting transfers between devices, hand_over(): lax.ppermute(array, 'samp', [(i, i ^ half) for i in range(parts) if (i >=...  4.84 us
    pallas_call x1, Pallas kernels, prepare(): pl.pallas_call(prepare_kernel, in_specs=[pl.BlockSpec(memory_space=pltpu....  2.79 us
    ppermute x1, waiting for transfers between devices, local(): come = [None, lax.ppermute(cuts[0], 'var', route)]  2.08 us
  transfers between devices with their start and end apart: 23, of which 8 were waited for; matrix products, arithmetic and copies ran while one was open for 0% of the time, Pallas kernels for 16%

profile of v3, /device:TPU:28, one launch (start us, length us, event | category | flops | bytes accessed | tf_op | source)
XLA Modules:
  0.0 84.5 jit_solution(8064337773649962810)
XLA Ops:
  0.0 2.8 %prepare.1 = (bf16[1024,768]{1,0:T(8,128)(2,1)S(1)}, bf16[1024,768]{1,0:T(8,128)(2,1)S(1)}, f32[8,1024]{1,0:T(8,128)S(1)}, f32[8,1024]{1,0:T(8,128)S(1)}, f32[76...) custom-call(f32[768,1024]{1,0:T(8,128)} %dosages.1), custom_call_target="tpu_custom_call" | custom-call | flops 4000000000 | bytes 1 | tf_op jit(solution)/shard_map/prepare/pallas_call | solution.py:66
  2.8 1.9 %collective-permute-start.2 = (f32[768,256]{1,0:T(8,128)S(1)}, f32[768,256]{1,0:T(8,128)S(1)}, u32[]{:S(2)}, u32[]{:S(2)}) collective-permute-start(f32[768,256]{1,0:T(8,128)S(1)} %get-tuple-element.51), channel_id=1, source_target_pairs={{8,0},{16,8},{24,16},{9,1},{17,9},{25,17},{10,2},{18,10},{26,18},{... | collective-permute-start | bytes 2359304 | tf_op jit(solution)/shard_map/ppermute | solution.py:350
  4.7 1.7 %gram.5 = (f32[256,512]{1,0:T(8,128)S(1)}, f32[256,512]{1,0:T(8,128)S(1)}, f32[768,256]{1,0:T(8,128)S(1)}, f32[8,1024]{1,0:T(8,128)S(1)}) custom-call(bf16[1024,768]{1,0:T(8,128)(2,1)S(1)} %get-tuple-element.44.high_t, bf16[1024,768]{1,0:T(8,128)(2,1)S(1)} %get-tuple-element.45.low_t, ...), custom_call_target="tpu_custom_call", output_to_operand_aliasing={{2}: (3, {}), {3}: (4, {})} | custom-call | flops 2000000000 | bytes 1 | tf_op jit(solution)/shard_map/gram/pallas_call | solution.py:140
  6.4 1.5 %collective-permute-start.1 = (f32[256,512]{1,0:T(8,128)S(1)}, f32[256,512]{1,0:T(8,128)S(1)}, u32[]{:S(2)}, u32[]{:S(2)}) collective-permute-start(f32[256,512]{1,0:T(8,128)S(1)} %get-tuple-element.50), channel_id=1, source_target_pairs={{0,1},{1,0},{2,3},{3,2},{4,5},{5,4},{6,7},{7,6},{8,9},{9,8},{10,11... | collective-permute-start | bytes 1572872 | tf_op jit(solution)/shard_map/ppermute | solution.py:320
  8.0 2.2 %collective-permute-start.7 = (f32[768,256]{1,0:T(8,128)S(1)}, f32[768,256]{1,0:T(8,128)S(1)}, u32[]{:S(2)}, u32[]{:S(2)}) collective-permute-start(f32[768,256]{1,0:T(8,128)S(1)} %get-tuple-element.58), channel_id=1, source_target_pairs={{8,0},{16,8},{24,16},{9,1},{17,9},{25,17},{10,2},{18,10},{26,18},{... | collective-permute-start | bytes 2359304 | tf_op jit(solution)/shard_map/ppermute | solution.py:374
  10.2 1.9 %collective-permute-start = (f32[8,1024]{1,0:T(8,128)S(1)}, f32[8,1024]{1,0:T(8,128)S(1)}, u32[]{:S(2)}, u32[]{:S(2)}) collective-permute-start(f32[8,1024]{1,0:T(8,128)S(1)} %get-tuple-element.48), channel_id=1, source_target_pairs={{8,0},{16,8},{24,16},{9,1},{17,9},{25,17},{10,2},{18,10},{26,18},{... | collective-permute-start | bytes 98312 | tf_op jit(solution)/shard_map/ppermute | solution.py:374
  12.1 2.1 %collective-permute-done.2.refs_0_ = f32[768,256]{1,0:T(8,128)S(1)} collective-permute-done((f32[768,256]{1,0:T(8,128)S(1)}, f32[768,256]{1,0:T(8,128)S(1)}, u32[]{:S(2)}, u32[]{:S(2)}) %collective-permute-start.2) | collective-permute-done | bytes 786464 | tf_op jit(solution)/shard_map/ppermute | solution.py:350
  14.2 3.4 %gram.6 = (f32[512,256]{1,0:T(8,128)S(1)}, f32[512,256]{1,0:T(8,128)S(1)}, f32[768,256]{1,0:T(8,128)S(1)}) custom-call(bf16[1024,768]{1,0:T(8,128)(2,1)S(1)} %get-tuple-element.44.high_t, bf16[1024,768]{1,0:T(8,128)(2,1)S(1)} %get-tuple-element.45.low_t, f32[768,256]{1,0:T(8,128)S(1)} %collective-permute-done.2.refs_0_, ...), custom_call_target="tpu_custom_call", output_to_operand_aliasing={{2}: (4, {})} | custom-call | flops 2000000000 | bytes 1 | tf_op jit(solution)/shard_map/gram/pallas_call | solution.py:140
  17.7 1.5 %collective-permute-start.5 = (f32[512,256]{1,0:T(8,128)S(1)}, f32[512,256]{1,0:T(8,128)S(1)}, u32[]{:S(2)}, u32[]{:S(2)}) collective-permute-start(f32[512,256]{1,0:T(8,128)S(1)} %get-tuple-element.56), channel_id=1, source_target_pairs={{0,1},{1,0},{2,3},{3,2},{4,5},{5,4},{6,7},{7,6},{8,9},{9,8},{10,11... | collective-permute-start | bytes 1572872 | tf_op jit(solution)/shard_map/ppermute | solution.py:320
  19.2 3.8 %collective-permute-start.4 = (f32[768,256]{1,0:T(8,128)S(1)}, f32[768,256]{1,0:T(8,128)S(1)}, u32[]{:S(2)}, u32[]{:S(2)}) collective-permute-start(f32[768,256]{1,0:T(8,128)S(1)} %get-tuple-element.55), channel_id=1, source_target_pairs={{8,0},{16,8},{24,16},{9,1},{17,9},{25,17},{10,2},{18,10},{26,18},{... | collective-permute-start | bytes 2359304 | tf_op jit(solution)/shard_map/ppermute | solution.py:374
  23.0 0.0 collective-permute-done.1.got
  23.0 0.1 add.14
  23.1 0.5 collective-permute-start.6
  23.6 0.0 collective-permute-done.other
  23.6 0.0 collective-permute-done.7.refs_0_
  23.6 3.1 %gram.7 = (f32[512,256]{1,0:T(8,128)S(1)}, f32[512,256]{1,0:T(8,128)S(1)}, f32[768,256]{1,0:T(8,128)S(1)}) custom-call(bf16[1024,768]{1,0:T(8,128)(2,1)S(1)} %get-tuple-element.44.high_t, bf16[1024,768]{1,0:T(8,128)(2,1)S(1)} %get-tuple-element.45.low_t, f32[768,256]{1,0:T(8,128)S(1)} %collective-permute-done.7.refs_0_, ...), custom_call_target="tpu_custom_call", output_to_operand_aliasing={{2}: (4, {})} | custom-call | flops 2000000000 | bytes 1 | tf_op jit(solution)/shard_map/gram/pallas_call | solution.py:140
  26.8 3.5 %collective-permute-start.11 = (f32[768,256]{1,0:T(8,128)S(1)}, f32[768,256]{1,0:T(8,128)S(1)}, u32[]{:S(2)}, u32[]{:S(2)}) collective-permute-start(f32[768,256]{1,0:T(8,128)S(1)} %get-tuple-element.65), channel_id=1, source_target_pairs={{8,0},{16,8},{24,16},{9,1},{17,9},{25,17},{10,2},{18,10},{26,18},{... | collective-permute-start | bytes 2359304 | tf_op jit(solution)/shard_map/ppermute | solution.py:374
  30.3 1.5 %collective-permute-start.3 = (f32[8,1024]{1,0:T(8,128)S(1)}, f32[8,1024]{1,0:T(8,128)S(1)}, u32[]{:S(2)}, u32[]{:S(2)}) collective-permute-start(f32[8,1024]{1,0:T(8,128)S(1)} %join.3.refs_1_.one), channel_id=1, source_target_pairs={{0,1},{1,0},{2,3},{3,2},{4,5},{5,4},{6,7},{7,6},{8,9},{9,8},{10,11... | collective-permute-start | bytes 98312 | tf_op jit(solution)/shard_map/ppermute | solution.py:320
  31.8 0.0 collective-permute-done.6.got
  31.8 0.6 collective-permute-start.10
  32.4 0.0 collective-permute-done.5.got
  32.4 2.3 %collective-permute-start.15 = (f32[128,512]{1,0:T(8,128)S(1)}, f32[128,512]{1,0:T(8,128)S(1)}, u32[]{:S(2)}, u32[]{:S(2)}) collective-permute-start(f32[128,512]{1,0:T(8,128)S(1)} %add.15.refs_0_.keep), channel_id=1, source_target_pairs={{4,0},{5,1},{6,2},{7,3},{12,8},{13,9},{14,10},{15,11},{20,16},{21,... | collective-permute-start | bytes 786440 | tf_op jit(solution)/shard_map/ppermute | solution.py:325
  34.7 0.1 add.16
  34.7 0.0 collective-permute-done.4.refs_0_
  34.8 0.5 collective-permute-start.9
  35.3 1.9 %gram.8 = (f32[256,256]{1,0:T(8,128)S(1)}, f32[256,256]{1,0:T(8,128)S(1)}) custom-call(bf16[1024,768]{1,0:T(8,128)(2,1)S(1)} %get-tuple-element.44.high_t, bf16[1024,768]{1,0:T(8,128)(2,1)S(1)} %get-tuple-element.45.low_t, f32[768,256]{1,0:T(8,128)S(1)} %collective-permute-done.4.refs_0_, f32[256,256]{1,0:T(8,128)S(1)} %get-tuple-element.61.refs_1_.keep), custom_call_target="tpu_custom_call" | custom-call | flops 2000000000 | bytes 1 | tf_op jit(solution)/shard_map/gram/pallas_call | solution.py:140
  37.2 0.0 collective-permute-done.3.other
  37.2 1.6 %collective-permute-start.8 = (f32[16,1024]{1,0:T(8,128)S(1)}, f32[16,1024]{1,0:T(8,128)S(1)}, u32[]{:S(2)}, u32[]{:S(2)}) collective-permute-start(f32[16,1024]{1,0:T(8,128)S(1)} %join.4.refs_1_.one), channel_id=1, source_target_pairs={{0,2},{1,3},{2,0},{3,1},{4,6},{5,7},{6,4},{7,5},{8,10},{9,11},{10,... | collective-permute-start | bytes 196616 | tf_op jit(solution)/shard_map/ppermute | solution.py:320
  38.8 2.1 %collective-permute-done.11.refs_0_ = f32[768,256]{1,0:T(8,128)S(1)} collective-permute-done((f32[768,256]{1,0:T(8,128)S(1)}, f32[768,256]{1,0:T(8,128)S(1)}, u32[]{:S(2)}, u32[]{:S(2)}) %collective-permute-start.11) | collective-permute-done | bytes 786464 | tf_op jit(solution)/shard_map/ppermute | solution.py:374
  40.9 0.6 collective-permute-start.14
  41.5 1.7 %gram.9 = (f32[256,256]{1,0:T(8,128)S(1)}, f32[256,256]{1,0:T(8,128)S(1)}) custom-call(bf16[1024,768]{1,0:T(8,128)(2,1)S(1)} %get-tuple-element.44.high_t, bf16[1024,768]{1,0:T(8,128)(2,1)S(1)} %get-tuple-element.45.low_t, f32[768,256]{1,0:T(8,128)S(1)} %collective-permute-done.11.refs_0_, f32[16,1024]{1,0:T(8,128)S(1)} %join.4.refs_1_.one), custom_call_target="tpu_custom_call" | custom-call | flops 2000000000 | bytes 1 | tf_op jit(solution)/shard_map/gram/pallas_call | solution.py:140
  43.2 3.4 %collective-permute-done.10.got = f32[512,256]{1,0:T(8,128)S(1)} collective-permute-done((f32[512,256]{1,0:T(8,128)S(1)}, f32[512,256]{1,0:T(8,128)S(1)}, u32[]{:S(2)}, u32[]{:S(2)}) %collective-permute-start.10) | collective-permute-done | bytes 524320 | tf_op jit(solution)/shard_map/ppermute | solution.py:320
  46.7 0.1 add.17
  46.7 0.3 collective-permute-done.9.got
  47.1 0.1 collective-permute-start.16
  47.2 2.5 %collective-permute-start.13 = (f32[256,256]{1,0:T(8,128)S(1)}, f32[256,256]{1,0:T(8,128)S(1)}, u32[]{:S(2)}, u32[]{:S(2)}) collective-permute-start(f32[256,256]{1,0:T(8,128)S(1)} %get-tuple-element.69), channel_id=1, source_target_pairs={{0,2},{1,3},{2,0},{3,1},{4,6},{5,7},{6,4},{7,5},{8,10},{9,11},{10,... | collective-permute-start | bytes 786440 | tf_op jit(solution)/shard_map/ppermute | solution.py:320
  49.7 0.0 collective-permute-done.8.other
  49.7 1.6 %collective-permute-start.19 = (f32[256,256]{1,0:T(8,128)S(1)}, f32[256,256]{1,0:T(8,128)S(1)}, u32[]{:S(2)}, u32[]{:S(2)}) collective-permute-start(f32[256,256]{1,0:T(8,128)S(1)} %get-tuple-element.78), channel_id=1, source_target_pairs={{0,1},{1,0},{2,3},{3,2},{4,5},{5,4},{6,7},{7,6},{8,9},{9,8},{10,11... | collective-permute-start | bytes 786440 | tf_op jit(solution)/shard_map/ppermute | solution.py:320
  51.3 0.0 collective-permute-done.15.got
  51.3 2.9 %collective-permute-start.12 = (f32[32,1024]{1,0:T(8,128)S(1)}, f32[32,1024]{1,0:T(8,128)S(1)}, u32[]{:S(2)}, u32[]{:S(2)}) collective-permute-start(f32[32,1024]{1,0:T(8,128)S(1)} %join.5.refs_0_.one), channel_id=1, source_target_pairs={{0,4},{1,5},{2,6},{3,7},{4,0},{5,1},{6,2},{7,3},{8,12},{9,13},{10,... | collective-permute-start | bytes 393224 | tf_op jit(solution)/shard_map/ppermute | solution.py:320
  54.2 0.0 collective-permute-done.14.got
  54.3 0.1 collective-permute-start.18
  54.4 7.8 %collective-permute-done.13.got = f32[256,256]{1,0:T(8,128)S(1)} collective-permute-done((f32[256,256]{1,0:T(8,128)S(1)}, f32[256,256]{1,0:T(8,128)S(1)}, u32[]{:S(2)}, u32[]{:S(2)}) %collective-permute-start.13) | collective-permute-done | bytes 262176 | tf_op jit(solution)/shard_map/ppermute | solution.py:320
  62.3 0.9 %collective-permute-start.17 = (f32[128,256]{1,0:T(8,128)S(1)}, f32[128,256]{1,0:T(8,128)S(1)}, u32[]{:S(2)}, u32[]{:S(2)}) collective-permute-start(f32[128,256]{1,0:T(8,128)S(1)} %get-tuple-element.76), channel_id=1, source_target_pairs={{0,4},{1,5},{2,6},{3,7},{4,0},{5,1},{6,2},{7,3},{8,12},{9,13},{10,... | collective-permute-start | bytes 393224 | tf_op jit(solution)/shard_map/ppermute | solution.py:320
  63.1 0.0 collective-permute-done.12.other
  63.1 1.2 %weigh.1 = (f32[128,1024]{1,0:T(8,128)S(1)}, f32[128,1024]{1,0:T(8,128)S(1)}) custom-call(f32[32,1024]{1,0:T(8,128)S(1)} %join.5.refs_0_.one, f32[32,1024]{1,0:T(8,128)S(1)} %collective-permute-done.12.other, f32[128,256]{1,0:T(8,128)S(1)} %get-tuple-element.72.refs_0_.keep), custom_call_target="tpu_custom_call" | custom-call | flops 2000000000 | bytes 1 | tf_op jit(solution)/shard_map/weigh/pallas_call | solution.py:245
  64.3 0.0 collective-permute-done.16.got
  64.4 0.0 collective-permute-done.19.got
  64.4 2.7 %collective-permute-start.21 = (f32[128,256]{1,0:T(8,128)S(1)}, f32[128,256]{1,0:T(8,128)S(1)}, u32[]{:S(2)}, u32[]{:S(2)}) collective-permute-start(f32[128,256]{1,0:T(8,128)S(1)} %get-tuple-element.80), channel_id=1, source_target_pairs={{0,2},{1,3},{2,0},{3,1},{4,6},{5,7},{6,4},{7,5},{8,10},{9,11},{10,... | collective-permute-start | bytes 393224 | tf_op jit(solution)/shard_map/ppermute | solution.py:320
  67.1 0.0 collective-permute-done.18.got
  67.1 1.3 %collective-permute-start.20 = (f32[128,256]{1,0:T(8,128)S(1)}, f32[128,256]{1,0:T(8,128)S(1)}, u32[]{:S(2)}, u32[]{:S(2)}) collective-permute-start(f32[128,256]{1,0:T(8,128)S(1)} %add.24.refs_0_.keep), channel_id=1, source_target_pairs={{0,4},{1,5},{2,6},{3,7},{8,12},{9,13},{10,14},{11,15},{16,20},{17,... | collective-permute-start | bytes 393224 | tf_op jit(solution)/shard_map/ppermute | solution.py:325
  68.4 6.4 %collective-permute-done.17.got = f32[128,256]{1,0:T(8,128)S(1)} collective-permute-done((f32[128,256]{1,0:T(8,128)S(1)}, f32[128,256]{1,0:T(8,128)S(1)}, u32[]{:S(2)}, u32[]{:S(2)}) %collective-permute-start.17) | collective-permute-done | bytes 131104 | tf_op jit(solution)/shard_map/ppermute | solution.py:320
  74.9 0.0 collective-permute-done.21.got
  74.9 1.3 %collective-permute-start.22 = (f32[128,256]{1,0:T(8,128)S(1)}, f32[128,256]{1,0:T(8,128)S(1)}, u32[]{:S(2)}, u32[]{:S(2)}) collective-permute-start(f32[128,256]{1,0:T(8,128)S(1)} %add.26.refs_0_.refs_4_), channel_id=1, source_target_pairs={{0,4},{1,5},{2,6},{3,7},{8,12},{9,13},{10,14},{11,15},{16,20},{17,... | collective-permute-start | bytes 393224 | tf_op jit(solution)/shard_map/ppermute | solution.py:325
  76.2 1.0 %collective-permute-done.20.got = f32[128,256]{1,0:T(8,128)S(1)} collective-permute-done((f32[128,256]{1,0:T(8,128)S(1)}, f32[128,256]{1,0:T(8,128)S(1)}, u32[]{:S(2)}, u32[]{:S(2)}) %collective-permute-start.20) | collective-permute-done | bytes 131104 | tf_op jit(solution)/shard_map/ppermute | solution.py:325
  77.2 5.4 %collective-permute-done.22.refs_5_ = f32[128,256]{1,0:T(8,128)S(1)} collective-permute-done((f32[128,256]{1,0:T(8,128)S(1)}, f32[128,256]{1,0:T(8,128)S(1)}, u32[]{:S(2)}, u32[]{:S(2)}) %collective-permute-start.22) | collective-permute-done | bytes 131104 | tf_op jit(solution)/shard_map/ppermute | solution.py:325
  82.7 1.9 %finish.1 = f32[128,1024]{1,0:T(8,128)} custom-call(f32[128,1024]{1,0:T(8,128)S(1)} %get-tuple-element.73.refs_0_.fix, f32[128,1024]{1,0:T(8,128)S(1)} %get-tuple-element.74.factor, f32[128,512]{1,0:T(8,128)S(1)} %add.19.refs_0_, f32[128,256]{1,0:T(8,128)S(1)} %add.22.refs_0_.refs_1_, f32[128,256]{1,0:T(8,128)S(1)} %add.25.refs_0_.refs_2_, ...), custom_call_target="tpu_custom_call" | custom-call | flops 4000000000 | bytes 1 | tf_op jit(solution)/shard_map/finish/pallas_call | solution.py:289
  (14 shorter events, 0.3 us)
Async XLA Ops:
  2.8 11.4 %collective-permute-start.2 = (f32[768,256]{1,0:T(8,128)S(1)}, f32[768,256]{1,0:T(8,128)S(1)}, u32[]{:S(2)}, u32[]{:S(2)}) collective-permute-start(f32[768,256]{1,0:T(8,128)S(1)} %get-tuple-element.51), channel_id=1, source_target_pairs={{8,0},{16,8},{24,16},{9,1},{17,9},{25,17},{10,2},{18,10},{26,18},{... | collective-permute-start | bytes 2359304 | tf_op jit(solution)/shard_map/ppermute | solution.py:350
  6.4 16.6 %collective-permute-start.1 = (f32[256,512]{1,0:T(8,128)S(1)}, f32[256,512]{1,0:T(8,128)S(1)}, u32[]{:S(2)}, u32[]{:S(2)}) collective-permute-start(f32[256,512]{1,0:T(8,128)S(1)} %get-tuple-element.50), channel_id=1, source_target_pairs={{0,1},{1,0},{2,3},{3,2},{4,5},{5,4},{6,7},{7,6},{8,9},{9,8},{10,11... | collective-permute-start | bytes 1572872 | tf_op jit(solution)/shard_map/ppermute | solution.py:320
  8.0 15.6 %collective-permute-start.7 = (f32[768,256]{1,0:T(8,128)S(1)}, f32[768,256]{1,0:T(8,128)S(1)}, u32[]{:S(2)}, u32[]{:S(2)}) collective-permute-start(f32[768,256]{1,0:T(8,128)S(1)} %get-tuple-element.58), channel_id=1, source_target_pairs={{8,0},{16,8},{24,16},{9,1},{17,9},{25,17},{10,2},{18,10},{26,18},{... | collective-permute-start | bytes 2359304 | tf_op jit(solution)/shard_map/ppermute | solution.py:374
  10.2 13.4 %collective-permute-start = (f32[8,1024]{1,0:T(8,128)S(1)}, f32[8,1024]{1,0:T(8,128)S(1)}, u32[]{:S(2)}, u32[]{:S(2)}) collective-permute-start(f32[8,1024]{1,0:T(8,128)S(1)} %get-tuple-element.48), channel_id=1, source_target_pairs={{8,0},{16,8},{24,16},{9,1},{17,9},{25,17},{10,2},{18,10},{26,18},{... | collective-permute-start | bytes 98312 | tf_op jit(solution)/shard_map/ppermute | solution.py:374
  17.7 14.8 %collective-permute-start.5 = (f32[512,256]{1,0:T(8,128)S(1)}, f32[512,256]{1,0:T(8,128)S(1)}, u32[]{:S(2)}, u32[]{:S(2)}) collective-permute-start(f32[512,256]{1,0:T(8,128)S(1)} %get-tuple-element.56), channel_id=1, source_target_pairs={{0,1},{1,0},{2,3},{3,2},{4,5},{5,4},{6,7},{7,6},{8,9},{9,8},{10,11... | collective-permute-start | bytes 1572872 | tf_op jit(solution)/shard_map/ppermute | solution.py:320
  19.2 15.6 %collective-permute-start.4 = (f32[768,256]{1,0:T(8,128)S(1)}, f32[768,256]{1,0:T(8,128)S(1)}, u32[]{:S(2)}, u32[]{:S(2)}) collective-permute-start(f32[768,256]{1,0:T(8,128)S(1)} %get-tuple-element.55), channel_id=1, source_target_pairs={{8,0},{16,8},{24,16},{9,1},{17,9},{25,17},{10,2},{18,10},{26,18},{... | collective-permute-start | bytes 2359304 | tf_op jit(solution)/shard_map/ppermute | solution.py:374
  23.1 8.7 %collective-permute-start.6 = (f32[128,512]{1,0:T(8,128)S(1)}, f32[128,512]{1,0:T(8,128)S(1)}, u32[]{:S(2)}, u32[]{:S(2)}) collective-permute-start(f32[128,512]{1,0:T(8,128)S(1)} %get-tuple-element.57), channel_id=1, source_target_pairs={{0,2},{1,3},{2,0},{3,1},{4,6},{5,7},{6,4},{7,5},{8,10},{9,11},{10,... | collective-permute-start | bytes 786440 | tf_op jit(solution)/shard_map/ppermute | solution.py:320
  26.8 14.1 %collective-permute-start.11 = (f32[768,256]{1,0:T(8,128)S(1)}, f32[768,256]{1,0:T(8,128)S(1)}, u32[]{:S(2)}, u32[]{:S(2)}) collective-permute-start(f32[768,256]{1,0:T(8,128)S(1)} %get-tuple-element.65), channel_id=1, source_target_pairs={{8,0},{16,8},{24,16},{9,1},{17,9},{25,17},{10,2},{18,10},{26,18},{... | collective-permute-start | bytes 2359304 | tf_op jit(solution)/shard_map/ppermute | solution.py:374
  30.3 6.9 %collective-permute-start.3 = (f32[8,1024]{1,0:T(8,128)S(1)}, f32[8,1024]{1,0:T(8,128)S(1)}, u32[]{:S(2)}, u32[]{:S(2)}) collective-permute-start(f32[8,1024]{1,0:T(8,128)S(1)} %join.3.refs_1_.one), channel_id=1, source_target_pairs={{0,1},{1,0},{2,3},{3,2},{4,5},{5,4},{6,7},{7,6},{8,9},{9,8},{10,11... | collective-permute-start | bytes 98312 | tf_op jit(solution)/shard_map/ppermute | solution.py:320
  31.8 14.9 %collective-permute-start.10 = (f32[512,256]{1,0:T(8,128)S(1)}, f32[512,256]{1,0:T(8,128)S(1)}, u32[]{:S(2)}, u32[]{:S(2)}) collective-permute-start(f32[512,256]{1,0:T(8,128)S(1)} %get-tuple-element.64), channel_id=1, source_target_pairs={{0,1},{1,0},{2,3},{3,2},{4,5},{5,4},{6,7},{7,6},{8,9},{9,8},{10,11... | collective-permute-start | bytes 1572872 | tf_op jit(solution)/shard_map/ppermute | solution.py:320
  32.4 18.9 %collective-permute-start.15 = (f32[128,512]{1,0:T(8,128)S(1)}, f32[128,512]{1,0:T(8,128)S(1)}, u32[]{:S(2)}, u32[]{:S(2)}) collective-permute-start(f32[128,512]{1,0:T(8,128)S(1)} %add.15.refs_0_.keep), channel_id=1, source_target_pairs={{4,0},{5,1},{6,2},{7,3},{12,8},{13,9},{14,10},{15,11},{20,16},{21,... | collective-permute-start | bytes 786440 | tf_op jit(solution)/shard_map/ppermute | solution.py:325
  34.8 12.3 %collective-permute-start.9 = (f32[256,256]{1,0:T(8,128)S(1)}, f32[256,256]{1,0:T(8,128)S(1)}, u32[]{:S(2)}, u32[]{:S(2)}) collective-permute-start(f32[256,256]{1,0:T(8,128)S(1)} %get-tuple-element.63), channel_id=1, source_target_pairs={{0,2},{1,3},{2,0},{3,1},{4,6},{5,7},{6,4},{7,5},{8,10},{9,11},{10,... | collective-permute-start | bytes 786440 | tf_op jit(solution)/shard_map/ppermute | solution.py:320
  37.2 12.5 %collective-permute-start.8 = (f32[16,1024]{1,0:T(8,128)S(1)}, f32[16,1024]{1,0:T(8,128)S(1)}, u32[]{:S(2)}, u32[]{:S(2)}) collective-permute-start(f32[16,1024]{1,0:T(8,128)S(1)} %join.4.refs_1_.one), channel_id=1, source_target_pairs={{0,2},{1,3},{2,0},{3,1},{4,6},{5,7},{6,4},{7,5},{8,10},{9,11},{10,... | collective-permute-start | bytes 196616 | tf_op jit(solution)/shard_map/ppermute | solution.py:320
  40.9 13.3 %collective-permute-start.14 = (f32[256,256]{1,0:T(8,128)S(1)}, f32[256,256]{1,0:T(8,128)S(1)}, u32[]{:S(2)}, u32[]{:S(2)}) collective-permute-start(f32[256,256]{1,0:T(8,128)S(1)} %get-tuple-element.70), channel_id=1, source_target_pairs={{0,1},{1,0},{2,3},{3,2},{4,5},{5,4},{6,7},{7,6},{8,9},{9,8},{10,11... | collective-permute-start | bytes 786440 | tf_op jit(solution)/shard_map/ppermute | solution.py:320
  47.1 17.3 %collective-permute-start.16 = (f32[128,256]{1,0:T(8,128)S(1)}, f32[128,256]{1,0:T(8,128)S(1)}, u32[]{:S(2)}, u32[]{:S(2)}) collective-permute-start(f32[128,256]{1,0:T(8,128)S(1)} %get-tuple-element.75), channel_id=1, source_target_pairs={{0,4},{1,5},{2,6},{3,7},{4,0},{5,1},{6,2},{7,3},{8,12},{9,13},{10,... | collective-permute-start | bytes 393224 | tf_op jit(solution)/shard_map/ppermute | solution.py:320
  47.2 15.0 %collective-permute-start.13 = (f32[256,256]{1,0:T(8,128)S(1)}, f32[256,256]{1,0:T(8,128)S(1)}, u32[]{:S(2)}, u32[]{:S(2)}) collective-permute-start(f32[256,256]{1,0:T(8,128)S(1)} %get-tuple-element.69), channel_id=1, source_target_pairs={{0,2},{1,3},{2,0},{3,1},{4,6},{5,7},{6,4},{7,5},{8,10},{9,11},{10,... | collective-permute-start | bytes 786440 | tf_op jit(solution)/shard_map/ppermute | solution.py:320
  49.7 14.7 %collective-permute-start.19 = (f32[256,256]{1,0:T(8,128)S(1)}, f32[256,256]{1,0:T(8,128)S(1)}, u32[]{:S(2)}, u32[]{:S(2)}) collective-permute-start(f32[256,256]{1,0:T(8,128)S(1)} %get-tuple-element.78), channel_id=1, source_target_pairs={{0,1},{1,0},{2,3},{3,2},{4,5},{5,4},{6,7},{7,6},{8,9},{9,8},{10,11... | collective-permute-start | bytes 786440 | tf_op jit(solution)/shard_map/ppermute | solution.py:320
  51.3 11.8 %collective-permute-start.12 = (f32[32,1024]{1,0:T(8,128)S(1)}, f32[32,1024]{1,0:T(8,128)S(1)}, u32[]{:S(2)}, u32[]{:S(2)}) collective-permute-start(f32[32,1024]{1,0:T(8,128)S(1)} %join.5.refs_0_.one), channel_id=1, source_target_pairs={{0,4},{1,5},{2,6},{3,7},{4,0},{5,1},{6,2},{7,3},{8,12},{9,13},{10,... | collective-permute-start | bytes 393224 | tf_op jit(solution)/shard_map/ppermute | solution.py:320
  54.3 12.8 %collective-permute-start.18 = (f32[128,256]{1,0:T(8,128)S(1)}, f32[128,256]{1,0:T(8,128)S(1)}, u32[]{:S(2)}, u32[]{:S(2)}) collective-permute-start(f32[128,256]{1,0:T(8,128)S(1)} %get-tuple-element.77), channel_id=1, source_target_pairs={{0,2},{1,3},{2,0},{3,1},{4,6},{5,7},{6,4},{7,5},{8,10},{9,11},{10,... | collective-permute-start | bytes 393224 | tf_op jit(solution)/shard_map/ppermute | solution.py:320
  62.3 12.6 %collective-permute-start.17 = (f32[128,256]{1,0:T(8,128)S(1)}, f32[128,256]{1,0:T(8,128)S(1)}, u32[]{:S(2)}, u32[]{:S(2)}) collective-permute-start(f32[128,256]{1,0:T(8,128)S(1)} %get-tuple-element.76), channel_id=1, source_target_pairs={{0,4},{1,5},{2,6},{3,7},{4,0},{5,1},{6,2},{7,3},{8,12},{9,13},{10,... | collective-permute-start | bytes 393224 | tf_op jit(solution)/shard_map/ppermute | solution.py:320
  64.4 10.4 %collective-permute-start.21 = (f32[128,256]{1,0:T(8,128)S(1)}, f32[128,256]{1,0:T(8,128)S(1)}, u32[]{:S(2)}, u32[]{:S(2)}) collective-permute-start(f32[128,256]{1,0:T(8,128)S(1)} %get-tuple-element.80), channel_id=1, source_target_pairs={{0,2},{1,3},{2,0},{3,1},{4,6},{5,7},{6,4},{7,5},{8,10},{9,11},{10,... | collective-permute-start | bytes 393224 | tf_op jit(solution)/shard_map/ppermute | solution.py:320
  67.1 10.1 %collective-permute-start.20 = (f32[128,256]{1,0:T(8,128)S(1)}, f32[128,256]{1,0:T(8,128)S(1)}, u32[]{:S(2)}, u32[]{:S(2)}) collective-permute-start(f32[128,256]{1,0:T(8,128)S(1)} %add.24.refs_0_.keep), channel_id=1, source_target_pairs={{0,4},{1,5},{2,6},{3,7},{8,12},{9,13},{10,14},{11,15},{16,20},{17,... | collective-permute-start | bytes 393224 | tf_op jit(solution)/shard_map/ppermute | solution.py:325
  74.9 7.8 %collective-permute-start.22 = (f32[128,256]{1,0:T(8,128)S(1)}, f32[128,256]{1,0:T(8,128)S(1)}, u32[]{:S(2)}, u32[]{:S(2)}) collective-permute-start(f32[128,256]{1,0:T(8,128)S(1)} %add.26.refs_0_.refs_4_), channel_id=1, source_target_pairs={{0,4},{1,5},{2,6},{3,7},{8,12},{9,13},{10,14},{11,15},{16,20},{17,... | collective-permute-start | bytes 393224 | tf_op jit(solution)/shard_map/ppermute | solution.py:325

commit v4 on v3

v4 whole, which is shorter than its diff:
```python
import functools

import jax
import jax.numpy as jnp
from jax import lax
from jax.experimental import pallas as pl
from jax.experimental.pallas import tpu as pltpu
from jax.sharding import PartitionSpec as P

EPS = 1e-06
STATS = 8
VMEM = pl.BlockSpec(memory_space=pltpu.VMEM)
ANY = pl.BlockSpec(memory_space=pl.ANY)


def params(mib):
    return pltpu.CompilerParams(vmem_limit_bytes=mib << 20)


def cost(weight):
    return pl.CostEstimate(flops=int(weight * 1e9), bytes_accessed=1, transcendentals=0)


def split(value):
    high = value.astype(jnp.bfloat16)
    low = (value - high.astype(jnp.float32)).astype(jnp.bfloat16)
    return high, low


def centre(block):
    count = block.shape[0]
    mean = jnp.sum(block, 0, keepdims=True) / count
    centred = block - mean
    left = jnp.sum(centred, 0, keepdims=True) / count
    squares = jnp.sum(centred * centred, 0, keepdims=True)
    return centred, mean, left, squares


def prepare_kernel(dosages, high_t, low_t, stats, *refs):
    blocks, done = refs[:-1], refs[-1]
    width = blocks[0].shape[1]
    long = stats.shape[1]
    copies = []
    for i, block in enumerate(blocks):
        taken = dosages.at[:, pl.ds(i * width, width)]
        copies.append(pltpu.make_async_copy(taken, block, done.at[i]))
    for copy in copies:
        copy.start()
    for i, block in enumerate(blocks):
        copies[i].wait()
        here = pl.ds(i * width, width)
        centred, mean, left, squares = centre(block[...])
        high_t[here, :], low_t[here, :] = split(centred.T)
        rows = [mean, left, squares] + [jnp.zeros_like(mean)] * (STATS - 3)
        first = i * width // long * STATS
        stats[first : first + STATS, i * width % long : i * width % long + width] = jnp.concatenate(rows, 0)


def prepare(dosages, width, long):
    samples, cols = dosages.shape
    count = cols // width
    half_t = jax.ShapeDtypeStruct((cols, samples), jnp.bfloat16)
    stats = jax.ShapeDtypeStruct((STATS * cols // long, long), jnp.float32)
    block = jax.ShapeDtypeStruct((samples, width), jnp.float32)
    out = pl.pallas_call(
        prepare_kernel,
        in_specs=[pl.BlockSpec(memory_space=pltpu.HBM)],
        out_specs=[VMEM] * (3 + count),
        out_shape=[half_t, half_t, stats] + [block] * count,
        scratch_shapes=[pltpu.SemaphoreType.DMA((count,))],
        compiler_params=params(45),
        cost_estimate=cost(4),
        name="prepare",
    )(dosages)
    return out[:2], out[2], out[3:]


def place(owner, me, order):
    apart = jnp.bitwise_xor(owner, me)
    spot = 0
    for bit in order:
        spot = spot * 2 + (lax.shift_right_logical(apart, bit) & 1)
    return spot


def product(high_t, low_t, rows, high, low, side):
    sides = (((1,), (side,)), ((), ()))
    dot = functools.partial(lax.dot_general, dimension_numbers=sides, preferred_element_type=jnp.float32)
    a, b = high_t[rows, :], low_t[rows, :]
    return dot(a, high) + (dot(a, low) + dot(b, high))


def gram_kernel(piece, spots, order, ahead, rows, high_t, low_t, *refs):
    first, last, start, width = piece
    send, keep = refs[-2:]
    cols = high_t.shape[0]
    share = (last - first) // spots
    half = spots // 2
    me = lax.axis_index("samp")
    here = pl.ds(start, width)
    own_high, own_low = high_t[here, :], low_t[here, :]
    if rows:
        for out in (send, keep):
            out[half * share :, :] = refs[ahead][...]
    if ahead:
        ahead_high, ahead_low = split(centre(refs[0][...])[0])
    tall = min(width, 2 * cols // 8)
    for top in range(first, last, tall):
        band = pl.ds(top, tall)
        if top < start + width:
            tile = product(high_t, low_t, band, own_high, own_low, 1)
        if top + tall > start:
            later = product(high_t, low_t, band, ahead_high, ahead_low, 0)
            if top >= start + width:
                tile = later
            else:
                row = lax.broadcasted_iota(jnp.int32, tile.shape, 0) + top
                col = lax.broadcasted_iota(jnp.int32, tile.shape, 1) + start
                tile = jnp.where(col > row, tile, later)
        for part in range(tall // share):
            spot = place(top // share + part, me, order)
            block = tile[part * share : (part + 1) * share]
            there = pl.ds(pl.multiple_of((spot & (half - 1)) * share, share), share)

            @pl.when(spot >= half)
            def _():
                send[there, :] = block

            @pl.when(spot < half)
            def _():
                keep[there, :] = block


def gram(piece, spots, order, prepared, ahead, rows, after, weight):
    first, last, start, width = piece
    extra = sum(array.shape[0] for array in rows)
    out = jax.ShapeDtypeStruct(((last - first) // 2 + extra, width), jnp.float32)
    return pl.pallas_call(
        functools.partial(gram_kernel, piece, spots, order, len(ahead), extra),
        in_specs=[VMEM] * (2 + len(ahead) + len(rows)) + [ANY] * len(after),
        out_specs=[VMEM] * 2,
        out_shape=[out, out],
        compiler_params=params(24),
        cost_estimate=cost(weight),
        name="gram",
    )(*prepared, *ahead, *rows, *after)


def add_kernel(size, parts, extra, keep, got, *refs):
    out = refs[len(refs) - parts :]
    kept = size // parts
    rows = keep.shape[0] - size
    for i, ref in enumerate(out):
        here = slice((parts - 1 - i) * kept, (parts - i) * kept)
        ref[:kept, :] = keep[here, :] + got[here, :]
        if extra == rows and rows:
            far = got[size:, :].reshape(rows // STATS, STATS, -1)
            ref[kept:, :] = keep[size:, :] + pltpu.roll(far, STATS // 2, 1).reshape(rows, -1)
        elif rows:
            ref[kept : kept + rows, :] = keep[size:, :]
            ref[kept + rows :, :] = got[size:, :]


def add(size, pair, parts, extra, after, weight):
    cols = pair[0].shape[1]
    out = jax.ShapeDtypeStruct((size // parts + extra, cols), jnp.float32)
    return pl.pallas_call(
        functools.partial(add_kernel, size, parts, extra),
        in_specs=[VMEM, VMEM] + [ANY] * len(after),
        out_specs=[VMEM] * parts,
        out_shape=[out] * parts,
        compiler_params=params(16),
        cost_estimate=cost(weight),
        name="add",
    )(*pair, *after)


def part_kernel(size, keep, got, *refs):
    body, rows = refs[-2:]
    extra = keep.shape[0] - size
    body[...] = keep[:size, :] + got[:size, :]
    rows[:extra, :] = keep[size:, :]
    rows[extra:, :] = got[size:, :]


def part(size, pair, after, weight):
    rows, cols = pair[0].shape
    shapes = [(size, cols), (2 * (rows - size), cols)]
    return pl.pallas_call(
        functools.partial(part_kernel, size),
        in_specs=[VMEM, VMEM] + [ANY] * len(after),
        out_specs=[VMEM] * 2,
        out_shape=[jax.ShapeDtypeStruct(shape, jnp.float32) for shape in shapes],
        compiler_params=params(16),
        cost_estimate=cost(weight),
        name="part",
    )(*pair, *after)


def join_kernel(one, other, *refs):
    rows = one.shape[0]
    refs[-1][:rows, :] = one[...]
    refs[-1][rows:, :] = other[...]


def join(pair, after, weight):
    rows, cols = pair[0].shape
    return pl.pallas_call(
        join_kernel,
        in_specs=[VMEM, VMEM] + [ANY] * len(after),
        out_specs=VMEM,
        out_shape=jax.ShapeDtypeStruct((2 * rows, cols), jnp.float32),
        compiler_params=params(16),
        cost_estimate=cost(weight),
        name="join",
    )(*pair, *after)


def cross_kernel(parts, start, keep, got, early, *refs):
    send, mine = refs[-2:]
    total = keep[...] + got[...]
    other = early[:, start : start + total.shape[1]]
    upper = lax.axis_index("samp") >= parts // 2

    @pl.when(upper)
    def _():
        send[...] = other
        mine[...] = total

    @pl.when(jnp.logical_not(upper))
    def _():
        send[...] = total
        mine[...] = other


def cross(parts, start, pair, early, after, weight):
    out = jax.ShapeDtypeStruct(pair[0].shape, jnp.float32)
    return pl.pallas_call(
        functools.partial(cross_kernel, parts, start),
        in_specs=[VMEM] * 3 + [ANY] * len(after),
        out_specs=[VMEM] * 2,
        out_shape=[out, out],
        compiler_params=params(16),
        cost_estimate=cost(weight),
        name="cross",
    )(*pair, early, *after)


def weigh_kernel(parts, samples, own, ahead, *refs):
    fix, factor, marks = refs[-3:]
    share, cols = fix.shape
    total = samples * parts
    height = parts * STATS // 2
    me = lax.axis_index("samp")
    long = own.shape[1]

    def every(value):
        value = jnp.sum(value, 0)
        return value + pltpu.roll(value, STATS // 2, 0)

    for side, ref in enumerate((own, ahead)):
        pairs = ref[...].reshape(parts // 2, cols // long, STATS, long)
        for i in range(cols // long):
            stats = pairs[:, i]
            apart = (stats - every(stats)[None] / parts) + pltpu.roll(stats, STATS - 1, 1)
            apart = apart - every(apart)[None] / parts
            kind = lax.broadcasted_iota(jnp.int32, stats.shape, 1) % (STATS // 2)
            mark = jnp.where(kind == 0, apart, jnp.where(kind == 1, stats, 0.0))
            moved = every(mark * mark) * samples
            squares = every(stats)
            spread = (squares[2:3] + (moved[0:1] - moved[1:2])) / total
            here = slice(i * long, (i + 1) * long)
            marks[side * height : (side + 1) * height, here] = mark.reshape(height, long)
            place = 2 * height + side * STATS
            marks[place : place + STATS, here] = jnp.broadcast_to(lax.rsqrt(spread + EPS), (STATS, long))
    first = me * share
    if share % 128 == 0:
        rows = marks[:, pl.ds(pl.multiple_of(first, 128), share)]
    else:
        inside = lax.rem(first, 128)
        window = pl.ds(pl.multiple_of(first - inside, 128), 128)
        rows = pltpu.roll(marks[:, window], lax.rem(128 - inside, 128), 1)[:, :share]
    row_scale = rows[2 * height : 2 * height + 1] / total
    row_scale = jnp.broadcast_to(row_scale, (128, share)).T
    rows = rows[:height]
    kind = lax.broadcasted_iota(jnp.int32, rows.shape, 0) % (STATS // 2)
    signed = jnp.where(kind == 0, rows, jnp.where(kind == 1, -rows, 0.0)) * samples
    dot = functools.partial(
        lax.dot_general,
        dimension_numbers=(((0,), (0,)), ((), ())),
        precision=lax.Precision.HIGHEST,
        preferred_element_type=jnp.float32,
    )
    own_fix, ahead_fix = dot(signed, marks[:height, :]), dot(signed, marks[height : 2 * height, :])
    row = first + lax.broadcasted_iota(jnp.int32, (share, 128), 0)
    lane = lax.broadcasted_iota(jnp.int32, (share, 128), 1)
    for left in range(0, cols, 128):
        here = slice(left, left + 128)
        mine = lane + left > row
        own_scale = marks[2 * height : 2 * height + 1, here]
        ahead_scale = marks[2 * height + STATS : 2 * height + STATS + 1, here]
        fix[:, here] = jnp.where(mine, own_fix[:, here], ahead_fix[:, here])
        factor[:, here] = jnp.where(mine, own_scale, ahead_scale) * row_scale


def weigh(parts, samples, share, cols, own, ahead, after, weight):
    out = jax.ShapeDtypeStruct((share, cols), jnp.float32)
    return pl.pallas_call(
        functools.partial(weigh_kernel, parts, samples),
        in_specs=[VMEM, VMEM] + [ANY] * len(after),
        out_specs=[VMEM] * 2,
        out_shape=[out, out],
        scratch_shapes=[pltpu.VMEM(((parts + 2) * STATS, cols), jnp.float32)],
        compiler_params=params(16),
        cost_estimate=cost(weight),
        name="weigh",
    )(own, ahead, *after)


def finish_kernel(starts, sizes, fix, factor, *refs):
    out, body = refs[-2:]
    share, cols = out.shape
    me = lax.axis_index("samp")
    for i, start in enumerate(starts):
        mine = refs[sum(sizes[:i]) : sum(sizes[: i + 1])]
        total = sum(ref[...] for ref in mine)
        here = slice(start, start + total.shape[1])
        body[:, here] = (total + fix[:, here]) * factor[:, here]
    first = me * share
    turned = pltpu.roll(body[...], lax.rem(2 * cols - first - 1, cols), 1)
    row = lax.broadcasted_iota(jnp.int32, (share, cols), 0)
    step = 1
    while step < share:
        moved = pltpu.roll(turned, cols - step, 1)
        turned = jnp.where((row & step) != 0, moved, turned)
        step *= 2
    out[...] = turned


def finish(starts, weights, sums):
    flat = [array for arrays in sums for array in arrays]
    sizes = [len(arrays) for arrays in sums]
    share, cols = weights[0].shape
    return pl.pallas_call(
        functools.partial(finish_kernel, starts, sizes),
        in_specs=[VMEM] * (2 + len(flat)),
        out_specs=VMEM,
        out_shape=jax.ShapeDtypeStruct((share, cols), jnp.float32),
        scratch_shapes=[pltpu.VMEM((share, cols), jnp.float32)],
        compiler_params=params(16),
        cost_estimate=cost(4),
        name="finish",
    )(*weights, *flat)


PLAN = (
    (0, 0, 0.01),
    (1, 0, 0.01),
    (0, 1, 0.01),
    (2, 0, 0.01),
    (0, 2, 0.01),
    (1, 1, 0.01),
    (5, 0, 1.8),
    (3, 0, 0.01),
    (1, 2, 0.01),
    (2, 1, 0.01),
    (4, 0, 0.01),
    (3, 1, 0.01),
    (1, 3, 2.5),
    (2, 2, 0.01),
    (4, 1, 0.01),
    (3, 2, 2.5),
    (4, 2, 0.01),
    (5, 1, 0.01),
    (2, 3, 1.6),
    (3, 3, 0.08),
)


def plan(steps, pieces):
    if steps == 3:
        return PLAN
    tasks = [(i, step, 1) for step in range(steps) for i in range(pieces)]
    return tasks + [(pieces, 0, 1), (pieces, 1, 1)]


def swap(array, bit, parts):
    return lax.ppermute(array, "samp", [(i, i ^ (1 << bit)) for i in range(parts)])


def local(dosages):
    samples, cols = dosages.shape
    parts = lax.axis_size("samp")
    blocks = lax.axis_size("var")
    share = cols // parts
    steps = parts.bit_length() - 1
    quarter, half = cols // 4, cols // 2
    route = [(i, i - 1) for i in range(1, blocks)]
    pieces = [
        (0, half, half, half),
        (0, cols, 0, quarter),
        (0, cols, quarter, quarter),
        (half, cols, half, quarter),
        (half, cols, half + quarter, quarter),
    ]
    prepared, stats, cuts = prepare(dosages, quarter, half)
    last = stats
    come = [[]] + [[lax.ppermute(cut, "var", route)] for cut in cuts]
    pairs, sums = {}, {}

    for i, step, weight in plan(steps, len(pieces)):
        after = [last]
        if i == len(pieces) and step == 0:
            stats = last = join(stats, after, weight)
            stats_next = lax.ppermute(stats, "var", route)
            continue
        if i == len(pieces):
            weights = weigh(parts, samples, share, cols, stats, stats_next, after, weight)
            last = weights[0]
            continue
        first, end, start, width = pieces[i]
        spots = parts * (end - first) // cols
        order = tuple(range(spots.bit_length() - 1))
        size = (end - first) >> step
        if step == 0:
            rows = [stats] if i == 0 else []
            send, last = gram(pieces[i], spots, order, prepared, come[i], rows, after, weight)
        elif step < steps - 1:
            rows = pairs[i][0].shape[0] - size
            send, last = add(size, pairs[i], 2, rows if step == 1 else 2 * rows, after, weight)
        elif step == steps:
            (last,) = sums[i] = add(share, pairs[i], 1, 0, after, weight)
            continue
        elif i == 0:
            pairs[i], stats = part(share, pairs[i], after, weight)
            last = pairs[i]
            stats = (stats, swap(stats, step, parts))
            continue
        elif end - first == cols:
            send, last = add(size, pairs[i], 2, 0, after, weight)
        else:
            send, last = cross(parts, start - half, pairs[i], pairs[0], after, weight)
        pairs[i] = (last, swap(send, step, parts))
    kept = range(1, len(pieces))
    return finish([pieces[i][2] for i in kept], weights, [sums.get(i, pairs[i]) for i in kept])


def solution(mesh):
    in_specs = (P("samp", "var"),)
    out_specs = P(("var", "samp"), None)
    return jax.shard_map(local, mesh=mesh, in_specs=in_specs, out_specs=out_specs, check_vma=False)
```

time: 84.8 us -> 80.8 us (0.953)
  the two profiles are of different devices: /device:TPU:28 before, /device:TPU:0 now
where the time goes in v4:
time: 80.8 us; the launch traced here: 80.6 us
  waiting for transfers between devices  33.9 us (42%)
  starting transfers between devices  28.6 us (35%)
  Pallas kernels  17.9 us (22%)
    ppermute x15, waiting for transfers between devices, swap(): lax.ppermute(array, 'samp', [(i, i ^ 1 << bit) for i in range(parts)])  33.9 us
    ppermute x15, starting transfers between devices, swap(): lax.ppermute(array, 'samp', [(i, i ^ 1 << bit) for i in range(parts)])  22.1 us
    pallas_call x5, Pallas kernels, gram(): pl.pallas_call(functools.partial(gram_kernel, piece, spots, order, len(ah...  11.7 us
    ppermute x4, starting transfers between devices, local(): come = [[]] + [[lax.ppermute(cut, 'var', route)] for cut in cuts]  5.16 us
    pallas_call x1, Pallas kernels, prepare(): pl.pallas_call(prepare_kernel, in_specs=[pl.BlockSpec(memory_space=pltpu....  2.79 us
    pallas_call x1, Pallas kernels, finish(): pl.pallas_call(functools.partial(finish_kernel, starts, sizes), in_specs=...  1.8 us
  transfers between devices with their start and end apart: 20, of which 11 were waited for; matrix products, arithmetic and copies ran while one was open for 0% of the time, Pallas kernels for 17%

profile of v4, /device:TPU:0, one launch (start us, length us, event | category | flops | bytes accessed | tf_op | source)
XLA Modules:
  0.0 80.6 jit_solution(15059515157565504736)
XLA Ops:
  0.0 2.8 %prepare.1 = (bf16[1024,768]{1,0:T(8,128)(2,1)S(1)}, bf16[1024,768]{1,0:T(8,128)(2,1)S(1)}, f32[16,512]{1,0:T(8,128)S(1)}, f32[768,256]{1,0:T(8,128)S(1)}, f32[7...) custom-call(f32[768,1024]{1,0:T(8,128)} %dosages.1), custom_call_target="tpu_custom_call" | custom-call | flops 4000000000 | bytes 1 | tf_op jit(solution)/shard_map/prepare/pallas_call | solution.py:65
  2.8 1.3 %collective-permute-start.1 = (f32[768,256]{1,0:T(8,128)S(1)}, f32[768,256]{1,0:T(8,128)S(1)}, u32[]{:S(2)}, u32[]{:S(2)}) collective-permute-start(f32[768,256]{1,0:T(8,128)S(1)} %get-tuple-element.49), channel_id=1, source_target_pairs={{8,0},{16,8},{24,16},{9,1},{17,9},{25,17},{10,2},{18,10},{26,18},{... | collective-permute-start | bytes 2359304 | tf_op jit(solution)/shard_map/ppermute | solution.py:408
  4.1 1.7 %gram.5 = (f32[272,512]{1,0:T(8,128)S(1)}, f32[272,512]{1,0:T(8,128)S(1)}) custom-call(bf16[1024,768]{1,0:T(8,128)(2,1)S(1)} %get-tuple-element.44.high_t, bf16[1024,768]{1,0:T(8,128)(2,1)S(1)} %get-tuple-element.45.low_t, f32[16,512]{1,0:T(8,128)S(1)} %get-tuple-element.46.refs_0_.refs_1_, f32[16,512]{1,0:T(8,128)S(1)} %get-tuple-element.46.refs_0_.refs_1_), custom_call_target="tpu_custom_call" | custom-call | flops 10000000 | bytes 1 | tf_op jit(solution)/shard_map/gram/pallas_call | solution.py:138
  5.8 3.0 %collective-permute-start = (f32[272,512]{1,0:T(8,128)S(1)}, f32[272,512]{1,0:T(8,128)S(1)}, u32[]{:S(2)}, u32[]{:S(2)}) collective-permute-start(f32[272,512]{1,0:T(8,128)S(1)} %get-tuple-element.48), channel_id=1, source_target_pairs={{0,1},{1,0},{2,3},{3,2},{4,5},{5,4},{6,7},{7,6},{8,9},{9,8},{10,11... | collective-permute-start | bytes 1671176 | tf_op jit(solution)/shard_map/ppermute | solution.py:388
  8.8 1.3 %collective-permute-start.3 = (f32[768,256]{1,0:T(8,128)S(1)}, f32[768,256]{1,0:T(8,128)S(1)}, u32[]{:S(2)}, u32[]{:S(2)}) collective-permute-start(f32[768,256]{1,0:T(8,128)S(1)} %get-tuple-element.53), channel_id=1, source_target_pairs={{8,0},{16,8},{24,16},{9,1},{17,9},{25,17},{10,2},{18,10},{26,18},{... | collective-permute-start | bytes 2359304 | tf_op jit(solution)/shard_map/ppermute | solution.py:408
  10.1 1.3 %collective-permute-start.10 = (f32[768,256]{1,0:T(8,128)S(1)}, f32[768,256]{1,0:T(8,128)S(1)}, u32[]{:S(2)}, u32[]{:S(2)}) collective-permute-start(f32[768,256]{1,0:T(8,128)S(1)} %get-tuple-element.62), channel_id=1, source_target_pairs={{8,0},{16,8},{24,16},{9,1},{17,9},{25,17},{10,2},{18,10},{26,18},{... | collective-permute-start | bytes 2359304 | tf_op jit(solution)/shard_map/ppermute | solution.py:408
  11.4 0.0 collective-permute-done.1.refs_0_
  11.4 3.4 %gram.6 = (f32[512,256]{1,0:T(8,128)S(1)}, f32[512,256]{1,0:T(8,128)S(1)}) custom-call(bf16[1024,768]{1,0:T(8,128)(2,1)S(1)} %get-tuple-element.44.high_t, bf16[1024,768]{1,0:T(8,128)(2,1)S(1)} %get-tuple-element.45.low_t, f32[768,256]{1,0:T(8,128)S(1)} %collective-permute-done.1.refs_0_, f32[272,512]{1,0:T(8,128)S(1)} %get-tuple-element.47.refs_1_.keep), custom_call_target="tpu_custom_call" | custom-call | flops 10000000 | bytes 1 | tf_op jit(solution)/shard_map/gram/pallas_call | solution.py:138
  14.8 0.1 collective-permute-start.5
  14.9 1.3 %collective-permute-start.7 = (f32[768,256]{1,0:T(8,128)S(1)}, f32[768,256]{1,0:T(8,128)S(1)}, u32[]{:S(2)}, u32[]{:S(2)}) collective-permute-start(f32[768,256]{1,0:T(8,128)S(1)} %get-tuple-element.59), channel_id=1, source_target_pairs={{8,0},{16,8},{24,16},{9,1},{17,9},{25,17},{10,2},{18,10},{26,18},{... | collective-permute-start | bytes 2359304 | tf_op jit(solution)/shard_map/ppermute | solution.py:408
  16.2 5.7 %collective-permute-done.got = f32[272,512]{1,0:T(8,128)S(1)} collective-permute-done((f32[272,512]{1,0:T(8,128)S(1)}, f32[272,512]{1,0:T(8,128)S(1)}, u32[]{:S(2)}, u32[]{:S(2)}) %collective-permute-start) | collective-permute-done | bytes 557088 | tf_op jit(solution)/shard_map/ppermute | solution.py:388
  21.9 0.1 add.10
  22.0 2.4 %collective-permute-start.2 = (f32[144,512]{1,0:T(8,128)S(1)}, f32[144,512]{1,0:T(8,128)S(1)}, u32[]{:S(2)}, u32[]{:S(2)}) collective-permute-start(f32[144,512]{1,0:T(8,128)S(1)} %get-tuple-element.52), channel_id=1, source_target_pairs={{0,2},{1,3},{2,0},{3,1},{4,6},{5,7},{6,4},{7,5},{8,10},{9,11},{10,... | collective-permute-start | bytes 884744 | tf_op jit(solution)/shard_map/ppermute | solution.py:388
  24.4 0.0 collective-permute-done.3.refs_0_
  24.4 3.1 %gram.7 = (f32[512,256]{1,0:T(8,128)S(1)}, f32[512,256]{1,0:T(8,128)S(1)}) custom-call(bf16[1024,768]{1,0:T(8,128)(2,1)S(1)} %get-tuple-element.44.high_t, bf16[1024,768]{1,0:T(8,128)(2,1)S(1)} %get-tuple-element.45.low_t, f32[768,256]{1,0:T(8,128)S(1)} %collective-permute-done.3.refs_0_, f32[144,512]{1,0:T(8,128)S(1)} %get-tuple-element.51.refs_1_.keep), custom_call_target="tpu_custom_call" | custom-call | flops 10000000 | bytes 1 | tf_op jit(solution)/shard_map/gram/pallas_call | solution.py:138
  27.5 1.5 %collective-permute-start.8 = (f32[512,256]{1,0:T(8,128)S(1)}, f32[512,256]{1,0:T(8,128)S(1)}, u32[]{:S(2)}, u32[]{:S(2)}) collective-permute-start(f32[512,256]{1,0:T(8,128)S(1)} %get-tuple-element.60), channel_id=1, source_target_pairs={{0,1},{1,0},{2,3},{3,2},{4,5},{5,4},{6,7},{7,6},{8,9},{9,8},{10,11... | collective-permute-start | bytes 1572872 | tf_op jit(solution)/shard_map/ppermute | solution.py:388
  29.0 2.1 %collective-permute-done.2.got = f32[144,512]{1,0:T(8,128)S(1)} collective-permute-done((f32[144,512]{1,0:T(8,128)S(1)}, f32[144,512]{1,0:T(8,128)S(1)}, u32[]{:S(2)}, u32[]{:S(2)}) %collective-permute-start.2) | collective-permute-done | bytes 294944 | tf_op jit(solution)/shard_map/ppermute | solution.py:388
  31.1 3.6 %collective-permute-start.4 = (f32[32,512]{1,0:T(8,128)S(1)}, f32[32,512]{1,0:T(8,128)S(1)}, u32[]{:S(2)}, u32[]{:S(2)}) collective-permute-start(f32[32,512]{1,0:T(8,128)S(1)} %get-tuple-element.55.one), channel_id=1, source_target_pairs={{0,4},{1,5},{2,6},{3,7},{4,0},{5,1},{6,2},{7,3},{8,12},{9,13},{10,... | collective-permute-start | bytes 196616 | tf_op jit(solution)/shard_map/ppermute | solution.py:388
  34.7 0.0 collective-permute-done.5.got
  34.7 0.1 add.11
  34.7 1.6 %collective-permute-start.9 = (f32[256,256]{1,0:T(8,128)S(1)}, f32[256,256]{1,0:T(8,128)S(1)}, u32[]{:S(2)}, u32[]{:S(2)}) collective-permute-start(f32[256,256]{1,0:T(8,128)S(1)} %get-tuple-element.61), channel_id=1, source_target_pairs={{0,2},{1,3},{2,0},{3,1},{4,6},{5,7},{6,4},{7,5},{8,10},{9,11},{10,... | collective-permute-start | bytes 786440 | tf_op jit(solution)/shard_map/ppermute | solution.py:388
  36.4 2.6 %collective-permute-done.4.other = f32[32,512]{1,0:T(8,128)S(1)} collective-permute-done((f32[32,512]{1,0:T(8,128)S(1)}, f32[32,512]{1,0:T(8,128)S(1)}, u32[]{:S(2)}, u32[]{:S(2)}) %collective-permute-start.4) | collective-permute-done | bytes 65568 | tf_op jit(solution)/shard_map/ppermute | solution.py:388
  39.0 0.0 collective-permute-done.10.refs_0_
  39.1 1.9 %gram.8 = (f32[256,256]{1,0:T(8,128)S(1)}, f32[256,256]{1,0:T(8,128)S(1)}) custom-call(bf16[1024,768]{1,0:T(8,128)(2,1)S(1)} %get-tuple-element.44.high_t, bf16[1024,768]{1,0:T(8,128)(2,1)S(1)} %get-tuple-element.45.low_t, f32[768,256]{1,0:T(8,128)S(1)} %collective-permute-done.10.refs_0_, f32[64,512]{1,0:T(8,128)S(1)} %join.1.refs_1_.own), custom_call_target="tpu_custom_call" | custom-call | flops 10000000 | bytes 1 | tf_op jit(solution)/shard_map/gram/pallas_call | solution.py:138
  41.0 1.8 %collective-permute-start.14 = (f32[256,256]{1,0:T(8,128)S(1)}, f32[256,256]{1,0:T(8,128)S(1)}, u32[]{:S(2)}, u32[]{:S(2)}) collective-permute-start(f32[256,256]{1,0:T(8,128)S(1)} %get-tuple-element.70), channel_id=1, source_target_pairs={{0,1},{1,0},{2,3},{3,2},{4,5},{5,4},{6,7},{7,6},{8,9},{9,8},{10,11... | collective-permute-start | bytes 786440 | tf_op jit(solution)/shard_map/ppermute | solution.py:388
  42.7 1.0 %collective-permute-done.9.got = f32[256,256]{1,0:T(8,128)S(1)} collective-permute-done((f32[256,256]{1,0:T(8,128)S(1)}, f32[256,256]{1,0:T(8,128)S(1)}, u32[]{:S(2)}, u32[]{:S(2)}) %collective-permute-start.9) | collective-permute-done | bytes 262176 | tf_op jit(solution)/shard_map/ppermute | solution.py:388
  43.8 0.5 collective-permute-start.13
  44.3 0.0 collective-permute-done.8.got
  44.3 0.1 add.13
  44.3 2.5 %collective-permute-start.12 = (f32[256,256]{1,0:T(8,128)S(1)}, f32[256,256]{1,0:T(8,128)S(1)}, u32[]{:S(2)}, u32[]{:S(2)}) collective-permute-start(f32[256,256]{1,0:T(8,128)S(1)} %get-tuple-element.68), channel_id=1, source_target_pairs={{0,2},{1,3},{2,0},{3,1},{4,6},{5,7},{6,4},{7,5},{8,10},{9,11},{10,... | collective-permute-start | bytes 786440 | tf_op jit(solution)/shard_map/ppermute | solution.py:388
  46.9 0.0 collective-permute-done.7.refs_0_
  46.9 1.6 %gram.9 = (f32[256,256]{1,0:T(8,128)S(1)}, f32[256,256]{1,0:T(8,128)S(1)}) custom-call(bf16[1024,768]{1,0:T(8,128)(2,1)S(1)} %get-tuple-element.44.high_t, bf16[1024,768]{1,0:T(8,128)(2,1)S(1)} %get-tuple-element.45.low_t, f32[768,256]{1,0:T(8,128)S(1)} %collective-permute-done.7.refs_0_, f32[256,256]{1,0:T(8,128)S(1)} %get-tuple-element.65.refs_1_.keep), custom_call_target="tpu_custom_call" | custom-call | flops 10000000 | bytes 1 | tf_op jit(solution)/shard_map/gram/pallas_call | solution.py:138
  48.4 1.8 %collective-permute-start.11 = (f32[256,256]{1,0:T(8,128)S(1)}, f32[256,256]{1,0:T(8,128)S(1)}, u32[]{:S(2)}, u32[]{:S(2)}) collective-permute-start(f32[256,256]{1,0:T(8,128)S(1)} %get-tuple-element.67), channel_id=1, source_target_pairs={{0,1},{1,0},{2,3},{3,2},{4,5},{5,4},{6,7},{7,6},{8,9},{9,8},{10,11... | collective-permute-start | bytes 786440 | tf_op jit(solution)/shard_map/ppermute | solution.py:388
  50.2 1.3 %collective-permute-start.6 = (f32[64,512]{1,0:T(8,128)S(1)}, f32[64,512]{1,0:T(8,128)S(1)}, u32[]{:S(2)}, u32[]{:S(2)}) collective-permute-start(f32[64,512]{1,0:T(8,128)S(1)} %join.1.refs_1_.own), channel_id=1, source_target_pairs={{8,0},{16,8},{24,16},{9,1},{17,9},{25,17},{10,2},{18,10},{26,18},{... | collective-permute-start | bytes 393224 | tf_op jit(solution)/shard_map/ppermute | solution.py:415
  51.5 0.0 collective-permute-done.14.got
  51.6 0.1 collective-permute-start.16
  51.7 1.2 %collective-permute-done.13.got = f32[128,256]{1,0:T(8,128)S(1)} collective-permute-done((f32[128,256]{1,0:T(8,128)S(1)}, f32[128,256]{1,0:T(8,128)S(1)}, u32[]{:S(2)}, u32[]{:S(2)}) %collective-permute-start.13) | collective-permute-done | bytes 131104 | tf_op jit(solution)/shard_map/ppermute | solution.py:388
  52.9 2.1 %collective-permute-done.12.got = f32[256,256]{1,0:T(8,128)S(1)} collective-permute-done((f32[256,256]{1,0:T(8,128)S(1)}, f32[256,256]{1,0:T(8,128)S(1)}, u32[]{:S(2)}, u32[]{:S(2)}) %collective-permute-start.12) | collective-permute-done | bytes 262176 | tf_op jit(solution)/shard_map/ppermute | solution.py:388
  55.0 2.6 %collective-permute-done.11.got = f32[256,256]{1,0:T(8,128)S(1)} collective-permute-done((f32[256,256]{1,0:T(8,128)S(1)}, f32[256,256]{1,0:T(8,128)S(1)}, u32[]{:S(2)}, u32[]{:S(2)}) %collective-permute-start.11) | collective-permute-done | bytes 262176 | tf_op jit(solution)/shard_map/ppermute | solution.py:388
  57.6 0.2 collective-permute-start.15
  57.9 2.5 %collective-permute-start.17 = (f32[128,256]{1,0:T(8,128)S(1)}, f32[128,256]{1,0:T(8,128)S(1)}, u32[]{:S(2)}, u32[]{:S(2)}) collective-permute-start(f32[128,256]{1,0:T(8,128)S(1)} %get-tuple-element.80), channel_id=1, source_target_pairs={{0,4},{1,5},{2,6},{3,7},{4,0},{5,1},{6,2},{7,3},{8,12},{9,13},{10,... | collective-permute-start | bytes 393224 | tf_op jit(solution)/shard_map/ppermute | solution.py:388
  60.3 0.0 collective-permute-done.16.got
  60.4 0.5 collective-permute-start.18
  60.9 5.0 %collective-permute-done.15.got = f32[128,256]{1,0:T(8,128)S(1)} collective-permute-done((f32[128,256]{1,0:T(8,128)S(1)}, f32[128,256]{1,0:T(8,128)S(1)}, u32[]{:S(2)}, u32[]{:S(2)}) %collective-permute-start.15) | collective-permute-done | bytes 131104 | tf_op jit(solution)/shard_map/ppermute | solution.py:388
  65.9 0.1 collective-permute-start.19
  66.0 0.0 collective-permute-done.6.ahead
  66.0 1.2 %weigh.1 = (f32[128,1024]{1,0:T(8,128)S(1)}, f32[128,1024]{1,0:T(8,128)S(1)}) custom-call(f32[64,512]{1,0:T(8,128)S(1)} %join.1.refs_1_.own, f32[64,512]{1,0:T(8,128)S(1)} %collective-permute-done.6.ahead, f32[128,256]{1,0:T(8,128)S(1)} %get-tuple-element.77.refs_0_.refs_3_), custom_call_target="tpu_custom_call" | custom-call | flops 10000000 | bytes 1 | tf_op jit(solution)/shard_map/weigh/pallas_call | solution.py:308
  67.2 6.3 %collective-permute-done.17.got = f32[128,256]{1,0:T(8,128)S(1)} collective-permute-done((f32[128,256]{1,0:T(8,128)S(1)}, f32[128,256]{1,0:T(8,128)S(1)}, u32[]{:S(2)}, u32[]{:S(2)}) %collective-permute-start.17) | collective-permute-done | bytes 131104 | tf_op jit(solution)/shard_map/ppermute | solution.py:388
  73.5 2.8 %collective-permute-done.18.got = f32[128,256]{1,0:T(8,128)S(1)} collective-permute-done((f32[128,256]{1,0:T(8,128)S(1)}, f32[128,256]{1,0:T(8,128)S(1)}, u32[]{:S(2)}, u32[]{:S(2)}) %collective-permute-start.18) | collective-permute-done | bytes 131104 | tf_op jit(solution)/shard_map/ppermute | solution.py:388
  76.3 2.4 %collective-permute-done.19.refs_4_ = f32[128,256]{1,0:T(8,128)S(1)} collective-permute-done((f32[128,256]{1,0:T(8,128)S(1)}, f32[128,256]{1,0:T(8,128)S(1)}, u32[]{:S(2)}, u32[]{:S(2)}) %collective-permute-start.19) | collective-permute-done | bytes 131104 | tf_op jit(solution)/shard_map/ppermute | solution.py:388
  78.8 1.8 %finish.1 = f32[128,1024]{1,0:T(8,128)} custom-call(f32[128,1024]{1,0:T(8,128)S(1)} %get-tuple-element.78.refs_0_.fix, f32[128,1024]{1,0:T(8,128)S(1)} %get-tuple-element.79.factor, f32[128,256]{1,0:T(8,128)S(1)} %add.15.refs_0_, f32[128,256]{1,0:T(8,128)S(1)} %add.18.refs_0_.refs_1_, f32[128,256]{1,0:T(8,128)S(1)} %add.19.refs_2_, ...), custom_call_target="tpu_custom_call" | custom-call | flops 4000000000 | bytes 1 | tf_op jit(solution)/shard_map/finish/pallas_call | solution.py:344
  (11 shorter events, 0.3 us)
Async XLA Ops:
  2.8 8.6 %collective-permute-start.1 = (f32[768,256]{1,0:T(8,128)S(1)}, f32[768,256]{1,0:T(8,128)S(1)}, u32[]{:S(2)}, u32[]{:S(2)}) collective-permute-start(f32[768,256]{1,0:T(8,128)S(1)} %get-tuple-element.49), channel_id=1, source_target_pairs={{8,0},{16,8},{24,16},{9,1},{17,9},{25,17},{10,2},{18,10},{26,18},{... | collective-permute-start | bytes 2359304 | tf_op jit(solution)/shard_map/ppermute | solution.py:408
  5.8 16.1 %collective-permute-start = (f32[272,512]{1,0:T(8,128)S(1)}, f32[272,512]{1,0:T(8,128)S(1)}, u32[]{:S(2)}, u32[]{:S(2)}) collective-permute-start(f32[272,512]{1,0:T(8,128)S(1)} %get-tuple-element.48), channel_id=1, source_target_pairs={{0,1},{1,0},{2,3},{3,2},{4,5},{5,4},{6,7},{7,6},{8,9},{9,8},{10,11... | collective-permute-start | bytes 1671176 | tf_op jit(solution)/shard_map/ppermute | solution.py:388
  8.8 15.6 %collective-permute-start.3 = (f32[768,256]{1,0:T(8,128)S(1)}, f32[768,256]{1,0:T(8,128)S(1)}, u32[]{:S(2)}, u32[]{:S(2)}) collective-permute-start(f32[768,256]{1,0:T(8,128)S(1)} %get-tuple-element.53), channel_id=1, source_target_pairs={{8,0},{16,8},{24,16},{9,1},{17,9},{25,17},{10,2},{18,10},{26,18},{... | collective-permute-start | bytes 2359304 | tf_op jit(solution)/shard_map/ppermute | solution.py:408
  10.1 29.0 %collective-permute-start.10 = (f32[768,256]{1,0:T(8,128)S(1)}, f32[768,256]{1,0:T(8,128)S(1)}, u32[]{:S(2)}, u32[]{:S(2)}) collective-permute-start(f32[768,256]{1,0:T(8,128)S(1)} %get-tuple-element.62), channel_id=1, source_target_pairs={{8,0},{16,8},{24,16},{9,1},{17,9},{25,17},{10,2},{18,10},{26,18},{... | collective-permute-start | bytes 2359304 | tf_op jit(solution)/shard_map/ppermute | solution.py:408
  14.8 19.9 %collective-permute-start.5 = (f32[512,256]{1,0:T(8,128)S(1)}, f32[512,256]{1,0:T(8,128)S(1)}, u32[]{:S(2)}, u32[]{:S(2)}) collective-permute-start(f32[512,256]{1,0:T(8,128)S(1)} %get-tuple-element.56), channel_id=1, source_target_pairs={{0,1},{1,0},{2,3},{3,2},{4,5},{5,4},{6,7},{7,6},{8,9},{9,8},{10,11... | collective-permute-start | bytes 1572872 | tf_op jit(solution)/shard_map/ppermute | solution.py:388
  14.9 32.0 %collective-permute-start.7 = (f32[768,256]{1,0:T(8,128)S(1)}, f32[768,256]{1,0:T(8,128)S(1)}, u32[]{:S(2)}, u32[]{:S(2)}) collective-permute-start(f32[768,256]{1,0:T(8,128)S(1)} %get-tuple-element.59), channel_id=1, source_target_pairs={{8,0},{16,8},{24,16},{9,1},{17,9},{25,17},{10,2},{18,10},{26,18},{... | collective-permute-start | bytes 2359304 | tf_op jit(solution)/shard_map/ppermute | solution.py:408
  22.0 9.1 %collective-permute-start.2 = (f32[144,512]{1,0:T(8,128)S(1)}, f32[144,512]{1,0:T(8,128)S(1)}, u32[]{:S(2)}, u32[]{:S(2)}) collective-permute-start(f32[144,512]{1,0:T(8,128)S(1)} %get-tuple-element.52), channel_id=1, source_target_pairs={{0,2},{1,3},{2,0},{3,1},{4,6},{5,7},{6,4},{7,5},{8,10},{9,11},{10,... | collective-permute-start | bytes 884744 | tf_op jit(solution)/shard_map/ppermute | solution.py:388
  27.5 16.7 %collective-permute-start.8 = (f32[512,256]{1,0:T(8,128)S(1)}, f32[512,256]{1,0:T(8,128)S(1)}, u32[]{:S(2)}, u32[]{:S(2)}) collective-permute-start(f32[512,256]{1,0:T(8,128)S(1)} %get-tuple-element.60), channel_id=1, source_target_pairs={{0,1},{1,0},{2,3},{3,2},{4,5},{5,4},{6,7},{7,6},{8,9},{9,8},{10,11... | collective-permute-start | bytes 1572872 | tf_op jit(solution)/shard_map/ppermute | solution.py:388
  31.1 7.9 %collective-permute-start.4 = (f32[32,512]{1,0:T(8,128)S(1)}, f32[32,512]{1,0:T(8,128)S(1)}, u32[]{:S(2)}, u32[]{:S(2)}) collective-permute-start(f32[32,512]{1,0:T(8,128)S(1)} %get-tuple-element.55.one), channel_id=1, source_target_pairs={{0,4},{1,5},{2,6},{3,7},{4,0},{5,1},{6,2},{7,3},{8,12},{9,13},{10,... | collective-permute-start | bytes 196616 | tf_op jit(solution)/shard_map/ppermute | solution.py:388
  34.7 9.0 %collective-permute-start.9 = (f32[256,256]{1,0:T(8,128)S(1)}, f32[256,256]{1,0:T(8,128)S(1)}, u32[]{:S(2)}, u32[]{:S(2)}) collective-permute-start(f32[256,256]{1,0:T(8,128)S(1)} %get-tuple-element.61), channel_id=1, source_target_pairs={{0,2},{1,3},{2,0},{3,1},{4,6},{5,7},{6,4},{7,5},{8,10},{9,11},{10,... | collective-permute-start | bytes 786440 | tf_op jit(solution)/shard_map/ppermute | solution.py:388
  41.0 10.6 %collective-permute-start.14 = (f32[256,256]{1,0:T(8,128)S(1)}, f32[256,256]{1,0:T(8,128)S(1)}, u32[]{:S(2)}, u32[]{:S(2)}) collective-permute-start(f32[256,256]{1,0:T(8,128)S(1)} %get-tuple-element.70), channel_id=1, source_target_pairs={{0,1},{1,0},{2,3},{3,2},{4,5},{5,4},{6,7},{7,6},{8,9},{9,8},{10,11... | collective-permute-start | bytes 786440 | tf_op jit(solution)/shard_map/ppermute | solution.py:388
  43.8 9.1 %collective-permute-start.13 = (f32[128,256]{1,0:T(8,128)S(1)}, f32[128,256]{1,0:T(8,128)S(1)}, u32[]{:S(2)}, u32[]{:S(2)}) collective-permute-start(f32[128,256]{1,0:T(8,128)S(1)} %get-tuple-element.69), channel_id=1, source_target_pairs={{0,4},{1,5},{2,6},{3,7},{4,0},{5,1},{6,2},{7,3},{8,12},{9,13},{10,... | collective-permute-start | bytes 393224 | tf_op jit(solution)/shard_map/ppermute | solution.py:388
  44.3 10.7 %collective-permute-start.12 = (f32[256,256]{1,0:T(8,128)S(1)}, f32[256,256]{1,0:T(8,128)S(1)}, u32[]{:S(2)}, u32[]{:S(2)}) collective-permute-start(f32[256,256]{1,0:T(8,128)S(1)} %get-tuple-element.68), channel_id=1, source_target_pairs={{0,2},{1,3},{2,0},{3,1},{4,6},{5,7},{6,4},{7,5},{8,10},{9,11},{10,... | collective-permute-start | bytes 786440 | tf_op jit(solution)/shard_map/ppermute | solution.py:388
  48.4 9.2 %collective-permute-start.11 = (f32[256,256]{1,0:T(8,128)S(1)}, f32[256,256]{1,0:T(8,128)S(1)}, u32[]{:S(2)}, u32[]{:S(2)}) collective-permute-start(f32[256,256]{1,0:T(8,128)S(1)} %get-tuple-element.67), channel_id=1, source_target_pairs={{0,1},{1,0},{2,3},{3,2},{4,5},{5,4},{6,7},{7,6},{8,9},{9,8},{10,11... | collective-permute-start | bytes 786440 | tf_op jit(solution)/shard_map/ppermute | solution.py:388
  50.2 15.8 %collective-permute-start.6 = (f32[64,512]{1,0:T(8,128)S(1)}, f32[64,512]{1,0:T(8,128)S(1)}, u32[]{:S(2)}, u32[]{:S(2)}) collective-permute-start(f32[64,512]{1,0:T(8,128)S(1)} %join.1.refs_1_.own), channel_id=1, source_target_pairs={{8,0},{16,8},{24,16},{9,1},{17,9},{25,17},{10,2},{18,10},{26,18},{... | collective-permute-start | bytes 393224 | tf_op jit(solution)/shard_map/ppermute | solution.py:415
  51.6 8.7 %collective-permute-start.16 = (f32[128,256]{1,0:T(8,128)S(1)}, f32[128,256]{1,0:T(8,128)S(1)}, u32[]{:S(2)}, u32[]{:S(2)}) collective-permute-start(f32[128,256]{1,0:T(8,128)S(1)} %get-tuple-element.75), channel_id=1, source_target_pairs={{0,2},{1,3},{2,0},{3,1},{4,6},{5,7},{6,4},{7,5},{8,10},{9,11},{10,... | collective-permute-start | bytes 393224 | tf_op jit(solution)/shard_map/ppermute | solution.py:388
  57.6 8.3 %collective-permute-start.15 = (f32[128,256]{1,0:T(8,128)S(1)}, f32[128,256]{1,0:T(8,128)S(1)}, u32[]{:S(2)}, u32[]{:S(2)}) collective-permute-start(f32[128,256]{1,0:T(8,128)S(1)} %get-tuple-element.74), channel_id=1, source_target_pairs={{0,2},{1,3},{2,0},{3,1},{4,6},{5,7},{6,4},{7,5},{8,10},{9,11},{10,... | collective-permute-start | bytes 393224 | tf_op jit(solution)/shard_map/ppermute | solution.py:388
  57.9 15.7 %collective-permute-start.17 = (f32[128,256]{1,0:T(8,128)S(1)}, f32[128,256]{1,0:T(8,128)S(1)}, u32[]{:S(2)}, u32[]{:S(2)}) collective-permute-start(f32[128,256]{1,0:T(8,128)S(1)} %get-tuple-element.80), channel_id=1, source_target_pairs={{0,4},{1,5},{2,6},{3,7},{4,0},{5,1},{6,2},{7,3},{8,12},{9,13},{10,... | collective-permute-start | bytes 393224 | tf_op jit(solution)/shard_map/ppermute | solution.py:388
  60.4 16.0 %collective-permute-start.18 = (f32[128,256]{1,0:T(8,128)S(1)}, f32[128,256]{1,0:T(8,128)S(1)}, u32[]{:S(2)}, u32[]{:S(2)}) collective-permute-start(f32[128,256]{1,0:T(8,128)S(1)} %get-tuple-element.81), channel_id=1, source_target_pairs={{0,4},{1,5},{2,6},{3,7},{4,0},{5,1},{6,2},{7,3},{8,12},{9,13},{10,... | collective-permute-start | bytes 393224 | tf_op jit(solution)/shard_map/ppermute | solution.py:388
  65.9 12.9 %collective-permute-start.19 = (f32[128,256]{1,0:T(8,128)S(1)}, f32[128,256]{1,0:T(8,128)S(1)}, u32[]{:S(2)}, u32[]{:S(2)}) collective-permute-start(f32[128,256]{1,0:T(8,128)S(1)} %get-tuple-element.82), channel_id=1, source_target_pairs={{0,4},{1,5},{2,6},{3,7},{4,0},{5,1},{6,2},{7,3},{8,12},{9,13},{10,... | collective-permute-start | bytes 393224 | tf_op jit(solution)/shard_map/ppermute | solution.py:388

commit v5 on v4

--- a/solution.py
+++ b/solution.py
@@ -320,20 +320,23 @@
 def finish_kernel(starts, sizes, fix, factor, *refs):
     out, body = refs[-2:]
     share, cols = out.shape
-    me = lax.axis_index("samp")
+    first = lax.axis_index("samp") * share
+    inside = lax.rem(first, 128)
     for i, start in enumerate(starts):
         mine = refs[sum(sizes[:i]) : sum(sizes[: i + 1])]
-        total = sum(ref[...] for ref in mine)
-        here = slice(start, start + total.shape[1])
-        body[:, here] = (total + fix[:, here]) * factor[:, here]
-    first = me * share
-    turned = pltpu.roll(body[...], lax.rem(2 * cols - first - 1, cols), 1)
+        for left in range(0, mine[0].shape[1], 128):
+            total = sum(ref[:, left : left + 128] for ref in mine)
+            here = slice(start + left, start + left + 128)
+            there = lax.rem(start + left + cols - (first - inside), cols)
+            there = pl.ds(pl.multiple_of(there, 128), 128)
+            body[:, there] = (total + fix[:, here]) * factor[:, here]
+    if share % 128:
+        body[...] = pltpu.roll(body[...], lax.rem(cols - inside, cols), 1)
+    tops = range(0, share, 8)
+    turned = jnp.concatenate([pltpu.roll(body[top : top + 8, :], cols - top - 1, 1) for top in tops], 0)
     row = lax.broadcasted_iota(jnp.int32, (share, cols), 0)
-    step = 1
-    while step < share:
-        moved = pltpu.roll(turned, cols - step, 1)
-        turned = jnp.where((row & step) != 0, moved, turned)
-        step *= 2
+    for step in (1, 2, 4):
+        turned = jnp.where((row & step) != 0, pltpu.roll(turned, cols - step, 1), turned)
     out[...] = turned
 
 
@@ -362,12 +365,12 @@
     (1, 1, 0.01),
     (5, 0, 1.8),
     (3, 0, 0.01),
+    (2, 1, 0.01),
     (1, 2, 0.01),
-    (2, 1, 0.01),
     (4, 0, 0.01),
     (3, 1, 0.01),
-    (1, 3, 2.5),
-    (2, 2, 0.01),
+    (1, 3, 0.6),
+    (2, 2, 1.66),
     (4, 1, 0.01),
     (3, 2, 2.5),
     (4, 2, 0.01),

time: 80.8 us -> 80.2 us (level)
  waiting for transfers between devices: 33.9 us -> 25.6 us
  starting transfers between devices: 28.6 us -> 36.2 us
    ppermute x15, waiting for transfers between devices: 33.9 us -> 25.6 us  [swap(): lax.ppermute(array, 'samp', [(i, i ^ 1 << bit) for i in range(parts)])]
    ppermute x15, starting transfers between devices: 22.1 us -> 29.8 us  [swap(): lax.ppermute(array, 'samp', [(i, i ^ 1 << bit) for i in range(parts)])]
  transfers between devices with their start and end apart: 20 -> 20, of which waited for: 11 -> 10; matrix products, arithmetic and copies ran while one was open for 0% -> 0% of each run, Pallas kernels for 17% -> 17%
where the time goes in v5:
time: 80.2 us; the launch traced here: 79.7 us
  starting transfers between devices  36.2 us (45%)
  waiting for transfers between devices  25.6 us (32%)
  Pallas kernels  17.7 us (22%)
    ppermute x15, starting transfers between devices, swap(): lax.ppermute(array, 'samp', [(i, i ^ 1 << bit) for i in range(parts)])  29.8 us
    ppermute x15, waiting for transfers between devices, swap(): lax.ppermute(array, 'samp', [(i, i ^ 1 << bit) for i in range(parts)])  25.6 us
    pallas_call x5, Pallas kernels, gram(): pl.pallas_call(functools.partial(gram_kernel, piece, spots, order, len(ah...  11.7 us
    ppermute x4, starting transfers between devices, local(): come = [[]] + [[lax.ppermute(cut, 'var', route)] for cut in cuts]  5.16 us
    pallas_call x1, Pallas kernels, prepare(): pl.pallas_call(prepare_kernel, in_specs=[pl.BlockSpec(memory_space=pltpu....  2.79 us
  transfers between devices with their start and end apart: 20, of which 10 were waited for; matrix products, arithmetic and copies ran while one was open for 0% of the time, Pallas kernels for 17%

profile of v5, /device:TPU:0, one launch (start us, length us, event | category | flops | bytes accessed | tf_op | source)
XLA Modules:
  0.0 79.7 jit_solution(14467402486781429611)
XLA Ops:
  0.0 2.8 %prepare.1 = (bf16[1024,768]{1,0:T(8,128)(2,1)S(1)}, bf16[1024,768]{1,0:T(8,128)(2,1)S(1)}, f32[16,512]{1,0:T(8,128)S(1)}, f32[768,256]{1,0:T(8,128)S(1)}, f32[7...) custom-call(f32[768,1024]{1,0:T(8,128)} %dosages.1), custom_call_target="tpu_custom_call" | custom-call | flops 4000000000 | bytes 1 | tf_op jit(solution)/shard_map/prepare/pallas_call | solution.py:65
  2.8 1.3 %collective-permute-start.1 = (f32[768,256]{1,0:T(8,128)S(1)}, f32[768,256]{1,0:T(8,128)S(1)}, u32[]{:S(2)}, u32[]{:S(2)}) collective-permute-start(f32[768,256]{1,0:T(8,128)S(1)} %get-tuple-element.49), channel_id=1, source_target_pairs={{8,0},{16,8},{24,16},{9,1},{17,9},{25,17},{10,2},{18,10},{26,18},{... | collective-permute-start | bytes 2359304 | tf_op jit(solution)/shard_map/ppermute | solution.py:411
  4.1 1.3 %collective-permute-start.3 = (f32[768,256]{1,0:T(8,128)S(1)}, f32[768,256]{1,0:T(8,128)S(1)}, u32[]{:S(2)}, u32[]{:S(2)}) collective-permute-start(f32[768,256]{1,0:T(8,128)S(1)} %get-tuple-element.53), channel_id=1, source_target_pairs={{8,0},{16,8},{24,16},{9,1},{17,9},{25,17},{10,2},{18,10},{26,18},{... | collective-permute-start | bytes 2359304 | tf_op jit(solution)/shard_map/ppermute | solution.py:411
  5.4 1.7 %gram.5 = (f32[272,512]{1,0:T(8,128)S(1)}, f32[272,512]{1,0:T(8,128)S(1)}) custom-call(bf16[1024,768]{1,0:T(8,128)(2,1)S(1)} %get-tuple-element.44.high_t, bf16[1024,768]{1,0:T(8,128)(2,1)S(1)} %get-tuple-element.45.low_t, f32[16,512]{1,0:T(8,128)S(1)} %get-tuple-element.46.refs_0_.refs_1_, f32[16,512]{1,0:T(8,128)S(1)} %get-tuple-element.46.refs_0_.refs_1_), custom_call_target="tpu_custom_call" | custom-call | flops 10000000 | bytes 1 | tf_op jit(solution)/shard_map/gram/pallas_call | solution.py:138
  7.1 3.0 %collective-permute-start = (f32[272,512]{1,0:T(8,128)S(1)}, f32[272,512]{1,0:T(8,128)S(1)}, u32[]{:S(2)}, u32[]{:S(2)}) collective-permute-start(f32[272,512]{1,0:T(8,128)S(1)} %get-tuple-element.48), channel_id=1, source_target_pairs={{0,1},{1,0},{2,3},{3,2},{4,5},{5,4},{6,7},{7,6},{8,9},{9,8},{10,11... | collective-permute-start | bytes 1671176 | tf_op jit(solution)/shard_map/ppermute | solution.py:391
  10.1 1.3 %collective-permute-start.10 = (f32[768,256]{1,0:T(8,128)S(1)}, f32[768,256]{1,0:T(8,128)S(1)}, u32[]{:S(2)}, u32[]{:S(2)}) collective-permute-start(f32[768,256]{1,0:T(8,128)S(1)} %get-tuple-element.62), channel_id=1, source_target_pairs={{8,0},{16,8},{24,16},{9,1},{17,9},{25,17},{10,2},{18,10},{26,18},{... | collective-permute-start | bytes 2359304 | tf_op jit(solution)/shard_map/ppermute | solution.py:411
  11.4 0.0 collective-permute-done.1.refs_0_
  11.4 3.4 %gram.6 = (f32[512,256]{1,0:T(8,128)S(1)}, f32[512,256]{1,0:T(8,128)S(1)}) custom-call(bf16[1024,768]{1,0:T(8,128)(2,1)S(1)} %get-tuple-element.44.high_t, bf16[1024,768]{1,0:T(8,128)(2,1)S(1)} %get-tuple-element.45.low_t, f32[768,256]{1,0:T(8,128)S(1)} %collective-permute-done.1.refs_0_, f32[272,512]{1,0:T(8,128)S(1)} %get-tuple-element.47.refs_1_.keep), custom_call_target="tpu_custom_call" | custom-call | flops 10000000 | bytes 1 | tf_op jit(solution)/shard_map/gram/pallas_call | solution.py:138
  14.8 0.1 collective-permute-start.5
  14.9 1.3 %collective-permute-start.7 = (f32[768,256]{1,0:T(8,128)S(1)}, f32[768,256]{1,0:T(8,128)S(1)}, u32[]{:S(2)}, u32[]{:S(2)}) collective-permute-start(f32[768,256]{1,0:T(8,128)S(1)} %get-tuple-element.59), channel_id=1, source_target_pairs={{8,0},{16,8},{24,16},{9,1},{17,9},{25,17},{10,2},{18,10},{26,18},{... | collective-permute-start | bytes 2359304 | tf_op jit(solution)/shard_map/ppermute | solution.py:411
  16.2 6.3 %collective-permute-done.got = f32[272,512]{1,0:T(8,128)S(1)} collective-permute-done((f32[272,512]{1,0:T(8,128)S(1)}, f32[272,512]{1,0:T(8,128)S(1)}, u32[]{:S(2)}, u32[]{:S(2)}) %collective-permute-start) | collective-permute-done | bytes 557088 | tf_op jit(solution)/shard_map/ppermute | solution.py:391
  22.5 0.1 add.10
  22.6 2.5 %collective-permute-start.2 = (f32[144,512]{1,0:T(8,128)S(1)}, f32[144,512]{1,0:T(8,128)S(1)}, u32[]{:S(2)}, u32[]{:S(2)}) collective-permute-start(f32[144,512]{1,0:T(8,128)S(1)} %get-tuple-element.52), channel_id=1, source_target_pairs={{0,2},{1,3},{2,0},{3,1},{4,6},{5,7},{6,4},{7,5},{8,10},{9,11},{10,... | collective-permute-start | bytes 884744 | tf_op jit(solution)/shard_map/ppermute | solution.py:391
  25.1 0.0 collective-permute-done.3.refs_0_
  25.1 3.1 %gram.7 = (f32[512,256]{1,0:T(8,128)S(1)}, f32[512,256]{1,0:T(8,128)S(1)}) custom-call(bf16[1024,768]{1,0:T(8,128)(2,1)S(1)} %get-tuple-element.44.high_t, bf16[1024,768]{1,0:T(8,128)(2,1)S(1)} %get-tuple-element.45.low_t, f32[768,256]{1,0:T(8,128)S(1)} %collective-permute-done.3.refs_0_, f32[144,512]{1,0:T(8,128)S(1)} %get-tuple-element.51.refs_1_.keep), custom_call_target="tpu_custom_call" | custom-call | flops 10000000 | bytes 1 | tf_op jit(solution)/shard_map/gram/pallas_call | solution.py:138
  28.2 1.5 %collective-permute-start.9 = (f32[512,256]{1,0:T(8,128)S(1)}, f32[512,256]{1,0:T(8,128)S(1)}, u32[]{:S(2)}, u32[]{:S(2)}) collective-permute-start(f32[512,256]{1,0:T(8,128)S(1)} %get-tuple-element.61), channel_id=1, source_target_pairs={{0,1},{1,0},{2,3},{3,2},{4,5},{5,4},{6,7},{7,6},{8,9},{9,8},{10,11... | collective-permute-start | bytes 1572872 | tf_op jit(solution)/shard_map/ppermute | solution.py:391
  29.7 2.3 %collective-permute-done.2.got = f32[144,512]{1,0:T(8,128)S(1)} collective-permute-done((f32[144,512]{1,0:T(8,128)S(1)}, f32[144,512]{1,0:T(8,128)S(1)}, u32[]{:S(2)}, u32[]{:S(2)}) %collective-permute-start.2) | collective-permute-done | bytes 294944 | tf_op jit(solution)/shard_map/ppermute | solution.py:391
  32.0 3.4 %collective-permute-start.4 = (f32[32,512]{1,0:T(8,128)S(1)}, f32[32,512]{1,0:T(8,128)S(1)}, u32[]{:S(2)}, u32[]{:S(2)}) collective-permute-start(f32[32,512]{1,0:T(8,128)S(1)} %get-tuple-element.55.one), channel_id=1, source_target_pairs={{0,4},{1,5},{2,6},{3,7},{4,0},{5,1},{6,2},{7,3},{8,12},{9,13},{10,... | collective-permute-start | bytes 196616 | tf_op jit(solution)/shard_map/ppermute | solution.py:391
  35.5 0.0 collective-permute-done.5.got
  35.5 0.1 add.11
  35.5 1.7 %collective-permute-start.8 = (f32[256,256]{1,0:T(8,128)S(1)}, f32[256,256]{1,0:T(8,128)S(1)}, u32[]{:S(2)}, u32[]{:S(2)}) collective-permute-start(f32[256,256]{1,0:T(8,128)S(1)} %get-tuple-element.60), channel_id=1, source_target_pairs={{0,2},{1,3},{2,0},{3,1},{4,6},{5,7},{6,4},{7,5},{8,10},{9,11},{10,... | collective-permute-start | bytes 786440 | tf_op jit(solution)/shard_map/ppermute | solution.py:391
  37.2 2.7 %collective-permute-done.4.other = f32[32,512]{1,0:T(8,128)S(1)} collective-permute-done((f32[32,512]{1,0:T(8,128)S(1)}, f32[32,512]{1,0:T(8,128)S(1)}, u32[]{:S(2)}, u32[]{:S(2)}) %collective-permute-start.4) | collective-permute-done | bytes 65568 | tf_op jit(solution)/shard_map/ppermute | solution.py:391
  39.9 0.0 collective-permute-done.10.refs_0_
  39.9 1.9 %gram.8 = (f32[256,256]{1,0:T(8,128)S(1)}, f32[256,256]{1,0:T(8,128)S(1)}) custom-call(bf16[1024,768]{1,0:T(8,128)(2,1)S(1)} %get-tuple-element.44.high_t, bf16[1024,768]{1,0:T(8,128)(2,1)S(1)} %get-tuple-element.45.low_t, f32[768,256]{1,0:T(8,128)S(1)} %collective-permute-done.10.refs_0_, f32[64,512]{1,0:T(8,128)S(1)} %join.1.refs_1_.own), custom_call_target="tpu_custom_call" | custom-call | flops 10000000 | bytes 1 | tf_op jit(solution)/shard_map/gram/pallas_call | solution.py:138
  41.8 1.6 %collective-permute-start.14 = (f32[256,256]{1,0:T(8,128)S(1)}, f32[256,256]{1,0:T(8,128)S(1)}, u32[]{:S(2)}, u32[]{:S(2)}) collective-permute-start(f32[256,256]{1,0:T(8,128)S(1)} %get-tuple-element.70), channel_id=1, source_target_pairs={{0,1},{1,0},{2,3},{3,2},{4,5},{5,4},{6,7},{7,6},{8,9},{9,8},{10,11... | collective-permute-start | bytes 786440 | tf_op jit(solution)/shard_map/ppermute | solution.py:391
  43.4 1.5 %collective-permute-done.9.got = f32[512,256]{1,0:T(8,128)S(1)} collective-permute-done((f32[512,256]{1,0:T(8,128)S(1)}, f32[512,256]{1,0:T(8,128)S(1)}, u32[]{:S(2)}, u32[]{:S(2)}) %collective-permute-start.9) | collective-permute-done | bytes 524320 | tf_op jit(solution)/shard_map/ppermute | solution.py:391
  45.0 0.1 add.12
  45.0 2.5 %collective-permute-start.12 = (f32[256,256]{1,0:T(8,128)S(1)}, f32[256,256]{1,0:T(8,128)S(1)}, u32[]{:S(2)}, u32[]{:S(2)}) collective-permute-start(f32[256,256]{1,0:T(8,128)S(1)} %get-tuple-element.68), channel_id=1, source_target_pairs={{0,2},{1,3},{2,0},{3,1},{4,6},{5,7},{6,4},{7,5},{8,10},{9,11},{10,... | collective-permute-start | bytes 786440 | tf_op jit(solution)/shard_map/ppermute | solution.py:391
  47.5 0.0 collective-permute-done.8.got
  47.6 2.7 %collective-permute-start.13 = (f32[128,256]{1,0:T(8,128)S(1)}, f32[128,256]{1,0:T(8,128)S(1)}, u32[]{:S(2)}, u32[]{:S(2)}) collective-permute-start(f32[128,256]{1,0:T(8,128)S(1)} %get-tuple-element.69), channel_id=1, source_target_pairs={{0,4},{1,5},{2,6},{3,7},{4,0},{5,1},{6,2},{7,3},{8,12},{9,13},{10,... | collective-permute-start | bytes 393224 | tf_op jit(solution)/shard_map/ppermute | solution.py:391
  50.2 0.0 collective-permute-done.7.refs_0_
  50.2 1.6 %gram.9 = (f32[256,256]{1,0:T(8,128)S(1)}, f32[256,256]{1,0:T(8,128)S(1)}) custom-call(bf16[1024,768]{1,0:T(8,128)(2,1)S(1)} %get-tuple-element.44.high_t, bf16[1024,768]{1,0:T(8,128)(2,1)S(1)} %get-tuple-element.45.low_t, f32[768,256]{1,0:T(8,128)S(1)} %collective-permute-done.7.refs_0_, f32[128,256]{1,0:T(8,128)S(1)} %get-tuple-element.65.refs_1_.keep), custom_call_target="tpu_custom_call" | custom-call | flops 10000000 | bytes 1 | tf_op jit(solution)/shard_map/gram/pallas_call | solution.py:138
  51.8 1.5 %collective-permute-start.11 = (f32[256,256]{1,0:T(8,128)S(1)}, f32[256,256]{1,0:T(8,128)S(1)}, u32[]{:S(2)}, u32[]{:S(2)}) collective-permute-start(f32[256,256]{1,0:T(8,128)S(1)} %get-tuple-element.67), channel_id=1, source_target_pairs={{0,1},{1,0},{2,3},{3,2},{4,5},{5,4},{6,7},{7,6},{8,9},{9,8},{10,11... | collective-permute-start | bytes 786440 | tf_op jit(solution)/shard_map/ppermute | solution.py:391
  53.3 1.3 %collective-permute-start.6 = (f32[64,512]{1,0:T(8,128)S(1)}, f32[64,512]{1,0:T(8,128)S(1)}, u32[]{:S(2)}, u32[]{:S(2)}) collective-permute-start(f32[64,512]{1,0:T(8,128)S(1)} %join.1.refs_1_.own), channel_id=1, source_target_pairs={{8,0},{16,8},{24,16},{9,1},{17,9},{25,17},{10,2},{18,10},{26,18},{... | collective-permute-start | bytes 393224 | tf_op jit(solution)/shard_map/ppermute | solution.py:418
  54.6 0.0 collective-permute-done.14.got
  54.7 0.5 collective-permute-start.16
  55.2 1.3 %collective-permute-done.13.got = f32[128,256]{1,0:T(8,128)S(1)} collective-permute-done((f32[128,256]{1,0:T(8,128)S(1)}, f32[128,256]{1,0:T(8,128)S(1)}, u32[]{:S(2)}, u32[]{:S(2)}) %collective-permute-start.13) | collective-permute-done | bytes 131104 | tf_op jit(solution)/shard_map/ppermute | solution.py:391
  56.5 0.1 collective-permute-done.12.got
  56.6 3.3 %collective-permute-start.17 = (f32[128,256]{1,0:T(8,128)S(1)}, f32[128,256]{1,0:T(8,128)S(1)}, u32[]{:S(2)}, u32[]{:S(2)}) collective-permute-start(f32[128,256]{1,0:T(8,128)S(1)} %get-tuple-element.80), channel_id=1, source_target_pairs={{0,4},{1,5},{2,6},{3,7},{4,0},{5,1},{6,2},{7,3},{8,12},{9,13},{10,... | collective-permute-start | bytes 393224 | tf_op jit(solution)/shard_map/ppermute | solution.py:391
  60.0 1.0 %collective-permute-done.11.got = f32[256,256]{1,0:T(8,128)S(1)} collective-permute-done((f32[256,256]{1,0:T(8,128)S(1)}, f32[256,256]{1,0:T(8,128)S(1)}, u32[]{:S(2)}, u32[]{:S(2)}) %collective-permute-start.11) | collective-permute-done | bytes 262176 | tf_op jit(solution)/shard_map/ppermute | solution.py:391
  61.0 0.7 collective-permute-start.15
  61.7 0.0 collective-permute-done.16.got
  61.8 1.4 %collective-permute-start.18 = (f32[128,256]{1,0:T(8,128)S(1)}, f32[128,256]{1,0:T(8,128)S(1)}, u32[]{:S(2)}, u32[]{:S(2)}) collective-permute-start(f32[128,256]{1,0:T(8,128)S(1)} %get-tuple-element.81), channel_id=1, source_target_pairs={{0,4},{1,5},{2,6},{3,7},{4,0},{5,1},{6,2},{7,3},{8,12},{9,13},{10,... | collective-permute-start | bytes 393224 | tf_op jit(solution)/shard_map/ppermute | solution.py:391
  63.2 3.7 %collective-permute-done.15.got = f32[128,256]{1,0:T(8,128)S(1)} collective-permute-done((f32[128,256]{1,0:T(8,128)S(1)}, f32[128,256]{1,0:T(8,128)S(1)}, u32[]{:S(2)}, u32[]{:S(2)}) %collective-permute-start.15) | collective-permute-done | bytes 131104 | tf_op jit(solution)/shard_map/ppermute | solution.py:391
  66.9 3.3 %collective-permute-start.19 = (f32[128,256]{1,0:T(8,128)S(1)}, f32[128,256]{1,0:T(8,128)S(1)}, u32[]{:S(2)}, u32[]{:S(2)}) collective-permute-start(f32[128,256]{1,0:T(8,128)S(1)} %get-tuple-element.82), channel_id=1, source_target_pairs={{0,4},{1,5},{2,6},{3,7},{4,0},{5,1},{6,2},{7,3},{8,12},{9,13},{10,... | collective-permute-start | bytes 393224 | tf_op jit(solution)/shard_map/ppermute | solution.py:391
  70.2 0.0 collective-permute-done.6.ahead
  70.2 1.2 %weigh.1 = (f32[128,1024]{1,0:T(8,128)S(1)}, f32[128,1024]{1,0:T(8,128)S(1)}) custom-call(f32[64,512]{1,0:T(8,128)S(1)} %join.1.refs_1_.own, f32[64,512]{1,0:T(8,128)S(1)} %collective-permute-done.6.ahead, f32[128,256]{1,0:T(8,128)S(1)} %get-tuple-element.77.refs_0_.refs_3_), custom_call_target="tpu_custom_call" | custom-call | flops 10000000 | bytes 1 | tf_op jit(solution)/shard_map/weigh/pallas_call | solution.py:308
  71.4 0.0 collective-permute-done.17.got
  71.4 3.9 %collective-permute-done.18.got = f32[128,256]{1,0:T(8,128)S(1)} collective-permute-done((f32[128,256]{1,0:T(8,128)S(1)}, f32[128,256]{1,0:T(8,128)S(1)}, u32[]{:S(2)}, u32[]{:S(2)}) %collective-permute-start.18) | collective-permute-done | bytes 131104 | tf_op jit(solution)/shard_map/ppermute | solution.py:391
  75.4 2.8 %collective-permute-done.19.refs_4_ = f32[128,256]{1,0:T(8,128)S(1)} collective-permute-done((f32[128,256]{1,0:T(8,128)S(1)}, f32[128,256]{1,0:T(8,128)S(1)}, u32[]{:S(2)}, u32[]{:S(2)}) %collective-permute-start.19) | collective-permute-done | bytes 131104 | tf_op jit(solution)/shard_map/ppermute | solution.py:391
  78.2 1.6 %finish.1 = f32[128,1024]{1,0:T(8,128)} custom-call(f32[128,1024]{1,0:T(8,128)S(1)} %get-tuple-element.78.refs_0_.fix, f32[128,1024]{1,0:T(8,128)S(1)} %get-tuple-element.79.factor, f32[128,256]{1,0:T(8,128)S(1)} %add.15.refs_0_, f32[128,256]{1,0:T(8,128)S(1)} %add.18.refs_0_.refs_1_, f32[128,256]{1,0:T(8,128)S(1)} %add.19.refs_2_, ...), custom_call_target="tpu_custom_call" | custom-call | flops 4000000000 | bytes 1 | tf_op jit(solution)/shard_map/finish/pallas_call | solution.py:347
  (11 shorter events, 0.3 us)
Async XLA Ops:
  2.8 8.6 %collective-permute-start.1 = (f32[768,256]{1,0:T(8,128)S(1)}, f32[768,256]{1,0:T(8,128)S(1)}, u32[]{:S(2)}, u32[]{:S(2)}) collective-permute-start(f32[768,256]{1,0:T(8,128)S(1)} %get-tuple-element.49), channel_id=1, source_target_pairs={{8,0},{16,8},{24,16},{9,1},{17,9},{25,17},{10,2},{18,10},{26,18},{... | collective-permute-start | bytes 2359304 | tf_op jit(solution)/shard_map/ppermute | solution.py:411
  4.1 21.0 %collective-permute-start.3 = (f32[768,256]{1,0:T(8,128)S(1)}, f32[768,256]{1,0:T(8,128)S(1)}, u32[]{:S(2)}, u32[]{:S(2)}) collective-permute-start(f32[768,256]{1,0:T(8,128)S(1)} %get-tuple-element.53), channel_id=1, source_target_pairs={{8,0},{16,8},{24,16},{9,1},{17,9},{25,17},{10,2},{18,10},{26,18},{... | collective-permute-start | bytes 2359304 | tf_op jit(solution)/shard_map/ppermute | solution.py:411
  7.1 15.4 %collective-permute-start = (f32[272,512]{1,0:T(8,128)S(1)}, f32[272,512]{1,0:T(8,128)S(1)}, u32[]{:S(2)}, u32[]{:S(2)}) collective-permute-start(f32[272,512]{1,0:T(8,128)S(1)} %get-tuple-element.48), channel_id=1, source_target_pairs={{0,1},{1,0},{2,3},{3,2},{4,5},{5,4},{6,7},{7,6},{8,9},{9,8},{10,11... | collective-permute-start | bytes 1671176 | tf_op jit(solution)/shard_map/ppermute | solution.py:391
  10.1 29.8 %collective-permute-start.10 = (f32[768,256]{1,0:T(8,128)S(1)}, f32[768,256]{1,0:T(8,128)S(1)}, u32[]{:S(2)}, u32[]{:S(2)}) collective-permute-start(f32[768,256]{1,0:T(8,128)S(1)} %get-tuple-element.62), channel_id=1, source_target_pairs={{8,0},{16,8},{24,16},{9,1},{17,9},{25,17},{10,2},{18,10},{26,18},{... | collective-permute-start | bytes 2359304 | tf_op jit(solution)/shard_map/ppermute | solution.py:411
  14.8 20.6 %collective-permute-start.5 = (f32[512,256]{1,0:T(8,128)S(1)}, f32[512,256]{1,0:T(8,128)S(1)}, u32[]{:S(2)}, u32[]{:S(2)}) collective-permute-start(f32[512,256]{1,0:T(8,128)S(1)} %get-tuple-element.56), channel_id=1, source_target_pairs={{0,1},{1,0},{2,3},{3,2},{4,5},{5,4},{6,7},{7,6},{8,9},{9,8},{10,11... | collective-permute-start | bytes 1572872 | tf_op jit(solution)/shard_map/ppermute | solution.py:391
  14.9 35.3 %collective-permute-start.7 = (f32[768,256]{1,0:T(8,128)S(1)}, f32[768,256]{1,0:T(8,128)S(1)}, u32[]{:S(2)}, u32[]{:S(2)}) collective-permute-start(f32[768,256]{1,0:T(8,128)S(1)} %get-tuple-element.59), channel_id=1, source_target_pairs={{8,0},{16,8},{24,16},{9,1},{17,9},{25,17},{10,2},{18,10},{26,18},{... | collective-permute-start | bytes 2359304 | tf_op jit(solution)/shard_map/ppermute | solution.py:411
  22.6 9.4 %collective-permute-start.2 = (f32[144,512]{1,0:T(8,128)S(1)}, f32[144,512]{1,0:T(8,128)S(1)}, u32[]{:S(2)}, u32[]{:S(2)}) collective-permute-start(f32[144,512]{1,0:T(8,128)S(1)} %get-tuple-element.52), channel_id=1, source_target_pairs={{0,2},{1,3},{2,0},{3,1},{4,6},{5,7},{6,4},{7,5},{8,10},{9,11},{10,... | collective-permute-start | bytes 884744 | tf_op jit(solution)/shard_map/ppermute | solution.py:391
  28.2 16.7 %collective-permute-start.9 = (f32[512,256]{1,0:T(8,128)S(1)}, f32[512,256]{1,0:T(8,128)S(1)}, u32[]{:S(2)}, u32[]{:S(2)}) collective-permute-start(f32[512,256]{1,0:T(8,128)S(1)} %get-tuple-element.61), channel_id=1, source_target_pairs={{0,1},{1,0},{2,3},{3,2},{4,5},{5,4},{6,7},{7,6},{8,9},{9,8},{10,11... | collective-permute-start | bytes 1572872 | tf_op jit(solution)/shard_map/ppermute | solution.py:391
  32.0 7.8 %collective-permute-start.4 = (f32[32,512]{1,0:T(8,128)S(1)}, f32[32,512]{1,0:T(8,128)S(1)}, u32[]{:S(2)}, u32[]{:S(2)}) collective-permute-start(f32[32,512]{1,0:T(8,128)S(1)} %get-tuple-element.55.one), channel_id=1, source_target_pairs={{0,4},{1,5},{2,6},{3,7},{4,0},{5,1},{6,2},{7,3},{8,12},{9,13},{10,... | collective-permute-start | bytes 196616 | tf_op jit(solution)/shard_map/ppermute | solution.py:391
  35.5 12.0 %collective-permute-start.8 = (f32[256,256]{1,0:T(8,128)S(1)}, f32[256,256]{1,0:T(8,128)S(1)}, u32[]{:S(2)}, u32[]{:S(2)}) collective-permute-start(f32[256,256]{1,0:T(8,128)S(1)} %get-tuple-element.60), channel_id=1, source_target_pairs={{0,2},{1,3},{2,0},{3,1},{4,6},{5,7},{6,4},{7,5},{8,10},{9,11},{10,... | collective-permute-start | bytes 786440 | tf_op jit(solution)/shard_map/ppermute | solution.py:391
  41.8 12.8 %collective-permute-start.14 = (f32[256,256]{1,0:T(8,128)S(1)}, f32[256,256]{1,0:T(8,128)S(1)}, u32[]{:S(2)}, u32[]{:S(2)}) collective-permute-start(f32[256,256]{1,0:T(8,128)S(1)} %get-tuple-element.70), channel_id=1, source_target_pairs={{0,1},{1,0},{2,3},{3,2},{4,5},{5,4},{6,7},{7,6},{8,9},{9,8},{10,11... | collective-permute-start | bytes 786440 | tf_op jit(solution)/shard_map/ppermute | solution.py:391
  45.0 11.6 %collective-permute-start.12 = (f32[256,256]{1,0:T(8,128)S(1)}, f32[256,256]{1,0:T(8,128)S(1)}, u32[]{:S(2)}, u32[]{:S(2)}) collective-permute-start(f32[256,256]{1,0:T(8,128)S(1)} %get-tuple-element.68), channel_id=1, source_target_pairs={{0,2},{1,3},{2,0},{3,1},{4,6},{5,7},{6,4},{7,5},{8,10},{9,11},{10,... | collective-permute-start | bytes 786440 | tf_op jit(solution)/shard_map/ppermute | solution.py:391
  47.6 8.9 %collective-permute-start.13 = (f32[128,256]{1,0:T(8,128)S(1)}, f32[128,256]{1,0:T(8,128)S(1)}, u32[]{:S(2)}, u32[]{:S(2)}) collective-permute-start(f32[128,256]{1,0:T(8,128)S(1)} %get-tuple-element.69), channel_id=1, source_target_pairs={{0,4},{1,5},{2,6},{3,7},{4,0},{5,1},{6,2},{7,3},{8,12},{9,13},{10,... | collective-permute-start | bytes 393224 | tf_op jit(solution)/shard_map/ppermute | solution.py:391
  51.8 9.2 %collective-permute-start.11 = (f32[256,256]{1,0:T(8,128)S(1)}, f32[256,256]{1,0:T(8,128)S(1)}, u32[]{:S(2)}, u32[]{:S(2)}) collective-permute-start(f32[256,256]{1,0:T(8,128)S(1)} %get-tuple-element.67), channel_id=1, source_target_pairs={{0,1},{1,0},{2,3},{3,2},{4,5},{5,4},{6,7},{7,6},{8,9},{9,8},{10,11... | collective-permute-start | bytes 786440 | tf_op jit(solution)/shard_map/ppermute | solution.py:391
  53.3 16.9 %collective-permute-start.6 = (f32[64,512]{1,0:T(8,128)S(1)}, f32[64,512]{1,0:T(8,128)S(1)}, u32[]{:S(2)}, u32[]{:S(2)}) collective-permute-start(f32[64,512]{1,0:T(8,128)S(1)} %join.1.refs_1_.own), channel_id=1, source_target_pairs={{8,0},{16,8},{24,16},{9,1},{17,9},{25,17},{10,2},{18,10},{26,18},{... | collective-permute-start | bytes 393224 | tf_op jit(solution)/shard_map/ppermute | solution.py:418
  54.7 7.1 %collective-permute-start.16 = (f32[128,256]{1,0:T(8,128)S(1)}, f32[128,256]{1,0:T(8,128)S(1)}, u32[]{:S(2)}, u32[]{:S(2)}) collective-permute-start(f32[128,256]{1,0:T(8,128)S(1)} %get-tuple-element.75), channel_id=1, source_target_pairs={{0,2},{1,3},{2,0},{3,1},{4,6},{5,7},{6,4},{7,5},{8,10},{9,11},{10,... | collective-permute-start | bytes 393224 | tf_op jit(solution)/shard_map/ppermute | solution.py:391
  56.6 14.8 %collective-permute-start.17 = (f32[128,256]{1,0:T(8,128)S(1)}, f32[128,256]{1,0:T(8,128)S(1)}, u32[]{:S(2)}, u32[]{:S(2)}) collective-permute-start(f32[128,256]{1,0:T(8,128)S(1)} %get-tuple-element.80), channel_id=1, source_target_pairs={{0,4},{1,5},{2,6},{3,7},{4,0},{5,1},{6,2},{7,3},{8,12},{9,13},{10,... | collective-permute-start | bytes 393224 | tf_op jit(solution)/shard_map/ppermute | solution.py:391
  61.0 5.9 %collective-permute-start.15 = (f32[128,256]{1,0:T(8,128)S(1)}, f32[128,256]{1,0:T(8,128)S(1)}, u32[]{:S(2)}, u32[]{:S(2)}) collective-permute-start(f32[128,256]{1,0:T(8,128)S(1)} %get-tuple-element.74), channel_id=1, source_target_pairs={{0,2},{1,3},{2,0},{3,1},{4,6},{5,7},{6,4},{7,5},{8,10},{9,11},{10,... | collective-permute-start | bytes 393224 | tf_op jit(solution)/shard_map/ppermute | solution.py:391
  61.8 13.6 %collective-permute-start.18 = (f32[128,256]{1,0:T(8,128)S(1)}, f32[128,256]{1,0:T(8,128)S(1)}, u32[]{:S(2)}, u32[]{:S(2)}) collective-permute-start(f32[128,256]{1,0:T(8,128)S(1)} %get-tuple-element.81), channel_id=1, source_target_pairs={{0,4},{1,5},{2,6},{3,7},{4,0},{5,1},{6,2},{7,3},{8,12},{9,13},{10,... | collective-permute-start | bytes 393224 | tf_op jit(solution)/shard_map/ppermute | solution.py:391
  66.9 11.2 %collective-permute-start.19 = (f32[128,256]{1,0:T(8,128)S(1)}, f32[128,256]{1,0:T(8,128)S(1)}, u32[]{:S(2)}, u32[]{:S(2)}) collective-permute-start(f32[128,256]{1,0:T(8,128)S(1)} %get-tuple-element.82), channel_id=1, source_target_pairs={{0,4},{1,5},{2,6},{3,7},{4,0},{5,1},{6,2},{7,3},{8,12},{9,13},{10,... | collective-permute-start | bytes 393224 | tf_op jit(solution)/shard_map/ppermute | solution.py:391

commit v6 on v5

--- a/solution.py
+++ b/solution.py
@@ -359,24 +359,24 @@
 PLAN = (
     (0, 0, 0.01),
     (1, 0, 0.01),
-    (0, 1, 0.01),
+    (0, 1, 3.2),
     (2, 0, 0.01),
     (0, 2, 0.01),
     (1, 1, 0.01),
-    (5, 0, 1.8),
     (3, 0, 0.01),
     (2, 1, 0.01),
     (1, 2, 0.01),
+    (5, 0, 1.8),
     (4, 0, 0.01),
     (3, 1, 0.01),
     (1, 3, 0.6),
     (2, 2, 1.66),
-    (4, 1, 0.01),
+    (4, 1, 2.5),
     (3, 2, 2.5),
     (4, 2, 0.01),
     (5, 1, 0.01),
     (2, 3, 1.6),
-    (3, 3, 0.08),
+    (3, 3, 2.5),
 )
 
 

time: 80.2 us -> 77.5 us (0.966)
  starting transfers between devices: 36.2 us -> 32.9 us
    ppermute x15, starting transfers between devices: 29.8 us -> 26.5 us  [swap(): lax.ppermute(array, 'samp', [(i, i ^ 1 << bit) for i in range(parts)])]
  transfers between devices with their start and end apart: 20 -> 20, of which waited for: 10 -> 8; matrix products, arithmetic and copies ran while one was open for 0% -> 0% of each run, Pallas kernels for 17% -> 17%
where the time goes in v6:
time: 77.5 us; the launch traced here: 77.3 us
  starting transfers between devices  32.9 us (42%)
  waiting for transfers between devices  26.4 us (34%)
  Pallas kernels  17.7 us (23%)
    ppermute x15, starting transfers between devices, swap(): lax.ppermute(array, 'samp', [(i, i ^ 1 << bit) for i in range(parts)])  26.5 us
    ppermute x15, waiting for transfers between devices, swap(): lax.ppermute(array, 'samp', [(i, i ^ 1 << bit) for i in range(parts)])  26.4 us
    pallas_call x5, Pallas kernels, gram(): pl.pallas_call(functools.partial(gram_kernel, piece, spots, order, len(ah...  11.7 us
    ppermute x4, starting transfers between devices, local(): come = [[]] + [[lax.ppermute(cut, 'var', route)] for cut in cuts]  5.16 us
    pallas_call x1, Pallas kernels, prepare(): pl.pallas_call(prepare_kernel, in_specs=[pl.BlockSpec(memory_space=pltpu....  2.79 us
    pallas_call x1, Pallas kernels, finish(): pl.pallas_call(functools.partial(finish_kernel, starts, sizes), in_specs=...  1.57 us
  transfers between devices with their start and end apart: 20, of which 8 were waited for; matrix products, arithmetic and copies ran while one was open for 0% of the time, Pallas kernels for 17%

profile of v6, /device:TPU:0, one launch (start us, length us, event | category | flops | bytes accessed | tf_op | source)
XLA Modules:
  0.0 77.3 jit_solution(11069939555903366161)
XLA Ops:
  0.0 2.8 %prepare.1 = (bf16[1024,768]{1,0:T(8,128)(2,1)S(1)}, bf16[1024,768]{1,0:T(8,128)(2,1)S(1)}, f32[16,512]{1,0:T(8,128)S(1)}, f32[768,256]{1,0:T(8,128)S(1)}, f32[7...) custom-call(f32[768,1024]{1,0:T(8,128)} %dosages.1), custom_call_target="tpu_custom_call" | custom-call | flops 4000000000 | bytes 1 | tf_op jit(solution)/shard_map/prepare/pallas_call | solution.py:65
  2.8 1.3 %collective-permute-start.1 = (f32[768,256]{1,0:T(8,128)S(1)}, f32[768,256]{1,0:T(8,128)S(1)}, u32[]{:S(2)}, u32[]{:S(2)}) collective-permute-start(f32[768,256]{1,0:T(8,128)S(1)} %get-tuple-element.49), channel_id=1, source_target_pairs={{8,0},{16,8},{24,16},{9,1},{17,9},{25,17},{10,2},{18,10},{26,18},{... | collective-permute-start | bytes 2359304 | tf_op jit(solution)/shard_map/ppermute | solution.py:411
  4.1 1.7 %gram.5 = (f32[272,512]{1,0:T(8,128)S(1)}, f32[272,512]{1,0:T(8,128)S(1)}) custom-call(bf16[1024,768]{1,0:T(8,128)(2,1)S(1)} %get-tuple-element.44.high_t, bf16[1024,768]{1,0:T(8,128)(2,1)S(1)} %get-tuple-element.45.low_t, f32[16,512]{1,0:T(8,128)S(1)} %get-tuple-element.46.refs_0_.refs_1_, f32[16,512]{1,0:T(8,128)S(1)} %get-tuple-element.46.refs_0_.refs_1_), custom_call_target="tpu_custom_call" | custom-call | flops 10000000 | bytes 1 | tf_op jit(solution)/shard_map/gram/pallas_call | solution.py:138
  5.8 3.0 %collective-permute-start = (f32[272,512]{1,0:T(8,128)S(1)}, f32[272,512]{1,0:T(8,128)S(1)}, u32[]{:S(2)}, u32[]{:S(2)}) collective-permute-start(f32[272,512]{1,0:T(8,128)S(1)} %get-tuple-element.48), channel_id=1, source_target_pairs={{0,1},{1,0},{2,3},{3,2},{4,5},{5,4},{6,7},{7,6},{8,9},{9,8},{10,11... | collective-permute-start | bytes 1671176 | tf_op jit(solution)/shard_map/ppermute | solution.py:391
  8.8 1.3 %collective-permute-start.3 = (f32[768,256]{1,0:T(8,128)S(1)}, f32[768,256]{1,0:T(8,128)S(1)}, u32[]{:S(2)}, u32[]{:S(2)}) collective-permute-start(f32[768,256]{1,0:T(8,128)S(1)} %get-tuple-element.53), channel_id=1, source_target_pairs={{8,0},{16,8},{24,16},{9,1},{17,9},{25,17},{10,2},{18,10},{26,18},{... | collective-permute-start | bytes 2359304 | tf_op jit(solution)/shard_map/ppermute | solution.py:411
  10.1 1.3 %collective-permute-start.8 = (f32[768,256]{1,0:T(8,128)S(1)}, f32[768,256]{1,0:T(8,128)S(1)}, u32[]{:S(2)}, u32[]{:S(2)}) collective-permute-start(f32[768,256]{1,0:T(8,128)S(1)} %get-tuple-element.61), channel_id=1, source_target_pairs={{8,0},{16,8},{24,16},{9,1},{17,9},{25,17},{10,2},{18,10},{26,18},{... | collective-permute-start | bytes 2359304 | tf_op jit(solution)/shard_map/ppermute | solution.py:411
  11.4 1.3 %collective-permute-start.10 = (f32[768,256]{1,0:T(8,128)S(1)}, f32[768,256]{1,0:T(8,128)S(1)}, u32[]{:S(2)}, u32[]{:S(2)}) collective-permute-start(f32[768,256]{1,0:T(8,128)S(1)} %get-tuple-element.65), channel_id=1, source_target_pairs={{8,0},{16,8},{24,16},{9,1},{17,9},{25,17},{10,2},{18,10},{26,18},{... | collective-permute-start | bytes 2359304 | tf_op jit(solution)/shard_map/ppermute | solution.py:411
  12.7 0.0 collective-permute-done.1.refs_0_
  12.7 3.4 %gram.6 = (f32[512,256]{1,0:T(8,128)S(1)}, f32[512,256]{1,0:T(8,128)S(1)}) custom-call(bf16[1024,768]{1,0:T(8,128)(2,1)S(1)} %get-tuple-element.44.high_t, bf16[1024,768]{1,0:T(8,128)(2,1)S(1)} %get-tuple-element.45.low_t, f32[768,256]{1,0:T(8,128)S(1)} %collective-permute-done.1.refs_0_, f32[272,512]{1,0:T(8,128)S(1)} %get-tuple-element.47.refs_1_.keep), custom_call_target="tpu_custom_call" | custom-call | flops 10000000 | bytes 1 | tf_op jit(solution)/shard_map/gram/pallas_call | solution.py:138
  16.1 0.1 collective-permute-start.5
  16.2 5.7 %collective-permute-done.got = f32[272,512]{1,0:T(8,128)S(1)} collective-permute-done((f32[272,512]{1,0:T(8,128)S(1)}, f32[272,512]{1,0:T(8,128)S(1)}, u32[]{:S(2)}, u32[]{:S(2)}) %collective-permute-start) | collective-permute-done | bytes 557088 | tf_op jit(solution)/shard_map/ppermute | solution.py:391
  21.9 0.1 add.10
  22.0 2.4 %collective-permute-start.2 = (f32[144,512]{1,0:T(8,128)S(1)}, f32[144,512]{1,0:T(8,128)S(1)}, u32[]{:S(2)}, u32[]{:S(2)}) collective-permute-start(f32[144,512]{1,0:T(8,128)S(1)} %get-tuple-element.52), channel_id=1, source_target_pairs={{0,2},{1,3},{2,0},{3,1},{4,6},{5,7},{6,4},{7,5},{8,10},{9,11},{10,... | collective-permute-start | bytes 884744 | tf_op jit(solution)/shard_map/ppermute | solution.py:391
  24.4 0.0 collective-permute-done.3.refs_0_
  24.4 3.1 %gram.7 = (f32[512,256]{1,0:T(8,128)S(1)}, f32[512,256]{1,0:T(8,128)S(1)}) custom-call(bf16[1024,768]{1,0:T(8,128)(2,1)S(1)} %get-tuple-element.44.high_t, bf16[1024,768]{1,0:T(8,128)(2,1)S(1)} %get-tuple-element.45.low_t, f32[768,256]{1,0:T(8,128)S(1)} %collective-permute-done.3.refs_0_, f32[144,512]{1,0:T(8,128)S(1)} %get-tuple-element.51.refs_1_.keep), custom_call_target="tpu_custom_call" | custom-call | flops 10000000 | bytes 1 | tf_op jit(solution)/shard_map/gram/pallas_call | solution.py:138
  27.5 1.5 %collective-permute-start.7 = (f32[512,256]{1,0:T(8,128)S(1)}, f32[512,256]{1,0:T(8,128)S(1)}, u32[]{:S(2)}, u32[]{:S(2)}) collective-permute-start(f32[512,256]{1,0:T(8,128)S(1)} %get-tuple-element.60), channel_id=1, source_target_pairs={{0,1},{1,0},{2,3},{3,2},{4,5},{5,4},{6,7},{7,6},{8,9},{9,8},{10,11... | collective-permute-start | bytes 1572872 | tf_op jit(solution)/shard_map/ppermute | solution.py:391
  29.0 3.0 %collective-permute-done.2.got = f32[144,512]{1,0:T(8,128)S(1)} collective-permute-done((f32[144,512]{1,0:T(8,128)S(1)}, f32[144,512]{1,0:T(8,128)S(1)}, u32[]{:S(2)}, u32[]{:S(2)}) %collective-permute-start.2) | collective-permute-done | bytes 294944 | tf_op jit(solution)/shard_map/ppermute | solution.py:391
  32.0 0.0 collective-permute-done.5.got
  32.0 0.1 add.11
  32.1 2.6 %collective-permute-start.6 = (f32[256,256]{1,0:T(8,128)S(1)}, f32[256,256]{1,0:T(8,128)S(1)}, u32[]{:S(2)}, u32[]{:S(2)}) collective-permute-start(f32[256,256]{1,0:T(8,128)S(1)} %get-tuple-element.59), channel_id=1, source_target_pairs={{0,2},{1,3},{2,0},{3,1},{4,6},{5,7},{6,4},{7,5},{8,10},{9,11},{10,... | collective-permute-start | bytes 786440 | tf_op jit(solution)/shard_map/ppermute | solution.py:391
  34.7 2.6 %collective-permute-start.4 = (f32[32,512]{1,0:T(8,128)S(1)}, f32[32,512]{1,0:T(8,128)S(1)}, u32[]{:S(2)}, u32[]{:S(2)}) collective-permute-start(f32[32,512]{1,0:T(8,128)S(1)} %get-tuple-element.55.one), channel_id=1, source_target_pairs={{0,4},{1,5},{2,6},{3,7},{4,0},{5,1},{6,2},{7,3},{8,12},{9,13},{10,... | collective-permute-start | bytes 196616 | tf_op jit(solution)/shard_map/ppermute | solution.py:391
  37.3 0.0 collective-permute-done.8.refs_0_
  37.3 1.9 %gram.8 = (f32[256,256]{1,0:T(8,128)S(1)}, f32[256,256]{1,0:T(8,128)S(1)}) custom-call(bf16[1024,768]{1,0:T(8,128)(2,1)S(1)} %get-tuple-element.44.high_t, bf16[1024,768]{1,0:T(8,128)(2,1)S(1)} %get-tuple-element.45.low_t, f32[768,256]{1,0:T(8,128)S(1)} %collective-permute-done.8.refs_0_, f32[256,256]{1,0:T(8,128)S(1)} %get-tuple-element.58.refs_1_.keep), custom_call_target="tpu_custom_call" | custom-call | flops 10000000 | bytes 1 | tf_op jit(solution)/shard_map/gram/pallas_call | solution.py:138
  39.2 1.5 %collective-permute-start.14 = (f32[256,256]{1,0:T(8,128)S(1)}, f32[256,256]{1,0:T(8,128)S(1)}, u32[]{:S(2)}, u32[]{:S(2)}) collective-permute-start(f32[256,256]{1,0:T(8,128)S(1)} %get-tuple-element.70), channel_id=1, source_target_pairs={{0,1},{1,0},{2,3},{3,2},{4,5},{5,4},{6,7},{7,6},{8,9},{9,8},{10,11... | collective-permute-start | bytes 786440 | tf_op jit(solution)/shard_map/ppermute | solution.py:391
  40.7 2.5 %collective-permute-done.7.got = f32[512,256]{1,0:T(8,128)S(1)} collective-permute-done((f32[512,256]{1,0:T(8,128)S(1)}, f32[512,256]{1,0:T(8,128)S(1)}, u32[]{:S(2)}, u32[]{:S(2)}) %collective-permute-start.7) | collective-permute-done | bytes 524320 | tf_op jit(solution)/shard_map/ppermute | solution.py:391
  43.2 0.1 add.12
  43.3 2.6 %collective-permute-start.12 = (f32[256,256]{1,0:T(8,128)S(1)}, f32[256,256]{1,0:T(8,128)S(1)}, u32[]{:S(2)}, u32[]{:S(2)}) collective-permute-start(f32[256,256]{1,0:T(8,128)S(1)} %get-tuple-element.68), channel_id=1, source_target_pairs={{0,2},{1,3},{2,0},{3,1},{4,6},{5,7},{6,4},{7,5},{8,10},{9,11},{10,... | collective-permute-start | bytes 786440 | tf_op jit(solution)/shard_map/ppermute | solution.py:391
  45.9 0.0 collective-permute-done.6.got
  45.9 2.7 %collective-permute-start.13 = (f32[128,256]{1,0:T(8,128)S(1)}, f32[128,256]{1,0:T(8,128)S(1)}, u32[]{:S(2)}, u32[]{:S(2)}) collective-permute-start(f32[128,256]{1,0:T(8,128)S(1)} %get-tuple-element.69), channel_id=1, source_target_pairs={{0,4},{1,5},{2,6},{3,7},{4,0},{5,1},{6,2},{7,3},{8,12},{9,13},{10,... | collective-permute-start | bytes 393224 | tf_op jit(solution)/shard_map/ppermute | solution.py:391
  48.6 0.0 collective-permute-done.4.other
  48.6 0.0 collective-permute-done.10.refs_0_
  48.6 1.6 %gram.9 = (f32[256,256]{1,0:T(8,128)S(1)}, f32[256,256]{1,0:T(8,128)S(1)}) custom-call(bf16[1024,768]{1,0:T(8,128)(2,1)S(1)} %get-tuple-element.44.high_t, bf16[1024,768]{1,0:T(8,128)(2,1)S(1)} %get-tuple-element.45.low_t, f32[768,256]{1,0:T(8,128)S(1)} %collective-permute-done.10.refs_0_, f32[64,512]{1,0:T(8,128)S(1)} %join.1.refs_1_.own), custom_call_target="tpu_custom_call" | custom-call | flops 10000000 | bytes 1 | tf_op jit(solution)/shard_map/gram/pallas_call | solution.py:138
  50.2 1.5 %collective-permute-start.11 = (f32[256,256]{1,0:T(8,128)S(1)}, f32[256,256]{1,0:T(8,128)S(1)}, u32[]{:S(2)}, u32[]{:S(2)}) collective-permute-start(f32[256,256]{1,0:T(8,128)S(1)} %get-tuple-element.67), channel_id=1, source_target_pairs={{0,1},{1,0},{2,3},{3,2},{4,5},{5,4},{6,7},{7,6},{8,9},{9,8},{10,11... | collective-permute-start | bytes 786440 | tf_op jit(solution)/shard_map/ppermute | solution.py:391
  51.7 1.3 %collective-permute-start.9 = (f32[64,512]{1,0:T(8,128)S(1)}, f32[64,512]{1,0:T(8,128)S(1)}, u32[]{:S(2)}, u32[]{:S(2)}) collective-permute-start(f32[64,512]{1,0:T(8,128)S(1)} %join.1.refs_1_.own), channel_id=1, source_target_pairs={{8,0},{16,8},{24,16},{9,1},{17,9},{25,17},{10,2},{18,10},{26,18},{... | collective-permute-start | bytes 393224 | tf_op jit(solution)/shard_map/ppermute | solution.py:418
  53.0 0.0 collective-permute-done.14.got
  53.1 0.5 collective-permute-start.16
  53.6 0.5 collective-permute-done.13.got
  54.1 0.0 collective-permute-done.12.got
  54.1 3.4 %collective-permute-start.17 = (f32[128,256]{1,0:T(8,128)S(1)}, f32[128,256]{1,0:T(8,128)S(1)}, u32[]{:S(2)}, u32[]{:S(2)}) collective-permute-start(f32[128,256]{1,0:T(8,128)S(1)} %get-tuple-element.80), channel_id=1, source_target_pairs={{0,4},{1,5},{2,6},{3,7},{4,0},{5,1},{6,2},{7,3},{8,12},{9,13},{10,... | collective-permute-start | bytes 393224 | tf_op jit(solution)/shard_map/ppermute | solution.py:391
  57.6 1.2 %collective-permute-done.11.got = f32[256,256]{1,0:T(8,128)S(1)} collective-permute-done((f32[256,256]{1,0:T(8,128)S(1)}, f32[256,256]{1,0:T(8,128)S(1)}, u32[]{:S(2)}, u32[]{:S(2)}) %collective-permute-start.11) | collective-permute-done | bytes 262176 | tf_op jit(solution)/shard_map/ppermute | solution.py:391
  58.7 0.6 collective-permute-start.15
  59.3 0.0 collective-permute-done.16.got
  59.4 1.4 %collective-permute-start.18 = (f32[128,256]{1,0:T(8,128)S(1)}, f32[128,256]{1,0:T(8,128)S(1)}, u32[]{:S(2)}, u32[]{:S(2)}) collective-permute-start(f32[128,256]{1,0:T(8,128)S(1)} %get-tuple-element.81), channel_id=1, source_target_pairs={{0,4},{1,5},{2,6},{3,7},{4,0},{5,1},{6,2},{7,3},{8,12},{9,13},{10,... | collective-permute-start | bytes 393224 | tf_op jit(solution)/shard_map/ppermute | solution.py:391
  60.8 5.7 %collective-permute-done.15.got = f32[128,256]{1,0:T(8,128)S(1)} collective-permute-done((f32[128,256]{1,0:T(8,128)S(1)}, f32[128,256]{1,0:T(8,128)S(1)}, u32[]{:S(2)}, u32[]{:S(2)}) %collective-permute-start.15) | collective-permute-done | bytes 131104 | tf_op jit(solution)/shard_map/ppermute | solution.py:391
  66.5 0.1 collective-permute-start.19
  66.6 0.0 collective-permute-done.9.ahead
  66.6 1.2 %weigh.1 = (f32[128,1024]{1,0:T(8,128)S(1)}, f32[128,1024]{1,0:T(8,128)S(1)}) custom-call(f32[64,512]{1,0:T(8,128)S(1)} %join.1.refs_1_.own, f32[64,512]{1,0:T(8,128)S(1)} %collective-permute-done.9.ahead, f32[128,256]{1,0:T(8,128)S(1)} %get-tuple-element.77.refs_0_.refs_3_), custom_call_target="tpu_custom_call" | custom-call | flops 10000000 | bytes 1 | tf_op jit(solution)/shard_map/weigh/pallas_call | solution.py:308
  67.8 0.0 collective-permute-done.17.got
  67.8 5.1 %collective-permute-done.18.got = f32[128,256]{1,0:T(8,128)S(1)} collective-permute-done((f32[128,256]{1,0:T(8,128)S(1)}, f32[128,256]{1,0:T(8,128)S(1)}, u32[]{:S(2)}, u32[]{:S(2)}) %collective-permute-start.18) | collective-permute-done | bytes 131104 | tf_op jit(solution)/shard_map/ppermute | solution.py:391
  72.9 2.8 %collective-permute-done.19.refs_4_ = f32[128,256]{1,0:T(8,128)S(1)} collective-permute-done((f32[128,256]{1,0:T(8,128)S(1)}, f32[128,256]{1,0:T(8,128)S(1)}, u32[]{:S(2)}, u32[]{:S(2)}) %collective-permute-start.19) | collective-permute-done | bytes 131104 | tf_op jit(solution)/shard_map/ppermute | solution.py:391
  75.7 1.6 %finish.1 = f32[128,1024]{1,0:T(8,128)} custom-call(f32[128,1024]{1,0:T(8,128)S(1)} %get-tuple-element.78.refs_0_.fix, f32[128,1024]{1,0:T(8,128)S(1)} %get-tuple-element.79.factor, f32[128,256]{1,0:T(8,128)S(1)} %add.15.refs_0_, f32[128,256]{1,0:T(8,128)S(1)} %add.18.refs_0_.refs_1_, f32[128,256]{1,0:T(8,128)S(1)} %add.19.refs_2_, ...), custom_call_target="tpu_custom_call" | custom-call | flops 4000000000 | bytes 1 | tf_op jit(solution)/shard_map/finish/pallas_call | solution.py:347
  (11 shorter events, 0.3 us)
Async XLA Ops:
  2.8 9.9 %collective-permute-start.1 = (f32[768,256]{1,0:T(8,128)S(1)}, f32[768,256]{1,0:T(8,128)S(1)}, u32[]{:S(2)}, u32[]{:S(2)}) collective-permute-start(f32[768,256]{1,0:T(8,128)S(1)} %get-tuple-element.49), channel_id=1, source_target_pairs={{8,0},{16,8},{24,16},{9,1},{17,9},{25,17},{10,2},{18,10},{26,18},{... | collective-permute-start | bytes 2359304 | tf_op jit(solution)/shard_map/ppermute | solution.py:411
  5.8 16.1 %collective-permute-start = (f32[272,512]{1,0:T(8,128)S(1)}, f32[272,512]{1,0:T(8,128)S(1)}, u32[]{:S(2)}, u32[]{:S(2)}) collective-permute-start(f32[272,512]{1,0:T(8,128)S(1)} %get-tuple-element.48), channel_id=1, source_target_pairs={{0,1},{1,0},{2,3},{3,2},{4,5},{5,4},{6,7},{7,6},{8,9},{9,8},{10,11... | collective-permute-start | bytes 1671176 | tf_op jit(solution)/shard_map/ppermute | solution.py:391
  8.8 15.6 %collective-permute-start.3 = (f32[768,256]{1,0:T(8,128)S(1)}, f32[768,256]{1,0:T(8,128)S(1)}, u32[]{:S(2)}, u32[]{:S(2)}) collective-permute-start(f32[768,256]{1,0:T(8,128)S(1)} %get-tuple-element.53), channel_id=1, source_target_pairs={{8,0},{16,8},{24,16},{9,1},{17,9},{25,17},{10,2},{18,10},{26,18},{... | collective-permute-start | bytes 2359304 | tf_op jit(solution)/shard_map/ppermute | solution.py:411
  10.1 27.2 %collective-permute-start.8 = (f32[768,256]{1,0:T(8,128)S(1)}, f32[768,256]{1,0:T(8,128)S(1)}, u32[]{:S(2)}, u32[]{:S(2)}) collective-permute-start(f32[768,256]{1,0:T(8,128)S(1)} %get-tuple-element.61), channel_id=1, source_target_pairs={{8,0},{16,8},{24,16},{9,1},{17,9},{25,17},{10,2},{18,10},{26,18},{... | collective-permute-start | bytes 2359304 | tf_op jit(solution)/shard_map/ppermute | solution.py:411
  11.4 37.2 %collective-permute-start.10 = (f32[768,256]{1,0:T(8,128)S(1)}, f32[768,256]{1,0:T(8,128)S(1)}, u32[]{:S(2)}, u32[]{:S(2)}) collective-permute-start(f32[768,256]{1,0:T(8,128)S(1)} %get-tuple-element.65), channel_id=1, source_target_pairs={{8,0},{16,8},{24,16},{9,1},{17,9},{25,17},{10,2},{18,10},{26,18},{... | collective-permute-start | bytes 2359304 | tf_op jit(solution)/shard_map/ppermute | solution.py:411
  16.1 15.9 %collective-permute-start.5 = (f32[512,256]{1,0:T(8,128)S(1)}, f32[512,256]{1,0:T(8,128)S(1)}, u32[]{:S(2)}, u32[]{:S(2)}) collective-permute-start(f32[512,256]{1,0:T(8,128)S(1)} %get-tuple-element.56), channel_id=1, source_target_pairs={{0,1},{1,0},{2,3},{3,2},{4,5},{5,4},{6,7},{7,6},{8,9},{9,8},{10,11... | collective-permute-start | bytes 1572872 | tf_op jit(solution)/shard_map/ppermute | solution.py:391
  22.0 10.0 %collective-permute-start.2 = (f32[144,512]{1,0:T(8,128)S(1)}, f32[144,512]{1,0:T(8,128)S(1)}, u32[]{:S(2)}, u32[]{:S(2)}) collective-permute-start(f32[144,512]{1,0:T(8,128)S(1)} %get-tuple-element.52), channel_id=1, source_target_pairs={{0,2},{1,3},{2,0},{3,1},{4,6},{5,7},{6,4},{7,5},{8,10},{9,11},{10,... | collective-permute-start | bytes 884744 | tf_op jit(solution)/shard_map/ppermute | solution.py:391
  27.5 15.7 %collective-permute-start.7 = (f32[512,256]{1,0:T(8,128)S(1)}, f32[512,256]{1,0:T(8,128)S(1)}, u32[]{:S(2)}, u32[]{:S(2)}) collective-permute-start(f32[512,256]{1,0:T(8,128)S(1)} %get-tuple-element.60), channel_id=1, source_target_pairs={{0,1},{1,0},{2,3},{3,2},{4,5},{5,4},{6,7},{7,6},{8,9},{9,8},{10,11... | collective-permute-start | bytes 1572872 | tf_op jit(solution)/shard_map/ppermute | solution.py:391
  32.1 13.8 %collective-permute-start.6 = (f32[256,256]{1,0:T(8,128)S(1)}, f32[256,256]{1,0:T(8,128)S(1)}, u32[]{:S(2)}, u32[]{:S(2)}) collective-permute-start(f32[256,256]{1,0:T(8,128)S(1)} %get-tuple-element.59), channel_id=1, source_target_pairs={{0,2},{1,3},{2,0},{3,1},{4,6},{5,7},{6,4},{7,5},{8,10},{9,11},{10,... | collective-permute-start | bytes 786440 | tf_op jit(solution)/shard_map/ppermute | solution.py:391
  34.7 13.9 %collective-permute-start.4 = (f32[32,512]{1,0:T(8,128)S(1)}, f32[32,512]{1,0:T(8,128)S(1)}, u32[]{:S(2)}, u32[]{:S(2)}) collective-permute-start(f32[32,512]{1,0:T(8,128)S(1)} %get-tuple-element.55.one), channel_id=1, source_target_pairs={{0,4},{1,5},{2,6},{3,7},{4,0},{5,1},{6,2},{7,3},{8,12},{9,13},{10,... | collective-permute-start | bytes 196616 | tf_op jit(solution)/shard_map/ppermute | solution.py:391
  39.2 13.8 %collective-permute-start.14 = (f32[256,256]{1,0:T(8,128)S(1)}, f32[256,256]{1,0:T(8,128)S(1)}, u32[]{:S(2)}, u32[]{:S(2)}) collective-permute-start(f32[256,256]{1,0:T(8,128)S(1)} %get-tuple-element.70), channel_id=1, source_target_pairs={{0,1},{1,0},{2,3},{3,2},{4,5},{5,4},{6,7},{7,6},{8,9},{9,8},{10,11... | collective-permute-start | bytes 786440 | tf_op jit(solution)/shard_map/ppermute | solution.py:391
  43.3 10.8 %collective-permute-start.12 = (f32[256,256]{1,0:T(8,128)S(1)}, f32[256,256]{1,0:T(8,128)S(1)}, u32[]{:S(2)}, u32[]{:S(2)}) collective-permute-start(f32[256,256]{1,0:T(8,128)S(1)} %get-tuple-element.68), channel_id=1, source_target_pairs={{0,2},{1,3},{2,0},{3,1},{4,6},{5,7},{6,4},{7,5},{8,10},{9,11},{10,... | collective-permute-start | bytes 786440 | tf_op jit(solution)/shard_map/ppermute | solution.py:391
  45.9 8.1 %collective-permute-start.13 = (f32[128,256]{1,0:T(8,128)S(1)}, f32[128,256]{1,0:T(8,128)S(1)}, u32[]{:S(2)}, u32[]{:S(2)}) collective-permute-start(f32[128,256]{1,0:T(8,128)S(1)} %get-tuple-element.69), channel_id=1, source_target_pairs={{0,4},{1,5},{2,6},{3,7},{4,0},{5,1},{6,2},{7,3},{8,12},{9,13},{10,... | collective-permute-start | bytes 393224 | tf_op jit(solution)/shard_map/ppermute | solution.py:391
  50.2 8.5 %collective-permute-start.11 = (f32[256,256]{1,0:T(8,128)S(1)}, f32[256,256]{1,0:T(8,128)S(1)}, u32[]{:S(2)}, u32[]{:S(2)}) collective-permute-start(f32[256,256]{1,0:T(8,128)S(1)} %get-tuple-element.67), channel_id=1, source_target_pairs={{0,1},{1,0},{2,3},{3,2},{4,5},{5,4},{6,7},{7,6},{8,9},{9,8},{10,11... | collective-permute-start | bytes 786440 | tf_op jit(solution)/shard_map/ppermute | solution.py:391
  51.7 14.9 %collective-permute-start.9 = (f32[64,512]{1,0:T(8,128)S(1)}, f32[64,512]{1,0:T(8,128)S(1)}, u32[]{:S(2)}, u32[]{:S(2)}) collective-permute-start(f32[64,512]{1,0:T(8,128)S(1)} %join.1.refs_1_.own), channel_id=1, source_target_pairs={{8,0},{16,8},{24,16},{9,1},{17,9},{25,17},{10,2},{18,10},{26,18},{... | collective-permute-start | bytes 393224 | tf_op jit(solution)/shard_map/ppermute | solution.py:418
  53.1 6.3 %collective-permute-start.16 = (f32[128,256]{1,0:T(8,128)S(1)}, f32[128,256]{1,0:T(8,128)S(1)}, u32[]{:S(2)}, u32[]{:S(2)}) collective-permute-start(f32[128,256]{1,0:T(8,128)S(1)} %get-tuple-element.75), channel_id=1, source_target_pairs={{0,2},{1,3},{2,0},{3,1},{4,6},{5,7},{6,4},{7,5},{8,10},{9,11},{10,... | collective-permute-start | bytes 393224 | tf_op jit(solution)/shard_map/ppermute | solution.py:391
  54.1 13.7 %collective-permute-start.17 = (f32[128,256]{1,0:T(8,128)S(1)}, f32[128,256]{1,0:T(8,128)S(1)}, u32[]{:S(2)}, u32[]{:S(2)}) collective-permute-start(f32[128,256]{1,0:T(8,128)S(1)} %get-tuple-element.80), channel_id=1, source_target_pairs={{0,4},{1,5},{2,6},{3,7},{4,0},{5,1},{6,2},{7,3},{8,12},{9,13},{10,... | collective-permute-start | bytes 393224 | tf_op jit(solution)/shard_map/ppermute | solution.py:391
  58.7 7.7 %collective-permute-start.15 = (f32[128,256]{1,0:T(8,128)S(1)}, f32[128,256]{1,0:T(8,128)S(1)}, u32[]{:S(2)}, u32[]{:S(2)}) collective-permute-start(f32[128,256]{1,0:T(8,128)S(1)} %get-tuple-element.74), channel_id=1, source_target_pairs={{0,2},{1,3},{2,0},{3,1},{4,6},{5,7},{6,4},{7,5},{8,10},{9,11},{10,... | collective-permute-start | bytes 393224 | tf_op jit(solution)/shard_map/ppermute | solution.py:391
  59.4 13.5 %collective-permute-start.18 = (f32[128,256]{1,0:T(8,128)S(1)}, f32[128,256]{1,0:T(8,128)S(1)}, u32[]{:S(2)}, u32[]{:S(2)}) collective-permute-start(f32[128,256]{1,0:T(8,128)S(1)} %get-tuple-element.81), channel_id=1, source_target_pairs={{0,4},{1,5},{2,6},{3,7},{4,0},{5,1},{6,2},{7,3},{8,12},{9,13},{10,... | collective-permute-start | bytes 393224 | tf_op jit(solution)/shard_map/ppermute | solution.py:391
  66.5 9.2 %collective-permute-start.19 = (f32[128,256]{1,0:T(8,128)S(1)}, f32[128,256]{1,0:T(8,128)S(1)}, u32[]{:S(2)}, u32[]{:S(2)}) collective-permute-start(f32[128,256]{1,0:T(8,128)S(1)} %get-tuple-element.82), channel_id=1, source_target_pairs={{0,4},{1,5},{2,6},{3,7},{4,0},{5,1},{6,2},{7,3},{8,12},{9,13},{10,... | collective-permute-start | bytes 393224 | tf_op jit(solution)/shard_map/ppermute | solution.py:391

commit v7 on v6

--- a/solution.py
+++ b/solution.py
@@ -374,9 +374,9 @@
     (4, 1, 2.5),
     (3, 2, 2.5),
     (4, 2, 0.01),
-    (5, 1, 0.01),
     (2, 3, 1.6),
     (3, 3, 2.5),
+    (5, 1, 0.01),
 )
 
 

time: 77.5 us -> 77.5 us (level)
  no operation moved by 1% of the time
where the time goes in v7:
time: 77.5 us; the launch traced here: 77.3 us
  starting transfers between devices  32.9 us (42%)
  waiting for transfers between devices  26.4 us (34%)
  Pallas kernels  17.7 us (23%)
    ppermute x15, starting transfers between devices, swap(): lax.ppermute(array, 'samp', [(i, i ^ 1 << bit) for i in range(parts)])  26.5 us
    ppermute x15, waiting for transfers between devices, swap(): lax.ppermute(array, 'samp', [(i, i ^ 1 << bit) for i in range(parts)])  26.4 us
    pallas_call x5, Pallas kernels, gram(): pl.pallas_call(functools.partial(gram_kernel, piece, spots, order, len(ah...  11.7 us
    ppermute x4, starting transfers between devices, local(): come = [[]] + [[lax.ppermute(cut, 'var', route)] for cut in cuts]  5.16 us
    pallas_call x1, Pallas kernels, prepare(): pl.pallas_call(prepare_kernel, in_specs=[pl.BlockSpec(memory_space=pltpu....  2.79 us
    pallas_call x1, Pallas kernels, finish(): pl.pallas_call(functools.partial(finish_kernel, starts, sizes), in_specs=...  1.57 us
  transfers between devices with their start and end apart: 20, of which 8 were waited for; matrix products, arithmetic and copies ran while one was open for 0% of the time, Pallas kernels for 17%

profile of v7, /device:TPU:0, one launch (start us, length us, event | category | flops | bytes accessed | tf_op | source)
XLA Modules:
  0.0 77.3 jit_solution(2717756654840975567)
XLA Ops:
  0.0 2.8 %prepare.1 = (bf16[1024,768]{1,0:T(8,128)(2,1)S(1)}, bf16[1024,768]{1,0:T(8,128)(2,1)S(1)}, f32[16,512]{1,0:T(8,128)S(1)}, f32[768,256]{1,0:T(8,128)S(1)}, f32[7...) custom-call(f32[768,1024]{1,0:T(8,128)} %dosages.1), custom_call_target="tpu_custom_call" | custom-call | flops 4000000000 | bytes 1 | tf_op jit(solution)/shard_map/prepare/pallas_call | solution.py:65
  2.8 1.3 %collective-permute-start.1 = (f32[768,256]{1,0:T(8,128)S(1)}, f32[768,256]{1,0:T(8,128)S(1)}, u32[]{:S(2)}, u32[]{:S(2)}) collective-permute-start(f32[768,256]{1,0:T(8,128)S(1)} %get-tuple-element.49), channel_id=1, source_target_pairs={{8,0},{16,8},{24,16},{9,1},{17,9},{25,17},{10,2},{18,10},{26,18},{... | collective-permute-start | bytes 2359304 | tf_op jit(solution)/shard_map/ppermute | solution.py:411
  4.1 1.7 %gram.5 = (f32[272,512]{1,0:T(8,128)S(1)}, f32[272,512]{1,0:T(8,128)S(1)}) custom-call(bf16[1024,768]{1,0:T(8,128)(2,1)S(1)} %get-tuple-element.44.high_t, bf16[1024,768]{1,0:T(8,128)(2,1)S(1)} %get-tuple-element.45.low_t, f32[16,512]{1,0:T(8,128)S(1)} %get-tuple-element.46.refs_0_.refs_1_, f32[16,512]{1,0:T(8,128)S(1)} %get-tuple-element.46.refs_0_.refs_1_), custom_call_target="tpu_custom_call" | custom-call | flops 10000000 | bytes 1 | tf_op jit(solution)/shard_map/gram/pallas_call | solution.py:138
  5.8 3.0 %collective-permute-start = (f32[272,512]{1,0:T(8,128)S(1)}, f32[272,512]{1,0:T(8,128)S(1)}, u32[]{:S(2)}, u32[]{:S(2)}) collective-permute-start(f32[272,512]{1,0:T(8,128)S(1)} %get-tuple-element.48), channel_id=1, source_target_pairs={{0,1},{1,0},{2,3},{3,2},{4,5},{5,4},{6,7},{7,6},{8,9},{9,8},{10,11... | collective-permute-start | bytes 1671176 | tf_op jit(solution)/shard_map/ppermute | solution.py:391
  8.8 1.3 %collective-permute-start.3 = (f32[768,256]{1,0:T(8,128)S(1)}, f32[768,256]{1,0:T(8,128)S(1)}, u32[]{:S(2)}, u32[]{:S(2)}) collective-permute-start(f32[768,256]{1,0:T(8,128)S(1)} %get-tuple-element.53), channel_id=1, source_target_pairs={{8,0},{16,8},{24,16},{9,1},{17,9},{25,17},{10,2},{18,10},{26,18},{... | collective-permute-start | bytes 2359304 | tf_op jit(solution)/shard_map/ppermute | solution.py:411
  10.1 1.3 %collective-permute-start.8 = (f32[768,256]{1,0:T(8,128)S(1)}, f32[768,256]{1,0:T(8,128)S(1)}, u32[]{:S(2)}, u32[]{:S(2)}) collective-permute-start(f32[768,256]{1,0:T(8,128)S(1)} %get-tuple-element.61), channel_id=1, source_target_pairs={{8,0},{16,8},{24,16},{9,1},{17,9},{25,17},{10,2},{18,10},{26,18},{... | collective-permute-start | bytes 2359304 | tf_op jit(solution)/shard_map/ppermute | solution.py:411
  11.4 1.3 %collective-permute-start.11 = (f32[768,256]{1,0:T(8,128)S(1)}, f32[768,256]{1,0:T(8,128)S(1)}, u32[]{:S(2)}, u32[]{:S(2)}) collective-permute-start(f32[768,256]{1,0:T(8,128)S(1)} %get-tuple-element.66), channel_id=1, source_target_pairs={{8,0},{16,8},{24,16},{9,1},{17,9},{25,17},{10,2},{18,10},{26,18},{... | collective-permute-start | bytes 2359304 | tf_op jit(solution)/shard_map/ppermute | solution.py:411
  12.7 0.0 collective-permute-done.1.refs_0_
  12.7 3.4 %gram.6 = (f32[512,256]{1,0:T(8,128)S(1)}, f32[512,256]{1,0:T(8,128)S(1)}) custom-call(bf16[1024,768]{1,0:T(8,128)(2,1)S(1)} %get-tuple-element.44.high_t, bf16[1024,768]{1,0:T(8,128)(2,1)S(1)} %get-tuple-element.45.low_t, f32[768,256]{1,0:T(8,128)S(1)} %collective-permute-done.1.refs_0_, f32[272,512]{1,0:T(8,128)S(1)} %get-tuple-element.47.refs_1_.keep), custom_call_target="tpu_custom_call" | custom-call | flops 10000000 | bytes 1 | tf_op jit(solution)/shard_map/gram/pallas_call | solution.py:138
  16.1 0.1 collective-permute-start.5
  16.2 5.7 %collective-permute-done.got = f32[272,512]{1,0:T(8,128)S(1)} collective-permute-done((f32[272,512]{1,0:T(8,128)S(1)}, f32[272,512]{1,0:T(8,128)S(1)}, u32[]{:S(2)}, u32[]{:S(2)}) %collective-permute-start) | collective-permute-done | bytes 557088 | tf_op jit(solution)/shard_map/ppermute | solution.py:391
  21.9 0.1 add.10
  22.0 2.4 %collective-permute-start.2 = (f32[144,512]{1,0:T(8,128)S(1)}, f32[144,512]{1,0:T(8,128)S(1)}, u32[]{:S(2)}, u32[]{:S(2)}) collective-permute-start(f32[144,512]{1,0:T(8,128)S(1)} %get-tuple-element.52), channel_id=1, source_target_pairs={{0,2},{1,3},{2,0},{3,1},{4,6},{5,7},{6,4},{7,5},{8,10},{9,11},{10,... | collective-permute-start | bytes 884744 | tf_op jit(solution)/shard_map/ppermute | solution.py:391
  24.4 0.0 collective-permute-done.3.refs_0_
  24.4 3.1 %gram.7 = (f32[512,256]{1,0:T(8,128)S(1)}, f32[512,256]{1,0:T(8,128)S(1)}) custom-call(bf16[1024,768]{1,0:T(8,128)(2,1)S(1)} %get-tuple-element.44.high_t, bf16[1024,768]{1,0:T(8,128)(2,1)S(1)} %get-tuple-element.45.low_t, f32[768,256]{1,0:T(8,128)S(1)} %collective-permute-done.3.refs_0_, f32[144,512]{1,0:T(8,128)S(1)} %get-tuple-element.51.refs_1_.keep), custom_call_target="tpu_custom_call" | custom-call | flops 10000000 | bytes 1 | tf_op jit(solution)/shard_map/gram/pallas_call | solution.py:138
  27.5 1.5 %collective-permute-start.7 = (f32[512,256]{1,0:T(8,128)S(1)}, f32[512,256]{1,0:T(8,128)S(1)}, u32[]{:S(2)}, u32[]{:S(2)}) collective-permute-start(f32[512,256]{1,0:T(8,128)S(1)} %get-tuple-element.60), channel_id=1, source_target_pairs={{0,1},{1,0},{2,3},{3,2},{4,5},{5,4},{6,7},{7,6},{8,9},{9,8},{10,11... | collective-permute-start | bytes 1572872 | tf_op jit(solution)/shard_map/ppermute | solution.py:391
  29.0 3.0 %collective-permute-done.2.got = f32[144,512]{1,0:T(8,128)S(1)} collective-permute-done((f32[144,512]{1,0:T(8,128)S(1)}, f32[144,512]{1,0:T(8,128)S(1)}, u32[]{:S(2)}, u32[]{:S(2)}) %collective-permute-start.2) | collective-permute-done | bytes 294944 | tf_op jit(solution)/shard_map/ppermute | solution.py:391
  32.0 0.0 collective-permute-done.5.got
  32.0 0.1 add.11
  32.1 2.6 %collective-permute-start.6 = (f32[256,256]{1,0:T(8,128)S(1)}, f32[256,256]{1,0:T(8,128)S(1)}, u32[]{:S(2)}, u32[]{:S(2)}) collective-permute-start(f32[256,256]{1,0:T(8,128)S(1)} %get-tuple-element.59), channel_id=1, source_target_pairs={{0,2},{1,3},{2,0},{3,1},{4,6},{5,7},{6,4},{7,5},{8,10},{9,11},{10,... | collective-permute-start | bytes 786440 | tf_op jit(solution)/shard_map/ppermute | solution.py:391
  34.7 2.6 %collective-permute-start.4 = (f32[32,512]{1,0:T(8,128)S(1)}, f32[32,512]{1,0:T(8,128)S(1)}, u32[]{:S(2)}, u32[]{:S(2)}) collective-permute-start(f32[32,512]{1,0:T(8,128)S(1)} %get-tuple-element.55.one), channel_id=1, source_target_pairs={{0,4},{1,5},{2,6},{3,7},{4,0},{5,1},{6,2},{7,3},{8,12},{9,13},{10,... | collective-permute-start | bytes 196616 | tf_op jit(solution)/shard_map/ppermute | solution.py:391
  37.3 0.0 collective-permute-done.8.refs_0_
  37.3 1.9 %gram.8 = (f32[256,256]{1,0:T(8,128)S(1)}, f32[256,256]{1,0:T(8,128)S(1)}) custom-call(bf16[1024,768]{1,0:T(8,128)(2,1)S(1)} %get-tuple-element.44.high_t, bf16[1024,768]{1,0:T(8,128)(2,1)S(1)} %get-tuple-element.45.low_t, f32[768,256]{1,0:T(8,128)S(1)} %collective-permute-done.8.refs_0_, f32[256,256]{1,0:T(8,128)S(1)} %get-tuple-element.58.refs_1_.keep), custom_call_target="tpu_custom_call" | custom-call | flops 10000000 | bytes 1 | tf_op jit(solution)/shard_map/gram/pallas_call | solution.py:138
  39.2 1.5 %collective-permute-start.10 = (f32[256,256]{1,0:T(8,128)S(1)}, f32[256,256]{1,0:T(8,128)S(1)}, u32[]{:S(2)}, u32[]{:S(2)}) collective-permute-start(f32[256,256]{1,0:T(8,128)S(1)} %get-tuple-element.65), channel_id=1, source_target_pairs={{0,1},{1,0},{2,3},{3,2},{4,5},{5,4},{6,7},{7,6},{8,9},{9,8},{10,11... | collective-permute-start | bytes 786440 | tf_op jit(solution)/shard_map/ppermute | solution.py:391
  40.7 2.5 %collective-permute-done.7.got = f32[512,256]{1,0:T(8,128)S(1)} collective-permute-done((f32[512,256]{1,0:T(8,128)S(1)}, f32[512,256]{1,0:T(8,128)S(1)}, u32[]{:S(2)}, u32[]{:S(2)}) %collective-permute-start.7) | collective-permute-done | bytes 524320 | tf_op jit(solution)/shard_map/ppermute | solution.py:391
  43.2 0.1 add.12
  43.3 2.6 %collective-permute-start.14 = (f32[256,256]{1,0:T(8,128)S(1)}, f32[256,256]{1,0:T(8,128)S(1)}, u32[]{:S(2)}, u32[]{:S(2)}) collective-permute-start(f32[256,256]{1,0:T(8,128)S(1)} %get-tuple-element.71), channel_id=1, source_target_pairs={{0,2},{1,3},{2,0},{3,1},{4,6},{5,7},{6,4},{7,5},{8,10},{9,11},{10,... | collective-permute-start | bytes 786440 | tf_op jit(solution)/shard_map/ppermute | solution.py:391
  45.9 0.0 collective-permute-done.6.got
  45.9 2.7 %collective-permute-start.15 = (f32[128,256]{1,0:T(8,128)S(1)}, f32[128,256]{1,0:T(8,128)S(1)}, u32[]{:S(2)}, u32[]{:S(2)}) collective-permute-start(f32[128,256]{1,0:T(8,128)S(1)} %get-tuple-element.72), channel_id=1, source_target_pairs={{0,4},{1,5},{2,6},{3,7},{4,0},{5,1},{6,2},{7,3},{8,12},{9,13},{10,... | collective-permute-start | bytes 393224 | tf_op jit(solution)/shard_map/ppermute | solution.py:391
  48.6 0.0 collective-permute-done.4.other
  48.6 0.0 collective-permute-done.11.refs_0_
  48.6 1.6 %gram.9 = (f32[256,256]{1,0:T(8,128)S(1)}, f32[256,256]{1,0:T(8,128)S(1)}) custom-call(bf16[1024,768]{1,0:T(8,128)(2,1)S(1)} %get-tuple-element.44.high_t, bf16[1024,768]{1,0:T(8,128)(2,1)S(1)} %get-tuple-element.45.low_t, f32[768,256]{1,0:T(8,128)S(1)} %collective-permute-done.11.refs_0_, f32[64,512]{1,0:T(8,128)S(1)} %join.1.refs_1_.own), custom_call_target="tpu_custom_call" | custom-call | flops 10000000 | bytes 1 | tf_op jit(solution)/shard_map/gram/pallas_call | solution.py:138
  50.2 1.5 %collective-permute-start.13 = (f32[256,256]{1,0:T(8,128)S(1)}, f32[256,256]{1,0:T(8,128)S(1)}, u32[]{:S(2)}, u32[]{:S(2)}) collective-permute-start(f32[256,256]{1,0:T(8,128)S(1)} %get-tuple-element.70), channel_id=1, source_target_pairs={{0,1},{1,0},{2,3},{3,2},{4,5},{5,4},{6,7},{7,6},{8,9},{9,8},{10,11... | collective-permute-start | bytes 786440 | tf_op jit(solution)/shard_map/ppermute | solution.py:391
  51.7 1.3 %collective-permute-start.9 = (f32[64,512]{1,0:T(8,128)S(1)}, f32[64,512]{1,0:T(8,128)S(1)}, u32[]{:S(2)}, u32[]{:S(2)}) collective-permute-start(f32[64,512]{1,0:T(8,128)S(1)} %join.1.refs_1_.own), channel_id=1, source_target_pairs={{8,0},{16,8},{24,16},{9,1},{17,9},{25,17},{10,2},{18,10},{26,18},{... | collective-permute-start | bytes 393224 | tf_op jit(solution)/shard_map/ppermute | solution.py:418
  53.0 0.0 collective-permute-done.10.got
  53.1 0.5 collective-permute-start.12
  53.6 0.5 collective-permute-done.15.got
  54.1 0.0 collective-permute-done.14.got
  54.1 3.4 %collective-permute-start.17 = (f32[128,256]{1,0:T(8,128)S(1)}, f32[128,256]{1,0:T(8,128)S(1)}, u32[]{:S(2)}, u32[]{:S(2)}) collective-permute-start(f32[128,256]{1,0:T(8,128)S(1)} %get-tuple-element.77), channel_id=1, source_target_pairs={{0,4},{1,5},{2,6},{3,7},{4,0},{5,1},{6,2},{7,3},{8,12},{9,13},{10,... | collective-permute-start | bytes 393224 | tf_op jit(solution)/shard_map/ppermute | solution.py:391
  57.6 1.2 %collective-permute-done.13.got = f32[256,256]{1,0:T(8,128)S(1)} collective-permute-done((f32[256,256]{1,0:T(8,128)S(1)}, f32[256,256]{1,0:T(8,128)S(1)}, u32[]{:S(2)}, u32[]{:S(2)}) %collective-permute-start.13) | collective-permute-done | bytes 262176 | tf_op jit(solution)/shard_map/ppermute | solution.py:391
  58.7 0.6 collective-permute-start.18
  59.3 0.0 collective-permute-done.12.got
  59.4 1.4 %collective-permute-start.16 = (f32[128,256]{1,0:T(8,128)S(1)}, f32[128,256]{1,0:T(8,128)S(1)}, u32[]{:S(2)}, u32[]{:S(2)}) collective-permute-start(f32[128,256]{1,0:T(8,128)S(1)} %get-tuple-element.76), channel_id=1, source_target_pairs={{0,4},{1,5},{2,6},{3,7},{4,0},{5,1},{6,2},{7,3},{8,12},{9,13},{10,... | collective-permute-start | bytes 393224 | tf_op jit(solution)/shard_map/ppermute | solution.py:391
  60.8 5.7 %collective-permute-done.18.got = f32[128,256]{1,0:T(8,128)S(1)} collective-permute-done((f32[128,256]{1,0:T(8,128)S(1)}, f32[128,256]{1,0:T(8,128)S(1)}, u32[]{:S(2)}, u32[]{:S(2)}) %collective-permute-start.18) | collective-permute-done | bytes 131104 | tf_op jit(solution)/shard_map/ppermute | solution.py:391
  66.5 0.1 collective-permute-start.19
  66.6 0.0 collective-permute-done.17.got
  66.6 6.2 %collective-permute-done.16.got = f32[128,256]{1,0:T(8,128)S(1)} collective-permute-done((f32[128,256]{1,0:T(8,128)S(1)}, f32[128,256]{1,0:T(8,128)S(1)}, u32[]{:S(2)}, u32[]{:S(2)}) %collective-permute-start.16) | collective-permute-done | bytes 131104 | tf_op jit(solution)/shard_map/ppermute | solution.py:391
  72.9 0.0 collective-permute-done.9.ahead
  72.9 1.2 %weigh.1 = (f32[128,1024]{1,0:T(8,128)S(1)}, f32[128,1024]{1,0:T(8,128)S(1)}) custom-call(f32[64,512]{1,0:T(8,128)S(1)} %join.1.refs_1_.own, f32[64,512]{1,0:T(8,128)S(1)} %collective-permute-done.9.ahead, f32[128,256]{1,0:T(8,128)S(1)} %add.19.refs_0_.refs_2_), custom_call_target="tpu_custom_call" | custom-call | flops 10000000 | bytes 1 | tf_op jit(solution)/shard_map/weigh/pallas_call | solution.py:308
  74.1 1.6 %collective-permute-done.19.refs_4_ = f32[128,256]{1,0:T(8,128)S(1)} collective-permute-done((f32[128,256]{1,0:T(8,128)S(1)}, f32[128,256]{1,0:T(8,128)S(1)}, u32[]{:S(2)}, u32[]{:S(2)}) %collective-permute-start.19) | collective-permute-done | bytes 131104 | tf_op jit(solution)/shard_map/ppermute | solution.py:391
  75.7 1.6 %finish.1 = f32[128,1024]{1,0:T(8,128)} custom-call(f32[128,1024]{1,0:T(8,128)S(1)} %get-tuple-element.80.fix, f32[128,1024]{1,0:T(8,128)S(1)} %get-tuple-element.81.factor, f32[128,256]{1,0:T(8,128)S(1)} %add.15.refs_0_, f32[128,256]{1,0:T(8,128)S(1)} %add.18.refs_0_.refs_1_, f32[128,256]{1,0:T(8,128)S(1)} %add.19.refs_0_.refs_2_, ...), custom_call_target="tpu_custom_call" | custom-call | flops 4000000000 | bytes 1 | tf_op jit(solution)/shard_map/finish/pallas_call | solution.py:347
  (11 shorter events, 0.3 us)
Async XLA Ops:
  2.8 9.9 %collective-permute-start.1 = (f32[768,256]{1,0:T(8,128)S(1)}, f32[768,256]{1,0:T(8,128)S(1)}, u32[]{:S(2)}, u32[]{:S(2)}) collective-permute-start(f32[768,256]{1,0:T(8,128)S(1)} %get-tuple-element.49), channel_id=1, source_target_pairs={{8,0},{16,8},{24,16},{9,1},{17,9},{25,17},{10,2},{18,10},{26,18},{... | collective-permute-start | bytes 2359304 | tf_op jit(solution)/shard_map/ppermute | solution.py:411
  5.8 16.1 %collective-permute-start = (f32[272,512]{1,0:T(8,128)S(1)}, f32[272,512]{1,0:T(8,128)S(1)}, u32[]{:S(2)}, u32[]{:S(2)}) collective-permute-start(f32[272,512]{1,0:T(8,128)S(1)} %get-tuple-element.48), channel_id=1, source_target_pairs={{0,1},{1,0},{2,3},{3,2},{4,5},{5,4},{6,7},{7,6},{8,9},{9,8},{10,11... | collective-permute-start | bytes 1671176 | tf_op jit(solution)/shard_map/ppermute | solution.py:391
  8.8 15.6 %collective-permute-start.3 = (f32[768,256]{1,0:T(8,128)S(1)}, f32[768,256]{1,0:T(8,128)S(1)}, u32[]{:S(2)}, u32[]{:S(2)}) collective-permute-start(f32[768,256]{1,0:T(8,128)S(1)} %get-tuple-element.53), channel_id=1, source_target_pairs={{8,0},{16,8},{24,16},{9,1},{17,9},{25,17},{10,2},{18,10},{26,18},{... | collective-permute-start | bytes 2359304 | tf_op jit(solution)/shard_map/ppermute | solution.py:411
  10.1 27.2 %collective-permute-start.8 = (f32[768,256]{1,0:T(8,128)S(1)}, f32[768,256]{1,0:T(8,128)S(1)}, u32[]{:S(2)}, u32[]{:S(2)}) collective-permute-start(f32[768,256]{1,0:T(8,128)S(1)} %get-tuple-element.61), channel_id=1, source_target_pairs={{8,0},{16,8},{24,16},{9,1},{17,9},{25,17},{10,2},{18,10},{26,18},{... | collective-permute-start | bytes 2359304 | tf_op jit(solution)/shard_map/ppermute | solution.py:411
  11.4 37.2 %collective-permute-start.11 = (f32[768,256]{1,0:T(8,128)S(1)}, f32[768,256]{1,0:T(8,128)S(1)}, u32[]{:S(2)}, u32[]{:S(2)}) collective-permute-start(f32[768,256]{1,0:T(8,128)S(1)} %get-tuple-element.66), channel_id=1, source_target_pairs={{8,0},{16,8},{24,16},{9,1},{17,9},{25,17},{10,2},{18,10},{26,18},{... | collective-permute-start | bytes 2359304 | tf_op jit(solution)/shard_map/ppermute | solution.py:411
  16.1 15.9 %collective-permute-start.5 = (f32[512,256]{1,0:T(8,128)S(1)}, f32[512,256]{1,0:T(8,128)S(1)}, u32[]{:S(2)}, u32[]{:S(2)}) collective-permute-start(f32[512,256]{1,0:T(8,128)S(1)} %get-tuple-element.56), channel_id=1, source_target_pairs={{0,1},{1,0},{2,3},{3,2},{4,5},{5,4},{6,7},{7,6},{8,9},{9,8},{10,11... | collective-permute-start | bytes 1572872 | tf_op jit(solution)/shard_map/ppermute | solution.py:391
  22.0 10.0 %collective-permute-start.2 = (f32[144,512]{1,0:T(8,128)S(1)}, f32[144,512]{1,0:T(8,128)S(1)}, u32[]{:S(2)}, u32[]{:S(2)}) collective-permute-start(f32[144,512]{1,0:T(8,128)S(1)} %get-tuple-element.52), channel_id=1, source_target_pairs={{0,2},{1,3},{2,0},{3,1},{4,6},{5,7},{6,4},{7,5},{8,10},{9,11},{10,... | collective-permute-start | bytes 884744 | tf_op jit(solution)/shard_map/ppermute | solution.py:391
  27.5 15.7 %collective-permute-start.7 = (f32[512,256]{1,0:T(8,128)S(1)}, f32[512,256]{1,0:T(8,128)S(1)}, u32[]{:S(2)}, u32[]{:S(2)}) collective-permute-start(f32[512,256]{1,0:T(8,128)S(1)} %get-tuple-element.60), channel_id=1, source_target_pairs={{0,1},{1,0},{2,3},{3,2},{4,5},{5,4},{6,7},{7,6},{8,9},{9,8},{10,11... | collective-permute-start | bytes 1572872 | tf_op jit(solution)/shard_map/ppermute | solution.py:391
  32.1 13.8 %collective-permute-start.6 = (f32[256,256]{1,0:T(8,128)S(1)}, f32[256,256]{1,0:T(8,128)S(1)}, u32[]{:S(2)}, u32[]{:S(2)}) collective-permute-start(f32[256,256]{1,0:T(8,128)S(1)} %get-tuple-element.59), channel_id=1, source_target_pairs={{0,2},{1,3},{2,0},{3,1},{4,6},{5,7},{6,4},{7,5},{8,10},{9,11},{10,... | collective-permute-start | bytes 786440 | tf_op jit(solution)/shard_map/ppermute | solution.py:391
  34.7 13.9 %collective-permute-start.4 = (f32[32,512]{1,0:T(8,128)S(1)}, f32[32,512]{1,0:T(8,128)S(1)}, u32[]{:S(2)}, u32[]{:S(2)}) collective-permute-start(f32[32,512]{1,0:T(8,128)S(1)} %get-tuple-element.55.one), channel_id=1, source_target_pairs={{0,4},{1,5},{2,6},{3,7},{4,0},{5,1},{6,2},{7,3},{8,12},{9,13},{10,... | collective-permute-start | bytes 196616 | tf_op jit(solution)/shard_map/ppermute | solution.py:391
  39.2 13.8 %collective-permute-start.10 = (f32[256,256]{1,0:T(8,128)S(1)}, f32[256,256]{1,0:T(8,128)S(1)}, u32[]{:S(2)}, u32[]{:S(2)}) collective-permute-start(f32[256,256]{1,0:T(8,128)S(1)} %get-tuple-element.65), channel_id=1, source_target_pairs={{0,1},{1,0},{2,3},{3,2},{4,5},{5,4},{6,7},{7,6},{8,9},{9,8},{10,11... | collective-permute-start | bytes 786440 | tf_op jit(solution)/shard_map/ppermute | solution.py:391
  43.3 10.8 %collective-permute-start.14 = (f32[256,256]{1,0:T(8,128)S(1)}, f32[256,256]{1,0:T(8,128)S(1)}, u32[]{:S(2)}, u32[]{:S(2)}) collective-permute-start(f32[256,256]{1,0:T(8,128)S(1)} %get-tuple-element.71), channel_id=1, source_target_pairs={{0,2},{1,3},{2,0},{3,1},{4,6},{5,7},{6,4},{7,5},{8,10},{9,11},{10,... | collective-permute-start | bytes 786440 | tf_op jit(solution)/shard_map/ppermute | solution.py:391
  45.9 8.1 %collective-permute-start.15 = (f32[128,256]{1,0:T(8,128)S(1)}, f32[128,256]{1,0:T(8,128)S(1)}, u32[]{:S(2)}, u32[]{:S(2)}) collective-permute-start(f32[128,256]{1,0:T(8,128)S(1)} %get-tuple-element.72), channel_id=1, source_target_pairs={{0,4},{1,5},{2,6},{3,7},{4,0},{5,1},{6,2},{7,3},{8,12},{9,13},{10,... | collective-permute-start | bytes 393224 | tf_op jit(solution)/shard_map/ppermute | solution.py:391
  50.2 8.5 %collective-permute-start.13 = (f32[256,256]{1,0:T(8,128)S(1)}, f32[256,256]{1,0:T(8,128)S(1)}, u32[]{:S(2)}, u32[]{:S(2)}) collective-permute-start(f32[256,256]{1,0:T(8,128)S(1)} %get-tuple-element.70), channel_id=1, source_target_pairs={{0,1},{1,0},{2,3},{3,2},{4,5},{5,4},{6,7},{7,6},{8,9},{9,8},{10,11... | collective-permute-start | bytes 786440 | tf_op jit(solution)/shard_map/ppermute | solution.py:391
  51.7 21.2 %collective-permute-start.9 = (f32[64,512]{1,0:T(8,128)S(1)}, f32[64,512]{1,0:T(8,128)S(1)}, u32[]{:S(2)}, u32[]{:S(2)}) collective-permute-start(f32[64,512]{1,0:T(8,128)S(1)} %join.1.refs_1_.own), channel_id=1, source_target_pairs={{8,0},{16,8},{24,16},{9,1},{17,9},{25,17},{10,2},{18,10},{26,18},{... | collective-permute-start | bytes 393224 | tf_op jit(solution)/shard_map/ppermute | solution.py:418
  53.1 6.3 %collective-permute-start.12 = (f32[128,256]{1,0:T(8,128)S(1)}, f32[128,256]{1,0:T(8,128)S(1)}, u32[]{:S(2)}, u32[]{:S(2)}) collective-permute-start(f32[128,256]{1,0:T(8,128)S(1)} %get-tuple-element.69), channel_id=1, source_target_pairs={{0,2},{1,3},{2,0},{3,1},{4,6},{5,7},{6,4},{7,5},{8,10},{9,11},{10,... | collective-permute-start | bytes 393224 | tf_op jit(solution)/shard_map/ppermute | solution.py:391
  54.1 12.5 %collective-permute-start.17 = (f32[128,256]{1,0:T(8,128)S(1)}, f32[128,256]{1,0:T(8,128)S(1)}, u32[]{:S(2)}, u32[]{:S(2)}) collective-permute-start(f32[128,256]{1,0:T(8,128)S(1)} %get-tuple-element.77), channel_id=1, source_target_pairs={{0,4},{1,5},{2,6},{3,7},{4,0},{5,1},{6,2},{7,3},{8,12},{9,13},{10,... | collective-permute-start | bytes 393224 | tf_op jit(solution)/shard_map/ppermute | solution.py:391
  58.7 7.7 %collective-permute-start.18 = (f32[128,256]{1,0:T(8,128)S(1)}, f32[128,256]{1,0:T(8,128)S(1)}, u32[]{:S(2)}, u32[]{:S(2)}) collective-permute-start(f32[128,256]{1,0:T(8,128)S(1)} %get-tuple-element.78), channel_id=1, source_target_pairs={{0,2},{1,3},{2,0},{3,1},{4,6},{5,7},{6,4},{7,5},{8,10},{9,11},{10,... | collective-permute-start | bytes 393224 | tf_op jit(solution)/shard_map/ppermute | solution.py:391
  59.4 13.5 %collective-permute-start.16 = (f32[128,256]{1,0:T(8,128)S(1)}, f32[128,256]{1,0:T(8,128)S(1)}, u32[]{:S(2)}, u32[]{:S(2)}) collective-permute-start(f32[128,256]{1,0:T(8,128)S(1)} %get-tuple-element.76), channel_id=1, source_target_pairs={{0,4},{1,5},{2,6},{3,7},{4,0},{5,1},{6,2},{7,3},{8,12},{9,13},{10,... | collective-permute-start | bytes 393224 | tf_op jit(solution)/shard_map/ppermute | solution.py:391
  66.5 9.2 %collective-permute-start.19 = (f32[128,256]{1,0:T(8,128)S(1)}, f32[128,256]{1,0:T(8,128)S(1)}, u32[]{:S(2)}, u32[]{:S(2)}) collective-permute-start(f32[128,256]{1,0:T(8,128)S(1)} %get-tuple-element.82), channel_id=1, source_target_pairs={{0,4},{1,5},{2,6},{3,7},{4,0},{5,1},{6,2},{7,3},{8,12},{9,13},{10,... | collective-permute-start | bytes 393224 | tf_op jit(solution)/shard_map/ppermute | solution.py:391
